TPU v7x, 256 devices: a whole 4x4x8 slice. The times are simulated.
256 devices in a mesh: row: 16 (over z, core), col: 16 (over y, x).
Axes of the slice: x: 4, y: 4, z: 8, core: 2. Of those that a mesh axis runs over, the one named last changes fastest.
Arguments:
- gradient: bfloat16 [8192, 26624], P('row', 'col'), may hold values from -128 to 128
- momentum: bfloat16 [8192, 26624], P('row', 'col'), may hold values from -6 to 6
- weight: bfloat16 [8192, 26624], P('row', 'col'), may hold values from -6 to 6
- right_factor: float32 [26624, 256], P('col'), may hold values from -6 to 6
Outputs:
- new_weight: bfloat16 [8192, 26624], P('row', 'col')
- new_momentum: bfloat16 [8192, 26624], P('row', 'col')
- new_factor: float32 [26624, 256], P('col')
All inputs are finite; a program needn't handle non-finite values.
Results may differ from a plain program's by a relative error of at most 0.0015.
Values sent between devices are 32-bit elements; how exact they have to be, the bound alone decides.
No kernel may reach another device: no remote copies, remote signals or barrier semaphores. Data moves between devices by JAX's collectives and lax.ppermute only.
A program may use at most 64 MiB of HBM per device.

v0:
```python
import jax
import jax.numpy as jnp
from jax import lax
from jax.sharding import PartitionSpec as P

ROWS = 8192
COLS = 26624
RANK = 256


decay = 0.95
step_size = 0.3


def factor_gram(gram):
    rank = gram.shape[0]
    jitter = 1e-06 * jnp.trace(gram) / rank
    return jnp.linalg.cholesky(gram + jitter * jnp.eye(rank, dtype=jnp.float32))


def solve_right(block, chol):
    return lax.linalg.triangular_solve(chol, block, left_side=False, lower=True, transpose_a=True)


def cross_product(buffer, source):
    return lax.dot_general(
        buffer, source, (((0,), (0,)), ((), ())), precision=lax.Precision.HIGHEST
    )


def gram_of(left):
    return jnp.dot(left.T, left, precision=lax.Precision.HIGHEST)


def gram_total(left):
    return lax.psum(gram_of(left), "row")


def local(gradient, momentum, weight, right_factor):
    high = lax.Precision.HIGHEST
    buffer = momentum.astype(jnp.float32) + gradient.astype(jnp.float32)
    left = lax.psum(jnp.dot(buffer, right_factor, precision=high), "col")
    chol = factor_gram(gram_total(left))
    ortho = solve_right(left, chol)
    right_part = lax.psum(cross_product(buffer, ortho), "row")
    squares = lax.psum(jnp.sum(right_part * right_part, axis=0), "col")
    new_momentum = (buffer - (1.0 - decay) * jnp.dot(ortho, right_part.T, precision=high)).astype(
        jnp.bfloat16
    )
    new_factor = right_part / jnp.sqrt(squares / COLS + 1e-06)
    update = jnp.dot(ortho, new_factor.T, precision=high)
    new_weight = (weight.astype(jnp.float32) - step_size * jnp.sqrt(ROWS / RANK) * update).astype(
        jnp.bfloat16
    )
    return (new_weight, new_momentum, new_factor)


def solution(mesh):
    in_specs = (P("row", "col"), P("row", "col"), P("row", "col"), P("col", None))
    out_specs = (P("row", "col"), P("row", "col"), P("col", None))
    return jax.shard_map(local, mesh=mesh, in_specs=in_specs, out_specs=out_specs, check_vma=False)
```

profile of v0, /device:TPU:1, one launch (start us, length us, event | category | flops | bytes accessed | tf_op | source)
XLA Modules:
  0.0 477.8 jit_solution(2352706316631316906)
XLA Ops:
  7.2 1.4 copy-done
  8.6 6.0 %fusion.1 = f32[512,256]{1,0:T(8,128)} fusion(f32[1664,256]{1,0:T(8,128)S(1)} %copy-done, bf16[512,1664]{1,0:T(8,128)(2,1)} %param.4, bf16[512,1664]{1,0:T(8,128)(2,1)} %param.5), kind=kOutput, calls=%fused_computation.6 | convolution fusion | flops 2619801600 | bytes 5636096 | tf_op jit(solution)/shard_map/dot_general | solution.py:42
  14.7 97.9 %all-reduce.5.cloned.1.call-done = f32[512,256]{1,0:T(8,128)} async-done(((f32[512,256]{1,0:T(8,128)}), f32[512,256]{1,0:T(8,128)}) %all-reduce.5.cloned.1.call-update) | async-done | bytes 524304 | tf_op jit(solution)/shard_map/psum | solution.py:42
  112.5 2.9 fusion.14
  115.7 109.0 %all-reduce.7.cloned.1.call-done = f32[256,256]{0,1:T(8,128)} async-done(((f32[256,256]{0,1:T(8,128)}), f32[256,256]{0,1:T(8,128)}) %all-reduce.7.cloned.1.call-update) | async-done | bytes 262160 | tf_op jit(solution)/shard_map/psum | solution.py:36
  224.7 1.6 select_reduce_fusion
  227.0 1.0 select_add_fusion
  228.1 1.0 fusion.4
  229.1 11.7 %cholesky.49 = f32[128,128]{1,0:T(8,128)S(1)} custom-call(f32[128,128]{1,0:T(8,128)S(1)} %cholesky.115), custom_call_target="Cholesky" | custom-call | tf_op jit(solution)/shard_map/jit(cholesky)/cholesky | solution.py:18
  240.9 9.8 %custom-call.14 = f32[1,128,128]{1,2,0:T(8,128)S(1)} custom-call(f32[1,128,128]{2,1,0:T(8,128)S(1)} %get-tuple-element.26), custom_call_target="InvertDiagBlocksLowerTriangular" | custom-call | tf_op jit(solution)/shard_map/jit(cholesky)/cholesky | solution.py:18
  251.3 11.7 %cholesky.103 = f32[128,128]{1,0:T(8,128)S(1)} custom-call(f32[128,128]{1,0:T(8,128)S(1)} %convolution_subtract_fusion.1), custom_call_target="Cholesky" | custom-call | tf_op jit(solution)/shard_map/jit(cholesky)/cholesky | solution.py:18
  263.2 0.7 compare_reduce_fusion
  265.3 0.7 select_select_fusion
  266.1 7.3 %while.1 = (s32[]{:T(128)}, f32[256,256]{0,1:T(8,128)}, s32[2,2]{1,0:T(2,128)S(1)}, f32[2,128,128]{2,1,0:T(8,128)}, s32[]{:T(128)}) while((s32[]{:T(128)}, f32[256,256]{0,1:T(8,128)}, s32[2,2]{1,0:T(2,128)S(1)}, f32[2,128,128]{2,1,0:T(8,128)}, s32[]{:T(128)}) %tuple.26), condition=%wide.while_cond, body=%wide.while_body.sunk | while | flops 2 | bytes 393329 | solution.py:22
  266.1 0.7 fusion.25
  266.8 2.3 dynamic-slice.7
  269.2 0.6 bitcast_dynamic-update-slice_fusion.2
  269.8 0.7 fusion.25
  270.5 2.2 dynamic-slice.7
  272.8 0.6 bitcast_dynamic-update-slice_fusion.2
  273.4 20.5 %custom-call.15 = f32[2,128,128]{1,2,0:T(8,128)S(1)} custom-call(f32[2,128,128]{2,1,0:T(8,128)} %get-tuple-element.10), custom_call_target="InvertDiagBlocksLowerTriangular" | custom-call | tf_op jit(solution)/shard_map/triangular_solve | solution.py:22
  293.9 1.4 fusion.2
  295.3 1.7 convolution_subtract_fusion
  297.4 0.7 copy-done.8
  298.1 8.1 %fusion = f32[1664,256]{1,0:T(8,128)} fusion(bf16[512,1664]{1,0:T(8,128)(2,1)S(1)} %copy-done.2, bf16[512,1664]{1,0:T(8,128)(2,1)} %param.5, f32[512,128]{0,1:T(8,128)S(1)} %fusion.5, f32[512,128]{0,1:T(8,128)S(1)} %fusion.2), kind=kOutput, calls=%fused_computation.5 | convolution fusion | flops 2619932672 | bytes 5636096 | tf_op jit(solution)/shard_map/dot_general | solution.py:26
  306.3 114.0 %all-reduce.9.cloned.1.call-done = f32[1664,256]{1,0:T(8,128)} async-done(((f32[1664,256]{1,0:T(8,128)}), f32[1664,256]{1,0:T(8,128)}) %all-reduce.9.cloned.1.call-update) | async-done | bytes 1703952 | tf_op jit(solution)/shard_map/psum | solution.py:45
  420.2 1.8 multiply_reduce_fusion
  422.1 33.1 %psum.31 = f32[256]{0:T(256)S(1)} all-reduce(f32[256]{0:T(256)S(1)} %multiply_reduce_fusion), channel_id=1, replica_groups=mesh['row'=16,'col'=16] {'col'}, use_global_device_ids=true, to_apply=%region_9.10 | all-reduce | flops 256 | bytes 2048 | tf_op jit(solution)/shard_map/psum | solution.py:46
  455.3 0.8 copy-done.7
  456.2 0.6 copy-done.10
  456.8 7.2 %subtract_convert_fusion.1 = bf16[512,1664]{1,0:T(8,128)(2,1)} fusion(bf16[512,1664]{1,0:T(8,128)(2,1)S(1)} %copy-done.10, f32[1664,256]{1,0:T(8,128)S(1)} %broadcast_divide_fusion, f32[512,128]{0,1:T(8,128)S(1)} %copy-done.9, f32[512,128]{0,1:T(8,128)S(1)} %copy-done.7), kind=kOutput, calls=%fused_computation.3 | convolution fusion | flops 2620784640 | bytes 5636096 | tf_op jit(solution)/shard_map/dot_general | solution.py:51
  464.0 7.3 %subtract_convert_fusion = bf16[512,1664]{1,0:T(8,128)(2,1)} fusion(f32[1664,256]{1,0:T(8,128)S(1)} %copy-done.1, bf16[512,1664]{1,0:T(8,128)(2,1)S(1)} %copy-done.3, bf16[512,1664]{1,0:T(8,128)(2,1)S(1)} %copy-done.4, f32[512,128]{0,1:T(8,128)S(1)} %copy-done.9, f32[512,128]{0,1:T(8,128)S(1)} %copy-done.7), kind=kOutput, calls=%fused_computation.2 | convolution fusion | flops 2622488576 | bytes 7340032 | tf_op jit(solution)/shard_map/dot_general | solution.py:47
  (46 shorter events, 2.3 us)
Async XLA Ops:
  7.2 1.5 copy-start
  7.2 105.4 %all-reduce.5.cloned.1.call-start = ((), (), s32[]{:S(2)}) async-start(), calls=%async_computation | async-start | bytes 1048576 | tf_op jit(solution)/shard_map/psum | solution.py:42
  14.6 210.1 %all-reduce.7.cloned.1.call-start = ((), (), s32[]{:S(2)}) async-start(), calls=%async_computation.1 | async-start | bytes 524288 | tf_op jit(solution)/shard_map/psum | solution.py:36
  115.5 304.8 %all-reduce.9.cloned.1.call-start = ((), (), s32[]{:S(2)}) async-start(), calls=%async_computation.2 | async-start | bytes 3407872 | tf_op jit(solution)/shard_map/psum | solution.py:45
  266.1 32.0 %copy-start.2 = (bf16[512,1664]{1,0:T(8,128)(2,1)S(1)}, bf16[512,1664]{1,0:T(8,128)(2,1)}, u32[]{:S(2)}) copy-start(bf16[512,1664]{1,0:T(8,128)(2,1)} %param.4) | copy-start | bytes 5111812
  295.3 2.1 copy-start.6
  297.4 0.7 copy-start.8
  420.2 34.9 %copy-start.1 = (f32[1664,256]{1,0:T(8,128)S(1)}, f32[1664,256]{1,0:T(8,128)}, u32[]{:S(2)}) copy-start(f32[1664,256]{1,0:T(8,128)} %all-reduce.9.cloned.1.call-done) | copy-start | bytes 5111812
  455.1 1.0 copy-start.7
  455.2 1.0 copy-start.9
  455.2 1.6 copy-start.10
  456.8 7.2 %copy-start.5 = (f32[1664,256]{1,0:T(8,128)}, f32[1664,256]{1,0:T(8,128)S(1)}, u32[]{:S(2)}) copy-start(f32[1664,256]{1,0:T(8,128)S(1)} %broadcast_divide_fusion) | copy-start | bytes 5111812
  456.8 7.2 %copy-start.3 = (bf16[512,1664]{1,0:T(8,128)(2,1)S(1)}, bf16[512,1664]{1,0:T(8,128)(2,1)}, u32[]{:S(2)}) copy-start(bf16[512,1664]{1,0:T(8,128)(2,1)} %param.4) | copy-start | bytes 5111812
  456.8 7.2 %copy-start.4 = (bf16[512,1664]{1,0:T(8,128)(2,1)S(1)}, bf16[512,1664]{1,0:T(8,128)(2,1)}, u32[]{:S(2)}) copy-start(bf16[512,1664]{1,0:T(8,128)(2,1)} %param.5) | copy-start | bytes 5111812
Sparse Core Ops, SparseCore 0:
  14.7 97.7 all-reduce.4
  115.6 109.0 all-reduce.6
  306.4 113.7 all-reduce.8
where the time goes:
time: 483 us; the launch traced here: 478 us
  waiting for transfers between devices  321 us (66%)
  other arithmetic  60.8 us (13%)
  matrix products  35.4 us (7%)
  blocking collectives  33.1 us (7%)
  between operations  15.9 us (3%)
  local copies, waits for them, and re-layouts  11.4 us (2%)
    psum x1, waiting for transfers between devices, local(): right_part = lax.psum(cross_product(buffer, ortho), 'row')  114 us
    psum x1, waiting for transfers between devices, gram_total(): return lax.psum(gram_of(left), 'row')  109 us
    psum x1, waiting for transfers between devices, local(): left = lax.psum(jnp.dot(buffer, right_factor, precision=high), 'col')  97.9 us
    another operation x6, other arithmetic, factor_gram(): return jnp.linalg.cholesky(gram + jitter * jnp.eye(rank, dtype=jnp.float32))  34 us
    psum x1, blocking collectives, local(): squares = lax.psum(jnp.sum(right_part * right_part, axis=0), 'col')  33.1 us
    another operation x3, other arithmetic, solve_right(): lax.linalg.triangular_solve(chol, block, left_side=False, lower=True, tra...  21.2 us
  transfers between devices with their start and end apart: 3, of which 3 were waited for; matrix products, arithmetic and copies ran while one was open for 0% of the time, Pallas kernels for 0%

commit v1 on v0

v1 whole, which is shorter than its diff:
```python
import jax
import jax.numpy as jnp
from jax import lax
from jax.experimental import pallas as pl
from jax.experimental.pallas import tpu as pltpu
from jax.sharding import PartitionSpec as P

ROWS = 8192
COLS = 26624
RANK = 256
HIGHEST = lax.Precision.HIGHEST
HIGH = lax.Precision.HIGH

decay = 0.95
step_size = 0.3

HALF = 128
GROUPS = HALF // 8
CORE_SWAP = [(i, i ^ 1) for i in range(16)]
Z_GROUPS = [[z * 2 + c for z in range(8)] for c in range(2)]


def z_shift(k):
    return [(z * 2 + c, ((z + k) % 8) * 2 + c) for z in range(8) for c in range(2)]


def dot_nt(a, b, precision=HIGHEST):
    return lax.dot_general(
        a, b, (((1,), (1,)), ((), ())), precision=precision, preferred_element_type=jnp.float32
    )


def dot_nn(a, b, precision=HIGHEST):
    return lax.dot_general(
        a, b, (((1,), (0,)), ((), ())), precision=precision, preferred_element_type=jnp.float32
    )


def dot_tn(a, b, precision=HIGHEST):
    return lax.dot_general(
        a, b, (((0,), (0,)), ((), ())), precision=precision, preferred_element_type=jnp.float32
    )


def inverse_factor(block):
    rows = lax.broadcasted_iota(jnp.int32, (8, HALF), 0)
    lanes = lax.broadcasted_iota(jnp.int32, (8, HALF), 1)
    a = [block[8 * g : 8 * g + 8, :] for g in range(GROUPS)]
    x = [jnp.where(lanes == rows + 8 * g, 1.0, 0.0).astype(jnp.float32) for g in range(GROUPS)]
    diag = [jnp.ones((8, HALF), jnp.float32) for _ in range(GROUPS)]
    for j in range(HALF):
        g, s = divmod(j, 8)
        column = jnp.broadcast_to(a[g][:, j : j + 1], (8, HALF))
        pivot = jnp.broadcast_to(column[s : s + 1, :], (8, HALF))
        diag[g] = jnp.where(rows == s, pivot, diag[g])
        inverse = 1.0 / pivot
        a_row = jnp.broadcast_to(a[g][s : s + 1, :], (8, HALF)) * inverse
        x_row = jnp.broadcast_to(x[g][s : s + 1, :], (8, HALF)) * inverse
        if s < 7:
            below = jnp.where(rows > s, column, 0.0)
            a[g] = a[g] - below * a_row
            x[g] = x[g] - below * x_row
        for h in range(g + 1, GROUPS):
            column = jnp.broadcast_to(a[h][:, j : j + 1], (8, HALF))
            a[h] = a[h] - column * a_row
            x[h] = x[h] - column * x_row
    return jnp.concatenate([x[g] * lax.rsqrt(diag[g]) for g in range(GROUPS)], axis=0)


def first_kernel(gram_ref, jitter_ref, w_ref):
    gram = gram_ref[...]
    eye = lax.broadcasted_iota(jnp.int32, (RANK, RANK), 0) == lax.broadcasted_iota(
        jnp.int32, (RANK, RANK), 1
    )
    jitter = 1e-06 * jnp.sum(jnp.where(eye, gram, 0.0)) / RANK
    jitter_ref[...] = jnp.full((8, HALF), jitter, jnp.float32)
    rows = lax.broadcasted_iota(jnp.int32, (HALF, HALF), 0)
    lanes = lax.broadcasted_iota(jnp.int32, (HALF, HALF), 1)
    w_ref[...] = inverse_factor(gram[:HALF, :HALF] + jnp.where(rows == lanes, jitter, 0.0))


def second_kernel(gram_ref, jitter_ref, first_ref, w_ref):
    first = first_ref[...]
    rows = lax.broadcasted_iota(jnp.int32, (HALF, HALF), 0)
    lanes = lax.broadcasted_iota(jnp.int32, (HALF, HALF), 1)
    low = dot_nt(gram_ref[HALF:, :HALF], first)
    rest = gram_ref[HALF:, HALF:] + jnp.where(rows == lanes, jitter_ref[0:1, :], 0.0)
    second = inverse_factor(rest - dot_nt(low, low))
    w_ref[:HALF, :HALF] = first
    w_ref[:HALF, HALF:] = jnp.zeros((HALF, HALF), jnp.float32)
    w_ref[HALF:, :HALF] = -dot_nn(second, dot_nn(low, first))
    w_ref[HALF:, HALF:] = second


def inverse_cholesky(gram):
    jitter, first = pl.pallas_call(
        first_kernel,
        out_shape=(
            jax.ShapeDtypeStruct((8, HALF), jnp.float32),
            jax.ShapeDtypeStruct((HALF, HALF), jnp.float32),
        ),
        cost_estimate=pl.CostEstimate(flops=6000000, bytes_accessed=20000000, transcendentals=0),
    )(gram)
    return pl.pallas_call(
        second_kernel,
        out_shape=jax.ShapeDtypeStruct((RANK, RANK), jnp.float32),
        cost_estimate=pl.CostEstimate(flops=6000000, bytes_accessed=20000000, transcendentals=0),
    )(gram, jitter, first)


def exchange(pieces, axis, groups=None):
    return lax.all_to_all(pieces, axis, 0, 0, axis_index_groups=groups)


def spread(piece, axis, count):
    return exchange(jnp.broadcast_to(piece[None], (count,) + piece.shape), axis)


def gather_z(piece):
    z = lax.axis_index("row") // 2
    out = jnp.zeros((8,) + piece.shape, piece.dtype)
    out = lax.dynamic_update_slice(out, piece[None], (z, 0, 0))
    up = down = piece
    for k in range(1, 4):
        up = lax.ppermute(up, "row", z_shift(1))
        down = lax.ppermute(down, "row", z_shift(-1))
        out = lax.dynamic_update_slice(out, up[None], ((z - k) % 8, 0, 0))
        out = lax.dynamic_update_slice(out, down[None], ((z + k) % 8, 0, 0))
    half = piece.shape[0] // 2 // 8 * 8
    up = lax.ppermute(up[:half], "row", z_shift(1))
    down = lax.ppermute(down[half:], "row", z_shift(-1))
    last = jnp.concatenate([up, down], axis=0)
    return lax.dynamic_update_slice(out, last[None], ((z + 4) % 8, 0, 0))


def local(gradient, momentum, weight, right_factor):
    core = lax.axis_index("row") % 2
    buffer = momentum.astype(jnp.float32) + gradient.astype(jnp.float32)
    partial = dot_nn(buffer, right_factor)
    piece = jnp.sum(exchange(partial.reshape(16, 32, RANK), "col"), axis=0)
    left = spread(piece, "col", 16).reshape(512, RANK)
    gram_part = dot_tn(left, left)
    y_part = dot_tn(buffer, left)
    both = jnp.concatenate(
        [y_part.reshape(2, 8, 104, RANK), gram_part.reshape(2, 8, 16, RANK)], axis=2
    )
    mine = lax.dynamic_index_in_dim(both, core, 0, keepdims=False)
    other = lax.dynamic_index_in_dim(both, 1 - core, 0, keepdims=False)
    mine = mine + lax.ppermute(other, "row", CORE_SWAP)
    mine = jnp.sum(exchange(mine, "row", Z_GROUPS), axis=0)
    gram = spread(mine[104:], "row", 16).reshape(8, 2, 16, RANK)
    gram = jnp.transpose(gram, (1, 0, 2, 3)).reshape(RANK, RANK)
    inverse = inverse_cholesky(gram)
    y_mine = gather_z(mine[:104]).reshape(832, RANK)
    y_other = lax.ppermute(y_mine, "row", CORE_SWAP)
    y = jnp.zeros((1664, RANK), jnp.float32)
    y = lax.dynamic_update_slice(y, y_mine, (core * 832, 0))
    y = lax.dynamic_update_slice(y, y_other, ((1 - core) * 832, 0))
    right = dot_nt(y, inverse)
    ortho = dot_nt(left, inverse)
    squares = jnp.sum(spread(jnp.sum(right * right, axis=0, keepdims=True), "col", 16), axis=(0, 1))
    new_momentum = (buffer - (1.0 - decay) * dot_nt(ortho, right, HIGH)).astype(jnp.bfloat16)
    new_factor = right / jnp.sqrt(squares / COLS + 1e-06)
    update = dot_nt(ortho, new_factor, HIGH)
    new_weight = (weight.astype(jnp.float32) - step_size * jnp.sqrt(ROWS / RANK) * update).astype(
        jnp.bfloat16
    )
    return (new_weight, new_momentum, new_factor)


def solution(mesh):
    in_specs = (P("row", "col"), P("row", "col"), P("row", "col"), P("col", None))
    out_specs = (P("row", "col"), P("row", "col"), P("col", None))
    return jax.shard_map(local, mesh=mesh, in_specs=in_specs, out_specs=out_specs, check_vma=False)
```

time: 483 us -> 204 us (0.42)
  waiting for transfers between devices: 321 us -> 63.1 us
  other arithmetic: 60.8 us -> 8.09 us
  starting transfers between devices: 0.3 us -> 47.9 us
  Pallas kernels: 0 us -> 38.5 us
  blocking collectives: 33.1 us -> 0 us
  between operations: 15.9 us -> 0.88 us
  matrix products: 35.4 us -> 26.5 us
  local copies, waits for them, and re-layouts: 11.4 us -> 17.9 us
    psum x3 -> x0, waiting for transfers between devices: 321 us -> none  [the longest x1 114 us: local(): right_part = lax.psum(cross_product(buffer, ortho), 'row')]
    another operation x9 -> x0, other arithmetic: 55.3 us -> none  [the longest x6 34 us: factor_gram(): return jnp.linalg.cholesky(gram + jitter * jnp.eye(rank, dtype=jnp.float32))]
    all_to_all x0 -> x5, waiting for transfers between devices: none -> 50.3 us  [exchange(): return lax.all_to_all(pieces, axis, 0, 0, axis_index_groups=groups)]
    pallas_call x0 -> x2, Pallas kernels: none -> 38.5 us  [the longest x1 19.7 us: inverse_cholesky(): pl.pallas_call(second_kernel, out_shape=jax.ShapeDtypeStruct((RANK, RANK)...]
    psum x1 -> x0, blocking collectives: 33.1 us -> none  [local(): squares = lax.psum(jnp.sum(right_part * right_part, axis=0), 'col')]
    all_to_all x0 -> x5, starting transfers between devices: none -> 28.4 us  [exchange(): return lax.all_to_all(pieces, axis, 0, 0, axis_index_groups=groups)]
    ppermute x0 -> x10, starting transfers between devices: none -> 19.5 us  [the longest x3 8.01 us: gather_z(): down = lax.ppermute(down, 'row', z_shift(-1))]
    ppermute x0 -> x10, waiting for transfers between devices: none -> 12.9 us  [the longest x3 4.55 us: gather_z(): up = lax.ppermute(up, 'row', z_shift(1))]
  transfers between devices with their start and end apart: 3 -> 15, of which waited for: 3 -> 10; matrix products, arithmetic and copies ran while one was open for 0% -> 10% of each run, Pallas kernels for 0% -> 19%
where the time goes in v1:
time: 204 us; the launch traced here: 203 us
  waiting for transfers between devices  63.1 us (31%)
  starting transfers between devices  47.9 us (23%)
  Pallas kernels  38.5 us (19%)
  matrix products  26.5 us (13%)
  local copies, waits for them, and re-layouts  17.9 us (9%)
  other arithmetic  8.09 us (4%)
    all_to_all x5, waiting for transfers between devices, exchange(): return lax.all_to_all(pieces, axis, 0, 0, axis_index_groups=groups)  50.3 us
    all_to_all x5, starting transfers between devices, exchange(): return lax.all_to_all(pieces, axis, 0, 0, axis_index_groups=groups)  28.4 us
    pallas_call x1, Pallas kernels, inverse_cholesky(): pl.pallas_call(second_kernel, out_shape=jax.ShapeDtypeStruct((RANK, RANK)...  19.7 us
    pallas_call x1, Pallas kernels, inverse_cholesky(): pl.pallas_call(first_kernel, out_shape=(jax.ShapeDtypeStruct((8, HALF), j...  18.9 us
    dot_general x4, matrix products, dot_nt(): lax.dot_general(a, b, (((1,), (1,)), ((), ())), precision=precision, pref...  14 us
    ppermute x3, starting transfers between devices, gather_z(): down = lax.ppermute(down, 'row', z_shift(-1))  8.01 us
    dot_general x2, local copies, waits for them, and re-layouts, dot_tn(): lax.dot_general(a, b, (((0,), (0,)), ((), ())), precision=precision, pref...  6.77 us
    dot_general x2, matrix products, dot_tn(): lax.dot_general(a, b, (((0,), (0,)), ((), ())), precision=precision, pref...  6.59 us
  transfers between devices with their start and end apart: 15, of which 10 were waited for; matrix products, arithmetic and copies ran while one was open for 10% of the time, Pallas kernels for 19%

profile of v1, /device:TPU:1, one launch (start us, length us, event | category | flops | bytes accessed | tf_op | source)
XLA Modules:
  0.0 202.9 jit_solution(8036327066272611227)
XLA Ops:
  2.1 6.0 %fusion.1 = f32[512,256]{1,0:T(8,128)} fusion(f32[1664,256]{1,0:T(8,128)S(1)} %copy-done, bf16[512,1664]{1,0:T(8,128)(2,1)} %param.4, bf16[512,1664]{1,0:T(8,128)(2,1)} %param.5), kind=kOutput, calls=%fused_computation.4 | convolution fusion | flops 2619801600 | bytes 5636096 | tf_op jit(solution)/shard_map/dot_general | solution.py:34
  8.0 7.8 %all-to-all-start = ((f32[16,32,256]{2,1,0:T(8,128)}), f32[16,32,256]{2,1,0:T(8,128)}, u32[]{:S(2)}, u32[]{:S(2)}) async-start(f32[16,32,256]{2,1,0:T(8,128)} %bitcast.60), calls=%async_computation | async-start | bytes 1048576 | tf_op jit(solution)/shard_map/all_to_all | solution.py:112
  15.8 10.5 %all-to-all-done = f32[16,32,256]{2,1,0:T(8,128)} async-done(((f32[16,32,256]{2,1,0:T(8,128)}), f32[16,32,256]{2,1,0:T(8,128)}, u32[]{:S(2)}, u32[]{:S(2)}) %all-to-all-start) | async-done | bytes 524320 | tf_op jit(solution)/shard_map/all_to_all | solution.py:112
  28.3 4.2 %all-to-all-start.1 = ((f32[16,32,256]{2,1,0:T(8,128)}), f32[16,32,256]{2,1,0:T(8,128)}, u32[]{:S(2)}, u32[]{:S(2)}) async-start(f32[16,32,256]{2,1,0:T(8,128)} %broadcast_in_dim.48), calls=%async_computation.1 | async-start | bytes 1048576 | tf_op jit(solution)/shard_map/all_to_all | solution.py:112
  32.6 3.5 %fusion = f32[1664,512]{0,1:T(8,128)} fusion(bf16[512,1664]{1,0:T(8,128)(2,1)S(1)} %copy-done.1, bf16[512,1664]{1,0:T(8,128)(2,1)} %param.5), kind=kLoop, calls=%fused_computation.3 | loop fusion | flops 2555904 | bytes 6815744 | tf_op jit(solution)/shard_map/dot_general | solution.py:40
  36.1 4.7 %copy.15 = f32[1664,512]{1,0:T(8,128)} copy(f32[1664,512]{0,1:T(8,128)} %fusion) | data formatting | bytes 6815744 | tf_op jit(solution)/shard_map/dot_general | solution.py:40
  42.3 2.0 %copy.16 = f32[256,512]{1,0:T(8,128)} copy(f32[256,512]{0,1:T(8,128)} %bitcast.6) | data formatting | bytes 1048576 | tf_op jit(solution)/shard_map/dot_general | solution.py:40
  44.3 4.9 %fusion.8 = f32[2,8,104,256]{3,2,1,0:T(8,128)S(1)} fusion(f32[2,8,104,512]{3,2,1,0:T(8,128)} %bitcast.54, f32[512,256,1,1]{1,0,3,2:T(8,128)} %bitcast.5), kind=kOutput, calls=%fused_computation.28 | convolution fusion | flops 2617245696 | bytes 5636096 | tf_op jit(solution)/shard_map/dot_general | solution.py:40
  52.6 2.8 %collective-permute-start = (f32[8,120,256]{2,1,0:T(8,128)}, f32[8,120,256]{2,1,0:T(8,128)}, u32[]{:S(2)}, u32[]{:S(2)}) collective-permute-start(f32[8,120,256]{2,1,0:T(8,128)} %fusion.3), channel_id=1, source_target_pairs={{0,16},{16,0},{32,48},{48,32},{64,80},{80,64},{96,112},{112,96},{1... | collective-permute-start | bytes 2949128 | tf_op jit(solution)/shard_map/ppermute | solution.py:149
  55.5 2.5 %collective-permute-done = f32[8,120,256]{2,1,0:T(8,128)} collective-permute-done((f32[8,120,256]{2,1,0:T(8,128)}, f32[8,120,256]{2,1,0:T(8,128)}, u32[]{:S(2)}, u32[]{:S(2)}) %collective-permute-start) | collective-permute-done | bytes 983072 | tf_op jit(solution)/shard_map/ppermute | solution.py:149
  58.0 2.3 %fusion.6 = f32[8,120,256]{2,1,0:T(8,128)} fusion(f32[8,120,256]{2,1,0:T(8,128)} %collective-permute-done, s32[]{:T(128)S(6)} %select_n.77, f32[2,8,104,256]{3,2,1,0:T(8,128)S(1)} %fusion.8, f32[2,8,16,256]{3,2,1,0:T(8,128)} %copy-done.4), kind=kLoop, calls=%fused_computation.14 | loop fusion | flops 491520 | bytes 3932164 | tf_op jit(solution)/shard_map/add | solution.py:149
  60.3 8.2 %all-to-all-start.2 = ((f32[8,120,256]{2,1,0:T(8,128)}), f32[8,120,256]{2,1,0:T(8,128)S(1)}, u32[]{:S(2)}, u32[]{:S(2)}) async-start(f32[8,120,256]{2,1,0:T(8,128)} %fusion.6), calls=%async_computation.2 | async-start | bytes 1966080 | tf_op jit(solution)/shard_map/all_to_all | solution.py:112
  68.5 27.8 %all-to-all-done.2 = f32[8,120,256]{2,1,0:T(8,128)S(1)} async-done(((f32[8,120,256]{2,1,0:T(8,128)}), f32[8,120,256]{2,1,0:T(8,128)S(1)}, u32[]{:S(2)}, u32[]{:S(2)}) %all-to-all-start.2) | async-done | bytes 983072 | tf_op jit(solution)/shard_map/all_to_all | solution.py:112
  96.4 2.7 %collective-permute-start.2 = (f32[104,256]{1,0:T(8,128)S(1)}, f32[104,256]{1,0:T(8,128)S(1)}, u32[]{:S(2)}, u32[]{:S(2)}) collective-permute-start(f32[104,256]{1,0:T(8,128)S(1)} %slice.17), channel_id=1, source_target_pairs={{0,224},{16,240},{32,0},{48,16},{64,32},{80,48},{96,64},{112,80},{... | collective-permute-start | bytes 319496 | tf_op jit(solution)/shard_map/ppermute | solution.py:126
  99.2 2.5 %collective-permute-done.1 = f32[104,256]{1,0:T(8,128)S(1)} collective-permute-done((f32[104,256]{1,0:T(8,128)S(1)}, f32[104,256]{1,0:T(8,128)S(1)}, u32[]{:S(2)}, u32[]{:S(2)}) %collective-permute-start.1) | collective-permute-done | bytes 106528 | tf_op jit(solution)/shard_map/ppermute | solution.py:125
  101.7 2.7 %collective-permute-start.4 = (f32[104,256]{1,0:T(8,128)S(1)}, f32[104,256]{1,0:T(8,128)S(1)}, u32[]{:S(2)}, u32[]{:S(2)}) collective-permute-start(f32[104,256]{1,0:T(8,128)S(1)} %collective-permute-done.2), channel_id=1, source_target_pairs={{0,224},{16,240},{32,0},{48,16},{64,32},{80,48},{96,64},{112,80},{... | collective-permute-start | bytes 319496 | tf_op jit(solution)/shard_map/ppermute | solution.py:126
  104.4 2.0 %collective-permute-done.3 = f32[104,256]{1,0:T(8,128)S(1)} collective-permute-done((f32[104,256]{1,0:T(8,128)S(1)}, f32[104,256]{1,0:T(8,128)S(1)}, u32[]{:S(2)}, u32[]{:S(2)}) %collective-permute-start.3) | collective-permute-done | bytes 106528 | tf_op jit(solution)/shard_map/ppermute | solution.py:125
  106.4 2.7 %collective-permute-start.6 = (f32[104,256]{1,0:T(8,128)S(1)}, f32[104,256]{1,0:T(8,128)S(1)}, u32[]{:S(2)}, u32[]{:S(2)}) collective-permute-start(f32[104,256]{1,0:T(8,128)S(1)} %collective-permute-done.4), channel_id=1, source_target_pairs={{0,224},{16,240},{32,0},{48,16},{64,32},{80,48},{96,64},{112,80},{... | collective-permute-start | bytes 319496 | tf_op jit(solution)/shard_map/ppermute | solution.py:126
  109.2 1.7 collective-permute-done.6
  110.8 3.0 %collective-permute-start.8 = (f32[56,256]{1,0:T(8,128)S(1)}, f32[56,256]{1,0:T(8,128)S(1)}, u32[]{:S(2)}, u32[]{:S(2)}) collective-permute-start(f32[56,256]{1,0:T(8,128)S(1)} %slice.19), channel_id=1, source_target_pairs={{0,224},{16,240},{32,0},{48,16},{64,32},{80,48},{96,64},{112,80},{... | collective-permute-start | bytes 172040 | tf_op jit(solution)/shard_map/ppermute | solution.py:131
  114.0 4.1 %collective-permute-done.7 = f32[48,256]{1,0:T(8,128)S(1)} collective-permute-done((f32[48,256]{1,0:T(8,128)S(1)}, f32[48,256]{1,0:T(8,128)S(1)}, u32[]{:S(2)}, u32[]{:S(2)}) %collective-permute-start.7) | collective-permute-done | bytes 49184 | tf_op jit(solution)/shard_map/ppermute | solution.py:130
  118.1 5.4 %collective-permute-start.9 = (f32[832,256]{1,0:T(8,128)S(1)}, f32[832,256]{1,0:T(8,128)}, u32[]{:S(2)}, u32[]{:S(2)}) collective-permute-start(f32[832,256]{1,0:T(8,128)S(1)} %bitcast.55), channel_id=1, source_target_pairs={{0,16},{16,0},{32,48},{48,32},{64,80},{80,64},{96,112},{112,96},{1... | collective-permute-start | bytes 2555912 | tf_op jit(solution)/shard_map/ppermute | solution.py:155
  124.3 3.7 %all-to-all-start.3 = ((f32[16,16,256]{2,1,0:T(8,128)}), f32[16,16,256]{2,1,0:T(8,128)S(1)}, u32[]{:S(2)}, u32[]{:S(2)}) async-start(f32[16,16,256]{2,1,0:T(8,128)} %broadcast_in_dim.49), calls=%async_computation.3 | async-start | bytes 524288 | tf_op jit(solution)/shard_map/all_to_all | solution.py:112
  130.2 9.3 %all-to-all-done.3 = f32[16,16,256]{2,1,0:T(8,128)S(1)} async-done(((f32[16,16,256]{2,1,0:T(8,128)}), f32[16,16,256]{2,1,0:T(8,128)S(1)}, u32[]{:S(2)}, u32[]{:S(2)}) %all-to-all-start.3) | async-done | bytes 262176 | tf_op jit(solution)/shard_map/all_to_all | solution.py:112
  140.3 18.9 %shard_map.67 = (f32[8,128]{1,0:T(8,128)}, f32[128,128]{1,0:T(8,128)}) custom-call(f32[256,256]{1,0:T(8,128)} %bitcast.57), custom_call_target="tpu_custom_call" | custom-call | flops 6000000 | bytes 20000000 | tf_op jit(solution)/shard_map/pallas_call | solution.py:96
  159.2 19.7 %shard_map.68 = f32[256,256]{1,0:T(8,128)} custom-call(f32[256,256]{1,0:T(8,128)} %bitcast.58, f32[8,128]{1,0:T(8,128)} %get-tuple-element.5.jitter_ref, f32[128,128]{1,0:T(8,128)} %get-tuple-element.6.first_ref), custom_call_target="tpu_custom_call" | custom-call | flops 6000000 | bytes 20000000 | tf_op jit(solution)/shard_map/pallas_call | solution.py:104
  178.8 2.6 %fusion.10 = f32[512,256]{1,0:T(8,128)} fusion(f32[512,256]{1,0:T(8,128)} %bitcast.1, f32[256,256]{1,0:T(8,128)} %shard_map.68), kind=kOutput, calls=%fused_computation.30 | convolution fusion | flops 402653184 | bytes 1310720 | tf_op jit(solution)/shard_map/dot_general | solution.py:28
  181.4 2.1 %constant_dynamic-update-slice_fusion = f32[1664,256]{1,0:T(8,128)} fusion(f32[1664,256]{1,0:T(8,128)} %constant_dynamic-update-slice_fusion.1, f32[832,256]{1,0:T(8,128)} %collective-permute-done.9, s32[]{:T(128)S(6)} %select_n.96), kind=kLoop, calls=%fused_computation.25 | loop fusion | bytes 1703940 | tf_op jit(solution)/shard_map/dynamic_update_slice | solution.py:158
  183.5 3.0 %multiply_reduce_fusion = (f32[256]{0:T(256)S(1)}, f32[1664,256]{1,0:T(8,128)S(1)}) fusion(f32[1664,256]{1,0:T(8,128)} %constant_dynamic-update-slice_fusion, f32[256,256]{1,0:T(8,128)S(1)} %copy-done.5), kind=kOutput, calls=%fused_computation.9 | convolution fusion | flops 1309474560 | bytes 3671040 | tf_op jit(solution)/shard_map/dot_general | solution.py:28
  187.1 4.5 %all-to-all-start.4 = ((f32[16,1,256]{2,1,0:T(1,128)}), f32[16,1,256]{2,1,0:T(1,128)S(1)}, u32[]{:S(2)}, u32[]{:S(2)}) async-start(f32[16,1,256]{2,1,0:T(1,128)} %broadcast_in_dim.60), calls=%async_computation.4 | async-start | bytes 32768 | tf_op jit(solution)/shard_map/all_to_all | solution.py:112
  191.7 5.3 %subtract_convert_fusion = bf16[512,1664]{1,0:T(8,128)(2,1)} fusion(f32[512,256]{1,0:T(8,128)} %fusion.10, f32[1664,256]{1,0:T(8,128)S(1)} %get-tuple-element.8, bf16[512,1664]{1,0:T(8,128)(2,1)} %param.4, bf16[512,1664]{1,0:T(8,128)(2,1)} %param.5), kind=kOutput, calls=%fused_computation | convolution fusion | flops 1313734656 | bytes 7340032 | tf_op jit(solution)/shard_map/dot_general | solution.py:28
  199.8 3.1 %subtract_convert_fusion.1 = bf16[512,1664]{1,0:T(8,128)(2,1)} fusion(bf16[512,1664]{1,0:T(8,128)(2,1)S(1)} %copy-done.7, f32[512,256]{1,0:T(8,128)S(1)} %copy-done.3, f32[1664,256]{1,0:T(8,128)S(1)} %broadcast_divide_fusion), kind=kOutput, calls=%fused_computation.1 | convolution fusion | flops 1312030720 | bytes 5636096 | tf_op jit(solution)/shard_map/dot_general | solution.py:28
  (53 shorter events, 15.7 us)
Async XLA Ops:
  0.6 1.5 copy-start
  8.0 24.5 %copy-start.1 = (bf16[512,1664]{1,0:T(8,128)(2,1)S(1)}, bf16[512,1664]{1,0:T(8,128)(2,1)}, u32[]{:S(2)}) copy-start(bf16[512,1664]{1,0:T(8,128)(2,1)} %param.4) | copy-start | bytes 5111812
  8.0 18.3 %all-to-all-start = ((f32[16,32,256]{2,1,0:T(8,128)}), f32[16,32,256]{2,1,0:T(8,128)}, u32[]{:S(2)}, u32[]{:S(2)}) async-start(f32[16,32,256]{2,1,0:T(8,128)} %bitcast.60), calls=%async_computation | async-start | bytes 1048576 | tf_op jit(solution)/shard_map/all_to_all | solution.py:112
  28.3 14.0 %all-to-all-start.1 = ((f32[16,32,256]{2,1,0:T(8,128)}), f32[16,32,256]{2,1,0:T(8,128)}, u32[]{:S(2)}, u32[]{:S(2)}) async-start(f32[16,32,256]{2,1,0:T(8,128)} %broadcast_in_dim.48), calls=%async_computation.1 | async-start | bytes 1048576 | tf_op jit(solution)/shard_map/all_to_all | solution.py:112
  44.3 5.0 %copy-start.6 = (f32[256,512]{1,0:T(8,128)S(1)}, f32[256,512]{1,0:T(8,128)}, u32[]{:S(2)}) copy-start(f32[256,512]{1,0:T(8,128)} %copy.16) | copy-start | bytes 1572868
  50.9 0.7 copy-start.4
  52.6 5.4 %collective-permute-start = (f32[8,120,256]{2,1,0:T(8,128)}, f32[8,120,256]{2,1,0:T(8,128)}, u32[]{:S(2)}, u32[]{:S(2)}) collective-permute-start(f32[8,120,256]{2,1,0:T(8,128)} %fusion.3), channel_id=1, source_target_pairs={{0,16},{16,0},{32,48},{48,32},{64,80},{80,64},{96,112},{112,96},{1... | collective-permute-start | bytes 2949128 | tf_op jit(solution)/shard_map/ppermute | solution.py:149
  60.3 36.0 %all-to-all-start.2 = ((f32[8,120,256]{2,1,0:T(8,128)}), f32[8,120,256]{2,1,0:T(8,128)S(1)}, u32[]{:S(2)}, u32[]{:S(2)}) async-start(f32[8,120,256]{2,1,0:T(8,128)} %fusion.6), calls=%async_computation.2 | async-start | bytes 1966080 | tf_op jit(solution)/shard_map/all_to_all | solution.py:112
  96.3 5.3 %collective-permute-start.1 = (f32[104,256]{1,0:T(8,128)S(1)}, f32[104,256]{1,0:T(8,128)S(1)}, u32[]{:S(2)}, u32[]{:S(2)}) collective-permute-start(f32[104,256]{1,0:T(8,128)S(1)} %slice.17), channel_id=1, source_target_pairs={{0,32},{16,48},{32,64},{48,80},{64,96},{80,112},{96,128},{112,144}... | collective-permute-start | bytes 319496 | tf_op jit(solution)/shard_map/ppermute | solution.py:125
  96.4 5.3 %collective-permute-start.2 = (f32[104,256]{1,0:T(8,128)S(1)}, f32[104,256]{1,0:T(8,128)S(1)}, u32[]{:S(2)}, u32[]{:S(2)}) collective-permute-start(f32[104,256]{1,0:T(8,128)S(1)} %slice.17), channel_id=1, source_target_pairs={{0,224},{16,240},{32,0},{48,16},{64,32},{80,48},{96,64},{112,80},{... | collective-permute-start | bytes 319496 | tf_op jit(solution)/shard_map/ppermute | solution.py:126
  101.7 4.8 %collective-permute-start.3 = (f32[104,256]{1,0:T(8,128)S(1)}, f32[104,256]{1,0:T(8,128)S(1)}, u32[]{:S(2)}, u32[]{:S(2)}) collective-permute-start(f32[104,256]{1,0:T(8,128)S(1)} %collective-permute-done.1), channel_id=1, source_target_pairs={{0,32},{16,48},{32,64},{48,80},{64,96},{80,112},{96,128},{112,144}... | collective-permute-start | bytes 319496 | tf_op jit(solution)/shard_map/ppermute | solution.py:125
  101.7 4.8 %collective-permute-start.4 = (f32[104,256]{1,0:T(8,128)S(1)}, f32[104,256]{1,0:T(8,128)S(1)}, u32[]{:S(2)}, u32[]{:S(2)}) collective-permute-start(f32[104,256]{1,0:T(8,128)S(1)} %collective-permute-done.2), channel_id=1, source_target_pairs={{0,224},{16,240},{32,0},{48,16},{64,32},{80,48},{96,64},{112,80},{... | collective-permute-start | bytes 319496 | tf_op jit(solution)/shard_map/ppermute | solution.py:126
  106.4 7.5 %collective-permute-start.5 = (f32[104,256]{1,0:T(8,128)S(1)}, f32[104,256]{1,0:T(8,128)S(1)}, u32[]{:S(2)}, u32[]{:S(2)}) collective-permute-start(f32[104,256]{1,0:T(8,128)S(1)} %collective-permute-done.3), channel_id=1, source_target_pairs={{0,32},{16,48},{32,64},{48,80},{64,96},{80,112},{96,128},{112,144}... | collective-permute-start | bytes 319496 | tf_op jit(solution)/shard_map/ppermute | solution.py:125
  106.4 4.4 %collective-permute-start.6 = (f32[104,256]{1,0:T(8,128)S(1)}, f32[104,256]{1,0:T(8,128)S(1)}, u32[]{:S(2)}, u32[]{:S(2)}) collective-permute-start(f32[104,256]{1,0:T(8,128)S(1)} %collective-permute-done.4), channel_id=1, source_target_pairs={{0,224},{16,240},{32,0},{48,16},{64,32},{80,48},{96,64},{112,80},{... | collective-permute-start | bytes 319496 | tf_op jit(solution)/shard_map/ppermute | solution.py:126
  110.8 7.3 %collective-permute-start.8 = (f32[56,256]{1,0:T(8,128)S(1)}, f32[56,256]{1,0:T(8,128)S(1)}, u32[]{:S(2)}, u32[]{:S(2)}) collective-permute-start(f32[56,256]{1,0:T(8,128)S(1)} %slice.19), channel_id=1, source_target_pairs={{0,224},{16,240},{32,0},{48,16},{64,32},{80,48},{96,64},{112,80},{... | collective-permute-start | bytes 172040 | tf_op jit(solution)/shard_map/ppermute | solution.py:131
  113.9 4.2 %collective-permute-start.7 = (f32[48,256]{1,0:T(8,128)S(1)}, f32[48,256]{1,0:T(8,128)S(1)}, u32[]{:S(2)}, u32[]{:S(2)}) collective-permute-start(f32[48,256]{1,0:T(8,128)S(1)} %slice.18), channel_id=1, source_target_pairs={{0,32},{16,48},{32,64},{48,80},{64,96},{80,112},{96,128},{112,144}... | collective-permute-start | bytes 147464 | tf_op jit(solution)/shard_map/ppermute | solution.py:130
  118.1 63.3 %collective-permute-start.9 = (f32[832,256]{1,0:T(8,128)S(1)}, f32[832,256]{1,0:T(8,128)}, u32[]{:S(2)}, u32[]{:S(2)}) collective-permute-start(f32[832,256]{1,0:T(8,128)S(1)} %bitcast.55), channel_id=1, source_target_pairs={{0,16},{16,0},{32,48},{48,32},{64,80},{80,64},{96,112},{112,96},{1... | collective-permute-start | bytes 2555912 | tf_op jit(solution)/shard_map/ppermute | solution.py:155
  124.3 15.3 %all-to-all-start.3 = ((f32[16,16,256]{2,1,0:T(8,128)}), f32[16,16,256]{2,1,0:T(8,128)S(1)}, u32[]{:S(2)}, u32[]{:S(2)}) async-start(f32[16,16,256]{2,1,0:T(8,128)} %broadcast_in_dim.49), calls=%async_computation.3 | async-start | bytes 524288 | tf_op jit(solution)/shard_map/all_to_all | solution.py:112
  178.8 4.7 %copy-start.5 = (f32[256,256]{1,0:T(8,128)S(1)}, f32[256,256]{1,0:T(8,128)}, u32[]{:S(2)}) copy-start(f32[256,256]{1,0:T(8,128)} %shard_map.68) | copy-start | bytes 786436
  187.1 10.9 %all-to-all-start.4 = ((f32[16,1,256]{2,1,0:T(1,128)}), f32[16,1,256]{2,1,0:T(1,128)S(1)}, u32[]{:S(2)}, u32[]{:S(2)}) async-start(f32[16,1,256]{2,1,0:T(1,128)} %broadcast_in_dim.60), calls=%async_computation.4 | async-start | bytes 32768 | tf_op jit(solution)/shard_map/all_to_all | solution.py:112
  198.1 1.0 copy-start.3
  198.1 1.6 copy-start.7
  199.8 3.1 %copy-start.2 = (f32[1664,256]{1,0:T(8,128)}, f32[1664,256]{1,0:T(8,128)S(1)}, u32[]{:S(2)}) copy-start(f32[1664,256]{1,0:T(8,128)S(1)} %broadcast_divide_fusion) | copy-start | bytes 5111812

commit v2 on v1

v2 whole, which is shorter than its diff:
```python
import jax
import jax.numpy as jnp
from jax import lax
from jax.experimental import pallas as pl
from jax.experimental.pallas import tpu as pltpu
from jax.sharding import PartitionSpec as P

ROWS = 8192
COLS = 26624
RANK = 256
HIGHEST = lax.Precision.HIGHEST
HIGH = lax.Precision.HIGH

decay = 0.95
step_size = 0.3

HALF = 128
GROUPS = HALF // 8
CORE_SWAP = [(i, i ^ 1) for i in range(16)]
Z_GROUPS = [[z * 2 + c for z in range(8)] for c in range(2)]


def dot_nt(a, b, precision=HIGHEST):
    return lax.dot_general(
        a, b, (((1,), (1,)), ((), ())), precision=precision, preferred_element_type=jnp.float32
    )


def dot_nn(a, b, precision=HIGHEST):
    return lax.dot_general(
        a, b, (((1,), (0,)), ((), ())), precision=precision, preferred_element_type=jnp.float32
    )


def dot_tn(a, b, precision=HIGHEST):
    return lax.dot_general(
        a, b, (((0,), (0,)), ((), ())), precision=precision, preferred_element_type=jnp.float32
    )


def inverse_factor(block):
    rows = lax.broadcasted_iota(jnp.int32, (8, HALF), 0)
    lanes = lax.broadcasted_iota(jnp.int32, (8, HALF), 1)
    a = [block[8 * g : 8 * g + 8, :] for g in range(GROUPS)]
    x = [jnp.where(lanes == rows + 8 * g, 1.0, 0.0).astype(jnp.float32) for g in range(GROUPS)]

    def lane(value, j):
        return jnp.broadcast_to(value[:, j : j + 1], (8, HALF))

    def row(value, s):
        return jnp.broadcast_to(value[s : s + 1, :], (8, HALF))

    done = []
    for g in range(GROUPS):
        columns = [lane(a[g], 8 * g + t) for t in range(8)]
        d = {(s, t): row(columns[t], s) for s in range(8) for t in range(s + 1)}
        a_rows = [row(a[g], t) for t in range(8)]
        x_rows = [row(x[g], t) for t in range(8)]
        inverse = []
        scale = jnp.ones((8, HALF), jnp.float32)
        for k in range(8):
            inverse.append(1.0 / d[k, k])
            scale = jnp.where(rows == k, d[k, k], scale)
            raw = [d.get((s, k)) for s in range(8)]
            for s in range(k + 1, 8):
                ratio = raw[s] * inverse[k]
                for t in range(k + 1, s + 1):
                    d[s, t] = d[s, t] - ratio * raw[t]
                a_rows[s] = a_rows[s] - ratio * a_rows[k]
                x_rows[s] = x_rows[s] - ratio * x_rows[k]
                d[s, k] = ratio
        final = x_rows[0]
        for s in range(1, 8):
            final = jnp.where(rows == s, x_rows[s], final)
        root = lax.rsqrt(scale)
        root = root * (1.5 - 0.5 * scale * root * root)
        done.append(final * root)
        if g == GROUPS - 1:
            break
        for t in range(7, -1, -1):
            a_rows[t] = a_rows[t] * inverse[t]
            x_rows[t] = x_rows[t] * inverse[t]
            for s in range(t + 1, 8):
                a_rows[t] = a_rows[t] - d[s, t] * a_rows[s]
                x_rows[t] = x_rows[t] - d[s, t] * x_rows[s]
        for h in range(g + 1, GROUPS):
            columns = [lane(a[h], 8 * g + t) for t in range(8)]
            for t in range(8):
                a[h] = a[h] - columns[t] * a_rows[t]
                x[h] = x[h] - columns[t] * x_rows[t]
    return jnp.concatenate(done, axis=0)


def first_kernel(col_ref, gather_ref, jitter_ref, w_ref, gram_ref):
    for k in range(16):
        gram_ref[16 * k : 16 * k + 16, :] = gather_ref[col_ref[0] ^ k]
    gram = gram_ref[...]
    eye = lax.broadcasted_iota(jnp.int32, (RANK, RANK), 0) == lax.broadcasted_iota(
        jnp.int32, (RANK, RANK), 1
    )
    jitter = 1e-06 * jnp.sum(jnp.where(eye, gram, 0.0)) / RANK
    jitter_ref[...] = jnp.full((8, HALF), jitter, jnp.float32)
    rows = lax.broadcasted_iota(jnp.int32, (HALF, HALF), 0)
    lanes = lax.broadcasted_iota(jnp.int32, (HALF, HALF), 1)
    w_ref[...] = inverse_factor(gram[:HALF, :HALF] + jnp.where(rows == lanes, jitter, 0.0))


def second_kernel(gram_ref, jitter_ref, first_ref, left_ref, w_ref, ortho_ref):
    first = first_ref[...]
    rows = lax.broadcasted_iota(jnp.int32, (HALF, HALF), 0)
    lanes = lax.broadcasted_iota(jnp.int32, (HALF, HALF), 1)
    low = dot_nt(gram_ref[HALF:, :HALF], first)
    rest = gram_ref[HALF:, HALF:] + jnp.where(rows == lanes, jitter_ref[0:1, :], 0.0)
    second = inverse_factor(rest - dot_nt(low, low))
    w_ref[:HALF, :HALF] = first
    w_ref[:HALF, HALF:] = jnp.zeros((HALF, HALF), jnp.float32)
    w_ref[HALF:, :HALF] = -dot_nn(second, dot_nn(low, first))
    w_ref[HALF:, HALF:] = second
    ortho_ref[...] = dot_nt(left_ref[...], w_ref[...])


def first_part(col, gather):
    vmem = pl.BlockSpec(memory_space=pltpu.VMEM)
    return pl.pallas_call(
        first_kernel,
        in_specs=[pl.BlockSpec(memory_space=pltpu.SMEM), vmem],
        out_specs=(vmem, vmem, vmem),
        out_shape=(
            jax.ShapeDtypeStruct((8, HALF), jnp.float32),
            jax.ShapeDtypeStruct((HALF, HALF), jnp.float32),
            jax.ShapeDtypeStruct((RANK, RANK), jnp.float32),
        ),
        cost_estimate=pl.CostEstimate(flops=6000000, bytes_accessed=20000000, transcendentals=0),
        name="first_factor",
    )(col, gather)


def second_part(jitter, first, gram, left):
    return pl.pallas_call(
        second_kernel,
        out_shape=(
            jax.ShapeDtypeStruct((RANK, RANK), jnp.float32),
            jax.ShapeDtypeStruct(left.shape, jnp.float32),
        ),
        cost_estimate=pl.CostEstimate(flops=6000000, bytes_accessed=24000000, transcendentals=0),
        name="second_factor",
    )(gram, jitter, first, left)


def halves(value):
    high = value.astype(jnp.bfloat16)
    return high, (value - high.astype(jnp.float32)).astype(jnp.bfloat16)


def product(a, b):
    return jnp.dot(a, b, preferred_element_type=jnp.float32)


def params(mib=40):
    return pltpu.CompilerParams(vmem_limit_bytes=mib * 1024 * 1024)


def left_kernel(m_ref, g_ref, r_ref, out_ref, high_ref, low_ref):
    @pl.when(pl.program_id(0) == 0)
    def _():
        high_ref[...], low_ref[...] = halves(r_ref[...])

    both = jnp.concatenate([m_ref[...], g_ref[...]], axis=0)
    total = product(both, high_ref[...]) + product(both, low_ref[...])
    count = m_ref.shape[0]
    out_ref[...] = total[:count] + total[count:]


def left_part(momentum, gradient, right_factor):
    rows, columns = momentum.shape
    step = rows // 2
    block = pl.BlockSpec((step, columns), lambda i: (i, 0))
    return pl.pallas_call(
        left_kernel,
        grid=(2,),
        in_specs=[block, block, pl.BlockSpec((columns, RANK), lambda i: (0, 0))],
        out_specs=pl.BlockSpec((step, RANK), lambda i: (i, 0)),
        out_shape=jax.ShapeDtypeStruct((rows, RANK), jnp.float32),
        scratch_shapes=[pltpu.VMEM((columns, RANK), jnp.bfloat16)] * 2,
        compiler_params=params(60),
        cost_estimate=pl.CostEstimate(flops=1744830464, bytes_accessed=5600000, transcendentals=0),
        name="left_part",
    )(momentum, gradient, right_factor)


def cross_kernel(core_ref, left_ref, m_ref, g_ref, mine_ref, other_ref, lhs_ref):
    turned = left_ref[...].T
    top, bottom = turned[:HALF], turned[HALF:]
    first = core_ref[0] == 0
    own = jnp.where(first, top, bottom)
    far = jnp.where(first, bottom, top)
    lhs_ref[0:HALF], lhs_ref[2 * HALF : 3 * HALF] = halves(own)
    lhs_ref[HALF : 2 * HALF], lhs_ref[3 * HALF :] = halves(far)
    columns = m_ref.shape[1]
    for start in range(0, columns, 256):
        stop = min(start + 256, columns)
        total = product(lhs_ref[...], m_ref[:, start:stop]) + product(lhs_ref[...], g_ref[:, start:stop])
        total = total[: 2 * HALF] + total[2 * HALF :]
        mine_ref[:, start:stop] = total[:HALF]
        other_ref[:, start:stop] = total[HALF:]


def cross_part(core, left, momentum, gradient):
    rows, columns = momentum.shape
    vmem = pl.BlockSpec(memory_space=pltpu.VMEM)
    return pl.pallas_call(
        cross_kernel,
        in_specs=[pl.BlockSpec(memory_space=pltpu.SMEM), vmem, vmem, vmem],
        out_specs=(vmem, vmem),
        out_shape=(jax.ShapeDtypeStruct((HALF, columns), jnp.float32),) * 2,
        scratch_shapes=[pltpu.VMEM((2 * RANK, rows), jnp.bfloat16)],
        compiler_params=params(),
        cost_estimate=pl.CostEstimate(flops=1744830464, bytes_accessed=5600000, transcendentals=0),
        name="cross_part",
    )(core, left, momentum, gradient)


def right_kernel(core_ref, w_ref, mine_ref, other_ref, right_ref, squares_ref):
    w = w_ref[...]
    whole = jnp.zeros((RANK, HALF), jnp.float32)
    first = core_ref[0] == 0
    columns = mine_ref.shape[1]
    for start in range(0, columns, 256):
        stop = min(start + 256, columns)
        mine, other = mine_ref[:, start:stop], other_ref[:, start:stop]
        y = jnp.concatenate([jnp.where(first, mine, other), jnp.where(first, other, mine)], axis=0)
        right = dot_nn(w, y)
        right_ref[:, start:stop] = right
        square = right * right
        for k in range(0, stop - start, HALF):
            whole = whole + square[:, k : k + HALF]
    squares_ref[...] = jnp.sum(whole.T, axis=0, keepdims=True)


def right_part(core, w, mine, other):
    columns = mine.shape[1]
    vmem = pl.BlockSpec(memory_space=pltpu.VMEM)
    return pl.pallas_call(
        right_kernel,
        in_specs=[pl.BlockSpec(memory_space=pltpu.SMEM), vmem, vmem, vmem],
        out_specs=(vmem, vmem),
        out_shape=(
            jax.ShapeDtypeStruct((RANK, columns), jnp.float32),
            jax.ShapeDtypeStruct((1, RANK), jnp.float32),
        ),
        compiler_params=params(60),
        cost_estimate=pl.CostEstimate(flops=1300000000, bytes_accessed=3400000, transcendentals=0),
        name="right_part",
    )(core, w, mine, other)


def low_rank(ortho, high_ref, low_ref, start, stop):
    count = ortho.shape[0] // 2
    total = product(ortho, high_ref[:, start:stop])
    return total[:count] + total[count:] + product(ortho[:count], low_ref[:, start:stop])


def momentum_kernel(m_ref, g_ref, ortho_ref, right_ref, out_ref, turned_ref, high_ref, low_ref):
    columns = right_ref.shape[1]

    @pl.when(pl.program_id(0) == 0)
    def _():
        for start in range(0, columns, HALF):
            block = right_ref[:, start : start + HALF]
            high_ref[:, start : start + HALF], low_ref[:, start : start + HALF] = halves(block)
            turned_ref[start : start + HALF, :] = block.T

    ortho = jnp.concatenate(halves(ortho_ref[...]), axis=0)
    for start in range(0, columns, 256):
        stop = min(start + 256, columns)
        buffer = m_ref[:, start:stop].astype(jnp.float32) + g_ref[:, start:stop].astype(jnp.float32)
        update = low_rank(ortho, high_ref, low_ref, start, stop)
        out_ref[:, start:stop] = (buffer - (1.0 - decay) * update).astype(jnp.bfloat16)


def momentum_part(momentum, gradient, ortho, right):
    rows, columns = momentum.shape
    step = rows // 4
    block = pl.BlockSpec((step, columns), lambda i: (i, 0))
    wide = pl.BlockSpec((RANK, columns), lambda i: (0, 0))
    return pl.pallas_call(
        momentum_kernel,
        grid=(4,),
        in_specs=[block, block, pl.BlockSpec((step, RANK), lambda i: (i, 0)), wide],
        out_specs=(block, pl.BlockSpec((columns, RANK), lambda i: (0, 0)), wide, wide),
        out_shape=(
            jax.ShapeDtypeStruct((rows, columns), jnp.bfloat16),
            jax.ShapeDtypeStruct((columns, RANK), jnp.float32),
            jax.ShapeDtypeStruct((RANK, columns), jnp.bfloat16),
            jax.ShapeDtypeStruct((RANK, columns), jnp.bfloat16),
        ),
        compiler_params=params(60),
        cost_estimate=pl.CostEstimate(flops=1308622848, bytes_accessed=7500000, transcendentals=0),
        name="momentum_part",
    )(momentum, gradient, ortho, right)


def weight_kernel(squares_ref, weight_ref, ortho_ref, turned_ref, high_ref, low_ref, out_ref, factor_ref):
    squares = jnp.sum(squares_ref[...], axis=0, keepdims=True)
    scale = 1.0 / jnp.sqrt(squares / COLS + 1e-06)
    rate = step_size * (ROWS / RANK) ** 0.5
    ortho = jnp.concatenate(halves(ortho_ref[...] * (scale * rate)), axis=0)
    columns = high_ref.shape[1]
    for start in range(0, columns, 256):
        stop = min(start + 256, columns)
        update = low_rank(ortho, high_ref, low_ref, start, stop)
        out_ref[:, start:stop] = (weight_ref[:, start:stop].astype(jnp.float32) - update).astype(
            jnp.bfloat16
        )
    factor_ref[...] = turned_ref[...] * scale


def weight_part(squares, weight, ortho, turned, high, low):
    rows, columns = weight.shape
    step = rows // 4
    block = pl.BlockSpec((step, columns), lambda i: (i, 0))
    wide = pl.BlockSpec((RANK, columns), lambda i: (0, 0))
    factor = pl.BlockSpec((columns // 4, RANK), lambda i: (i, 0))
    return pl.pallas_call(
        weight_kernel,
        grid=(4,),
        in_specs=[
            pl.BlockSpec((16, RANK), lambda i: (0, 0)),
            block,
            pl.BlockSpec((step, RANK), lambda i: (i, 0)),
            factor,
            wide,
            wide,
        ],
        out_specs=(block, factor),
        out_shape=(
            jax.ShapeDtypeStruct((rows, columns), jnp.bfloat16),
            jax.ShapeDtypeStruct((columns, RANK), jnp.float32),
        ),
        compiler_params=params(60),
        cost_estimate=pl.CostEstimate(flops=1308622848, bytes_accessed=7500000, transcendentals=0),
        name="weight_part",
    )(squares, weight, ortho, turned, high, low)


def exchange(pieces, axis, groups=None):
    return lax.all_to_all(pieces, axis, 0, 0, axis_index_groups=groups)


def spread(piece, axis, count, groups=None):
    return exchange(jnp.broadcast_to(piece[None], (count,) + piece.shape), axis, groups)


def gather_col(piece):
    out = piece[None]
    for bit in (1, 2, 4, 8):
        pairs = [(i, i ^ bit) for i in range(16)]
        out = jnp.concatenate([out, lax.ppermute(out, "col", pairs)], axis=0)
    return out


def local(gradient, momentum, weight, right_factor):
    core = (lax.axis_index("row") % 2).reshape(1)
    col = lax.axis_index("col")
    partial = left_part(momentum, gradient, right_factor)
    piece = jnp.sum(exchange(partial.reshape(16, 32, RANK), "col"), axis=0)
    left = spread(piece, "col", 16).reshape(512, RANK)
    gram = dot_tn(lax.dynamic_slice(left, (0, col * 16), (512, 16)), left)
    gram = jnp.sum(spread(gram, "row", 16), axis=0)
    mine, other = cross_part(core, left, momentum, gradient)
    gram, other = lax.optimization_barrier((gram, other))
    mine = mine + lax.ppermute(other, "row", CORE_SWAP)
    mine = jnp.sum(exchange(mine.reshape(8, 16, 1664), "row", Z_GROUPS), axis=0)
    jitter, first, gram = first_part(col.reshape(1), gather_col(gram))
    mine, first = lax.optimization_barrier((mine, first))
    inverse, ortho = second_part(jitter, first, gram, left)
    mine = spread(mine, "row", 8, Z_GROUPS).reshape(HALF, 1664)
    mine, inverse = lax.optimization_barrier((mine, inverse))
    other = lax.ppermute(mine, "row", CORE_SWAP)
    right, squares = right_part(core, inverse, mine, other)
    squares = spread(squares, "col", 16).reshape(16, RANK)
    new_momentum, turned, high, low = momentum_part(momentum, gradient, ortho, right)
    new_weight, new_factor = weight_part(squares, weight, ortho, turned, high, low)
    return (new_weight, new_momentum, new_factor)


def solution(mesh):
    in_specs = (P("row", "col"), P("row", "col"), P("row", "col"), P("col", None))
    out_specs = (P("row", "col"), P("row", "col"), P("col", None))
    return jax.shard_map(local, mesh=mesh, in_specs=in_specs, out_specs=out_specs, check_vma=False)
```

time: 204 us -> 154 us (0.75)
  matrix products: 26.5 us -> 0.65 us
  blocking collectives: 0 us -> 18.1 us
  waiting for transfers between devices: 63.1 us -> 48.2 us
  starting transfers between devices: 47.9 us -> 34.2 us
  local copies, waits for them, and re-layouts: 17.9 us -> 8.4 us
  other arithmetic: 8.09 us -> 1.11 us
  Pallas kernels: 38.5 us -> 41.8 us
    all_to_all x5, waiting for transfers between devices: 50.3 us -> 29 us  [exchange(): return lax.all_to_all(pieces, axis, 0, 0, axis_index_groups=groups)]
    dot_general x5 -> x0, matrix products: 19.9 us -> none  [the longest x4 14 us: dot_nt(): lax.dot_general(a, b, (((1,), (1,)), ((), ())), precision=precision, pref...]
    all_to_all x0 -> x1, blocking collectives: none -> 18.1 us  [exchange(): return lax.all_to_all(pieces, axis, 0, 0, axis_index_groups=groups)]
    ppermute x9 -> x5, starting transfers between devices: 16.7 us -> 5.52 us  [the longest x1 4.09 us: local(): other = lax.ppermute(mine, 'row', CORE_SWAP)]
    dot_general x2 -> x0, local copies, waits for them, and re-layouts: 6.77 us -> none  [dot_tn(): lax.dot_general(a, b, (((0,), (0,)), ((), ())), precision=precision, pref...]
    ppermute x9 -> x5, waiting for transfers between devices: 10.3 us -> 16.6 us  [the longest x4 14.6 us: gather_col(): out = jnp.concatenate([out, lax.ppermute(out, 'col', pairs)], axis=0)]
    dot_general x2 -> x1, matrix products: 6.59 us -> 0.65 us  [dot_tn(): lax.dot_general(a, b, (((0,), (0,)), ((), ())), precision=precision, pref...]
    dot_general x1 -> x0, other arithmetic: 3.5 us -> none  [dot_tn(): lax.dot_general(a, b, (((0,), (0,)), ((), ())), precision=precision, pref...]
  transfers between devices with their start and end apart: 15 -> 11, of which waited for: 10 -> 10; matrix products, arithmetic and copies ran while one was open for 10% -> 0% of each run, Pallas kernels for 19% -> 17%
where the time goes in v2:
time: 154 us; the launch traced here: 153 us
  waiting for transfers between devices  48.2 us (31%)
  Pallas kernels  41.8 us (27%)
  starting transfers between devices  34.2 us (22%)
  blocking collectives  18.1 us (12%)
  local copies, waits for them, and re-layouts  8.4 us (5%)
    all_to_all x5, waiting for transfers between devices, exchange(): return lax.all_to_all(pieces, axis, 0, 0, axis_index_groups=groups)  29 us
    all_to_all x5, starting transfers between devices, exchange(): return lax.all_to_all(pieces, axis, 0, 0, axis_index_groups=groups)  28.6 us
    all_to_all x1, blocking collectives, exchange(): return lax.all_to_all(pieces, axis, 0, 0, axis_index_groups=groups)  18.1 us
    ppermute x4, waiting for transfers between devices, gather_col(): out = jnp.concatenate([out, lax.ppermute(out, 'col', pairs)], axis=0)  14.6 us
    pallas_call x1, Pallas kernels, second_part(): pl.pallas_call(second_kernel, out_shape=(jax.ShapeDtypeStruct((RANK, RANK...  9.71 us
    pallas_call x1, Pallas kernels, first_part(): pl.pallas_call(first_kernel, in_specs=[pl.BlockSpec(memory_space=pltpu.SM...  7.68 us
    pallas_call x1, Pallas kernels, momentum_part(): pl.pallas_call(momentum_kernel, grid=(4,), in_specs=[block, block, pl.Blo...  6.86 us
    pallas_call x1, Pallas kernels, weight_part(): pl.pallas_call(weight_kernel, grid=(4,), in_specs=[pl.BlockSpec((16, RANK...  5.93 us
  transfers between devices with their start and end apart: 11, of which 10 were waited for; matrix products, arithmetic and copies ran while one was open for 0% of the time, Pallas kernels for 17%

profile of v2, /device:TPU:1, one launch (start us, length us, event | category | flops | bytes accessed | tf_op | source)
XLA Modules:
  0.0 153.2 jit_solution(14082778378522043253)
XLA Ops:
  0.6 5.2 %left_part.1 = f32[512,256]{1,0:T(8,128)} custom-call(bf16[512,1664]{1,0:T(8,128)(2,1)} %m_ref.5, bf16[512,1664]{1,0:T(8,128)(2,1)} %g_ref.5, f32[1664,256]{1,0:T(8,128)} %r_ref.1), custom_call_target="tpu_custom_call" | custom-call | flops 1744830464 | bytes 5600000 | tf_op jit(solution)/shard_map/left_part/pallas_call | solution.py:178
  5.8 18.1 %all_to_all.30 = f32[16,32,256]{2,1,0:T(8,128)S(1)} all-to-all(f32[16,32,256]{2,1,0:T(8,128)} %bitcast.18), channel_id=1, replica_groups=mesh['row'=16,'col'=16] {'col'}, dimensions={0} | all-to-all | bytes 1048576 | tf_op jit(solution)/shard_map/all_to_all | solution.py:347
  23.9 0.8 broadcast_in_dim.12
  24.8 3.6 %all-to-all-start.1 = ((f32[16,32,256]{2,1,0:T(8,128)}), f32[16,32,256]{2,1,0:T(8,128)S(1)}, u32[]{:S(2)}, u32[]{:S(2)}) async-start(f32[16,32,256]{2,1,0:T(8,128)} %broadcast_in_dim.12), calls=%async_computation.1 | async-start | bytes 1048576 | tf_op jit(solution)/shard_map/all_to_all | solution.py:347
  28.4 9.7 %all-to-all-done.1 = f32[16,32,256]{2,1,0:T(8,128)S(1)} async-done(((f32[16,32,256]{2,1,0:T(8,128)}), f32[16,32,256]{2,1,0:T(8,128)S(1)}, u32[]{:S(2)}, u32[]{:S(2)}) %all-to-all-start.1) | async-done | bytes 524320 | tf_op jit(solution)/shard_map/all_to_all | solution.py:347
  38.7 0.7 broadcast_in_dim.13
  39.4 11.3 %all-to-all-start.2 = ((f32[16,16,256]{2,1,0:T(8,128)}), f32[16,16,256]{2,1,0:T(8,128)S(1)}, u32[]{:S(2)}, u32[]{:S(2)}) async-start(f32[16,16,256]{2,1,0:T(8,128)} %broadcast_in_dim.13), calls=%async_computation.2 | async-start | bytes 524288 | tf_op jit(solution)/shard_map/all_to_all | solution.py:347
  50.7 1.4 copy-done.2
  52.2 2.1 %cross_part.1 = (f32[128,1664]{1,0:T(8,128)S(1)}, f32[128,1664]{1,0:T(8,128)S(1)}) custom-call(s32[1]{0:T(128)} %bitcast.core_ref, f32[512,256]{1,0:T(8,128)S(1)} %bitcast.14, bf16[512,1664]{1,0:T(8,128)(2,1)S(1)} %copy-done.1, bf16[512,1664]{1,0:T(8,128)(2,1)S(1)} %copy-done.2), custom_call_target="tpu_custom_call" | custom-call | flops 1744830464 | bytes 5600000 | tf_op jit(solution)/shard_map/cross_part/pallas_call | solution.py:211
  54.3 0.9 copy-done.3
  55.2 7.2 %all-to-all-done.2 = f32[16,16,256]{2,1,0:T(8,128)S(1)} async-done(((f32[16,16,256]{2,1,0:T(8,128)}), f32[16,16,256]{2,1,0:T(8,128)S(1)}, u32[]{:S(2)}, u32[]{:S(2)}) %all-to-all-start.2) | async-done | bytes 262176 | tf_op jit(solution)/shard_map/all_to_all | solution.py:347
  62.6 2.6 %collective-permute-done = f32[128,1664]{1,0:T(8,128)S(1)} collective-permute-done((f32[128,1664]{1,0:T(8,128)}, f32[128,1664]{1,0:T(8,128)S(1)}, u32[]{:S(2)}, u32[]{:S(2)}) %collective-permute-start) | collective-permute-done | bytes 852000 | tf_op jit(solution)/shard_map/ppermute | solution.py:372
  65.1 1.0 add.12
  66.1 3.6 %all-to-all-start.3 = ((f32[8,16,1664]{2,1,0:T(8,128)}), f32[8,16,1664]{2,1,0:T(8,128)S(1)}, u32[]{:S(2)}, u32[]{:S(2)}) async-start(f32[8,16,1664]{2,1,0:T(8,128)} %bitcast.3), calls=%async_computation.3 | async-start | bytes 1703936 | tf_op jit(solution)/shard_map/all_to_all | solution.py:347
  70.1 2.3 %collective-permute-done.1 = f32[1,16,256]{2,1,0:T(8,128)S(1)} collective-permute-done((f32[1,16,256]{2,1,0:T(8,128)S(1)}, f32[1,16,256]{2,1,0:T(8,128)S(1)}, u32[]{:S(2)}, u32[]{:S(2)}) %collective-permute-start.1) | collective-permute-done | bytes 16416 | tf_op jit(solution)/shard_map/ppermute | solution.py:358
  72.8 4.1 %collective-permute-done.2 = f32[2,16,256]{2,1,0:T(8,128)S(1)} collective-permute-done((f32[2,16,256]{2,1,0:T(8,128)S(1)}, f32[2,16,256]{2,1,0:T(8,128)S(1)}, u32[]{:S(2)}, u32[]{:S(2)}) %collective-permute-start.2) | collective-permute-done | bytes 32800 | tf_op jit(solution)/shard_map/ppermute | solution.py:358
  76.9 3.4 %collective-permute-done.3 = f32[4,16,256]{2,1,0:T(8,128)S(1)} collective-permute-done((f32[4,16,256]{2,1,0:T(8,128)S(1)}, f32[4,16,256]{2,1,0:T(8,128)S(1)}, u32[]{:S(2)}, u32[]{:S(2)}) %collective-permute-start.3) | collective-permute-done | bytes 65568 | tf_op jit(solution)/shard_map/ppermute | solution.py:358
  81.0 4.8 %collective-permute-done.4 = f32[8,16,256]{2,1,0:T(8,128)S(1)} collective-permute-done((f32[8,16,256]{2,1,0:T(8,128)S(1)}, f32[8,16,256]{2,1,0:T(8,128)S(1)}, u32[]{:S(2)}, u32[]{:S(2)}) %collective-permute-start.4) | collective-permute-done | bytes 131104 | tf_op jit(solution)/shard_map/ppermute | solution.py:358
  85.8 0.7 copy-done.5
  86.5 7.7 %first_factor.1 = (f32[8,128]{1,0:T(8,128)}, f32[128,128]{1,0:T(8,128)}, f32[256,256]{1,0:T(8,128)}) custom-call(s32[1]{0:T(128)} %bitcast.4.col_ref, f32[16,16,256]{2,1,0:T(8,128)} %copy-done.5), custom_call_target="tpu_custom_call" | custom-call | flops 6000000 | bytes 20000000 | tf_op jit(solution)/shard_map/first_factor/pallas_call | solution.py:124
  94.7 1.0 broadcast_in_dim.15
  95.6 6.6 %all-to-all-start.4 = ((f32[8,16,1664]{2,1,0:T(8,128)}), f32[8,16,1664]{2,1,0:T(8,128)S(1)}, u32[]{:S(2)}, u32[]{:S(2)}) async-start(f32[8,16,1664]{2,1,0:T(8,128)} %broadcast_in_dim.15), calls=%async_computation.4 | async-start | bytes 1703936 | tf_op jit(solution)/shard_map/all_to_all | solution.py:347
  102.2 9.7 %second_factor.1 = (f32[256,256]{1,0:T(8,128)}, f32[512,256]{1,0:T(8,128)}) custom-call(f32[256,256]{1,0:T(8,128)} %get-tuple-element.30.gram_ref, f32[8,128]{1,0:T(8,128)} %get-tuple-element.31.jitter_ref, f32[128,128]{1,0:T(8,128)} %get-tuple-element.32.first_ref, f32[512,256]{1,0:T(8,128)} %bitcast.15), custom_call_target="tpu_custom_call" | custom-call | flops 6000000 | bytes 24000000 | tf_op jit(solution)/shard_map/second_factor/pallas_call | solution.py:139
  111.9 11.7 %all-to-all-done.4 = f32[8,16,1664]{2,1,0:T(8,128)S(1)} async-done(((f32[8,16,1664]{2,1,0:T(8,128)}), f32[8,16,1664]{2,1,0:T(8,128)S(1)}, u32[]{:S(2)}, u32[]{:S(2)}) %all-to-all-start.4) | async-done | bytes 852000 | tf_op jit(solution)/shard_map/all_to_all | solution.py:347
  123.7 4.1 %collective-permute-start.5 = (f32[128,1664]{1,0:T(8,128)S(1)}, f32[128,1664]{1,0:T(8,128)S(1)}, u32[]{:S(2)}, u32[]{:S(2)}) collective-permute-start(f32[128,1664]{1,0:T(8,128)S(1)} %bitcast.16), channel_id=1, source_target_pairs={{0,16},{16,0},{32,48},{48,32},{64,80},{80,64},{96,112},{112,96},{1... | collective-permute-start | bytes 2555912 | tf_op jit(solution)/shard_map/ppermute | solution.py:379
  127.8 2.0 %collective-permute-done.5.other_ref = f32[128,1664]{1,0:T(8,128)S(1)} collective-permute-done((f32[128,1664]{1,0:T(8,128)S(1)}, f32[128,1664]{1,0:T(8,128)S(1)}, u32[]{:S(2)}, u32[]{:S(2)}) %collective-permute-start.5) | collective-permute-done | bytes 852000 | tf_op jit(solution)/shard_map/ppermute | solution.py:379
  129.8 0.9 copy-done.6
  130.7 4.4 %right_part.1 = (f32[256,1664]{1,0:T(8,128)}, f32[1,256]{1,0:T(1,128)}) custom-call(s32[1]{0:T(128)} %bitcast.core_ref, f32[256,256]{1,0:T(8,128)} %get-tuple-element.34.w_ref, f32[128,1664]{1,0:T(8,128)} %bitcast.17, f32[128,1664]{1,0:T(8,128)} %copy-done.6), custom_call_target="tpu_custom_call" | custom-call | flops 1300000000 | bytes 3400000 | tf_op jit(solution)/shard_map/right_part/pallas_call | solution.py:243
  135.0 1.3 broadcast_in_dim.34
  136.3 3.5 %all-to-all-start.5 = ((f32[16,1,256]{2,1,0:T(1,128)}), f32[16,1,256]{2,1,0:T(1,128)S(1)}, u32[]{:S(2)}, u32[]{:S(2)}) async-start(f32[16,1,256]{2,1,0:T(1,128)} %broadcast_in_dim.34), calls=%async_computation.5 | async-start | bytes 32768 | tf_op jit(solution)/shard_map/all_to_all | solution.py:347
  139.8 6.9 %momentum_part.1 = (bf16[512,1664]{1,0:T(8,128)(2,1)}, f32[1664,256]{1,0:T(8,128)}, bf16[256,1664]{1,0:T(8,128)(2,1)}, bf16[256,1664]{1,0:T(8,128)(2,1)}) custom-call(bf16[512,1664]{1,0:T(8,128)(2,1)} %m_ref.5, bf16[512,1664]{1,0:T(8,128)(2,1)} %g_ref.5, f32[512,256]{1,0:T(8,128)} %get-tuple-element.37.ortho_ref, f32[256,1664]{1,0:T(8,128)} %get-tuple-element.38.right_ref), custom_call_target="tpu_custom_call" | custom-call | flops 1308622848 | bytes 7500000 | tf_op jit(solution)/shard_map/momentum_part/pallas_call | solution.py:286
  147.3 5.9 %weight_part.1 = (bf16[512,1664]{1,0:T(8,128)(2,1)}, f32[1664,256]{1,0:T(8,128)}) custom-call(f32[16,256]{1,0:T(8,128)} %bitcast.23, bf16[512,1664]{1,0:T(8,128)(2,1)} %weight_ref.1, f32[512,256]{1,0:T(8,128)} %get-tuple-element.37.ortho_ref, f32[1664,256]{1,0:T(8,128)} %get-tuple-element.39.turned_ref, bf16[256,1664]{1,0:T(8,128)(2,1)} %get-tuple-element.40.high_ref, ...), custom_call_target="tpu_custom_call" | custom-call | flops 1308622848 | bytes 7500000 | tf_op jit(solution)/shard_map/weight_part/pallas_call | solution.py:324
  (30 shorter events, 3.4 us)
Async XLA Ops:
  23.9 26.8 %copy-start.1 = (bf16[512,1664]{1,0:T(8,128)(2,1)S(1)}, bf16[512,1664]{1,0:T(8,128)(2,1)}, u32[]{:S(2)}) copy-start(bf16[512,1664]{1,0:T(8,128)(2,1)} %m_ref.5) | copy-start | bytes 5111812
  24.8 13.2 %all-to-all-start.1 = ((f32[16,32,256]{2,1,0:T(8,128)}), f32[16,32,256]{2,1,0:T(8,128)S(1)}, u32[]{:S(2)}, u32[]{:S(2)}) async-start(f32[16,32,256]{2,1,0:T(8,128)} %broadcast_in_dim.12), calls=%async_computation.1 | async-start | bytes 1048576 | tf_op jit(solution)/shard_map/all_to_all | solution.py:347
  38.0 16.3 %copy-start = (f32[16,32,256]{2,1,0:T(8,128)}, f32[16,32,256]{2,1,0:T(8,128)S(1)}, u32[]{:S(2)}) copy-start(f32[16,32,256]{2,1,0:T(8,128)S(1)} %all-to-all-done.1) | copy-start | bytes 1572868
  39.4 23.0 %all-to-all-start.2 = ((f32[16,16,256]{2,1,0:T(8,128)}), f32[16,16,256]{2,1,0:T(8,128)S(1)}, u32[]{:S(2)}, u32[]{:S(2)}) async-start(f32[16,16,256]{2,1,0:T(8,128)} %broadcast_in_dim.13), calls=%async_computation.2 | async-start | bytes 524288 | tf_op jit(solution)/shard_map/all_to_all | solution.py:347
  50.7 1.5 copy-start.2
  54.3 0.9 copy-start.3
  62.5 2.7 %collective-permute-start = (f32[128,1664]{1,0:T(8,128)}, f32[128,1664]{1,0:T(8,128)S(1)}, u32[]{:S(2)}, u32[]{:S(2)}) collective-permute-start(f32[128,1664]{1,0:T(8,128)} %copy-done.3), channel_id=1, source_target_pairs={{0,16},{16,0},{32,48},{48,32},{64,80},{80,64},{96,112},{112,96},{1... | collective-permute-start | bytes 2555912 | tf_op jit(solution)/shard_map/ppermute | solution.py:372
  66.1 28.5 %all-to-all-start.3 = ((f32[8,16,1664]{2,1,0:T(8,128)}), f32[8,16,1664]{2,1,0:T(8,128)S(1)}, u32[]{:S(2)}, u32[]{:S(2)}) async-start(f32[8,16,1664]{2,1,0:T(8,128)} %bitcast.3), calls=%async_computation.3 | async-start | bytes 1703936 | tf_op jit(solution)/shard_map/all_to_all | solution.py:347
  69.7 2.7 %collective-permute-start.1 = (f32[1,16,256]{2,1,0:T(8,128)S(1)}, f32[1,16,256]{2,1,0:T(8,128)S(1)}, u32[]{:S(2)}, u32[]{:S(2)}) collective-permute-start(f32[1,16,256]{2,1,0:T(8,128)S(1)} %bitcast.19), channel_id=1, source_target_pairs={{0,1},{1,0},{2,3},{3,2},{4,5},{5,4},{6,7},{7,6},{8,9},{9,8},{10,11... | collective-permute-start | bytes 49160 | tf_op jit(solution)/shard_map/ppermute | solution.py:358
  72.4 4.6 %collective-permute-start.2 = (f32[2,16,256]{2,1,0:T(8,128)S(1)}, f32[2,16,256]{2,1,0:T(8,128)S(1)}, u32[]{:S(2)}, u32[]{:S(2)}) collective-permute-start(f32[2,16,256]{2,1,0:T(8,128)S(1)} %pad_maximum_fusion.2), channel_id=1, source_target_pairs={{0,2},{1,3},{2,0},{3,1},{4,6},{5,7},{6,4},{7,5},{8,10},{9,11},{10,... | collective-permute-start | bytes 98312 | tf_op jit(solution)/shard_map/ppermute | solution.py:358
  76.9 3.4 %collective-permute-start.3 = (f32[4,16,256]{2,1,0:T(8,128)S(1)}, f32[4,16,256]{2,1,0:T(8,128)S(1)}, u32[]{:S(2)}, u32[]{:S(2)}) collective-permute-start(f32[4,16,256]{2,1,0:T(8,128)S(1)} %pad_maximum_fusion.1), channel_id=1, source_target_pairs={{0,4},{1,5},{2,6},{3,7},{4,0},{5,1},{6,2},{7,3},{8,12},{9,13},{10,... | collective-permute-start | bytes 196616 | tf_op jit(solution)/shard_map/ppermute | solution.py:358
  80.4 5.4 %collective-permute-start.4 = (f32[8,16,256]{2,1,0:T(8,128)S(1)}, f32[8,16,256]{2,1,0:T(8,128)S(1)}, u32[]{:S(2)}, u32[]{:S(2)}) collective-permute-start(f32[8,16,256]{2,1,0:T(8,128)S(1)} %pad_maximum_fusion), channel_id=1, source_target_pairs={{0,8},{1,9},{2,10},{3,11},{4,12},{5,13},{6,14},{7,15},{8,0},{9,1},... | collective-permute-start | bytes 393224 | tf_op jit(solution)/shard_map/ppermute | solution.py:358
  85.8 0.7 copy-start.5
  95.6 28.0 %all-to-all-start.4 = ((f32[8,16,1664]{2,1,0:T(8,128)}), f32[8,16,1664]{2,1,0:T(8,128)S(1)}, u32[]{:S(2)}, u32[]{:S(2)}) async-start(f32[8,16,1664]{2,1,0:T(8,128)} %broadcast_in_dim.15), calls=%async_computation.4 | async-start | bytes 1703936 | tf_op jit(solution)/shard_map/all_to_all | solution.py:347
  123.7 6.1 %copy-start.4 = (f32[8,16,1664]{2,1,0:T(8,128)}, f32[8,16,1664]{2,1,0:T(8,128)S(1)}, u32[]{:S(2)}) copy-start(f32[8,16,1664]{2,1,0:T(8,128)S(1)} %all-to-all-done.4) | copy-start | bytes 2555908
  123.7 6.1 %collective-permute-start.5 = (f32[128,1664]{1,0:T(8,128)S(1)}, f32[128,1664]{1,0:T(8,128)S(1)}, u32[]{:S(2)}, u32[]{:S(2)}) collective-permute-start(f32[128,1664]{1,0:T(8,128)S(1)} %bitcast.16), channel_id=1, source_target_pairs={{0,16},{16,0},{32,48},{48,32},{64,80},{80,64},{96,112},{112,96},{1... | collective-permute-start | bytes 2555912 | tf_op jit(solution)/shard_map/ppermute | solution.py:379
  129.8 0.9 copy-start.6
  136.3 10.4 %all-to-all-start.5 = ((f32[16,1,256]{2,1,0:T(1,128)}), f32[16,1,256]{2,1,0:T(1,128)S(1)}, u32[]{:S(2)}, u32[]{:S(2)}) async-start(f32[16,1,256]{2,1,0:T(1,128)} %broadcast_in_dim.34), calls=%async_computation.5 | async-start | bytes 32768 | tf_op jit(solution)/shard_map/all_to_all | solution.py:347

commit v3 on v2

--- a/solution.py
+++ b/solution.py
@@ -234,7 +234,8 @@
         square = right * right
         for k in range(0, stop - start, HALF):
             whole = whole + square[:, k : k + HALF]
-    squares_ref[...] = jnp.sum(whole.T, axis=0, keepdims=True)
+    total = jnp.sum(whole.T, axis=0, keepdims=True)
+    squares_ref[...] = jnp.broadcast_to(total[None], squares_ref.shape)
 
 
 def right_part(core, w, mine, other):
@@ -246,9 +247,9 @@
         out_specs=(vmem, vmem),
         out_shape=(
             jax.ShapeDtypeStruct((RANK, columns), jnp.float32),
-            jax.ShapeDtypeStruct((1, RANK), jnp.float32),
+            jax.ShapeDtypeStruct((16, 8, RANK), jnp.float32),
         ),
-        compiler_params=params(60),
+        compiler_params=params(40),
         cost_estimate=pl.CostEstimate(flops=1300000000, bytes_accessed=3400000, transcendentals=0),
         name="right_part",
     )(core, w, mine, other)
@@ -301,7 +302,7 @@
 
 
 def weight_kernel(squares_ref, weight_ref, ortho_ref, turned_ref, high_ref, low_ref, out_ref, factor_ref):
-    squares = jnp.sum(squares_ref[...], axis=0, keepdims=True)
+    squares = jnp.sum(squares_ref[...], axis=0)[0:1]
     scale = 1.0 / jnp.sqrt(squares / COLS + 1e-06)
     rate = step_size * (ROWS / RANK) ** 0.5
     ortho = jnp.concatenate(halves(ortho_ref[...] * (scale * rate)), axis=0)
@@ -325,7 +326,7 @@
         weight_kernel,
         grid=(4,),
         in_specs=[
-            pl.BlockSpec((16, RANK), lambda i: (0, 0)),
+            pl.BlockSpec((16, 8, RANK), lambda i: (0, 0, 0)),
             block,
             pl.BlockSpec((step, RANK), lambda i: (i, 0)),
             factor,
@@ -351,12 +352,34 @@
     return exchange(jnp.broadcast_to(piece[None], (count,) + piece.shape), axis, groups)
 
 
-def gather_col(piece):
-    out = piece[None]
-    for bit in (1, 2, 4, 8):
-        pairs = [(i, i ^ bit) for i in range(16)]
-        out = jnp.concatenate([out, lax.ppermute(out, "col", pairs)], axis=0)
-    return out
+def swap(value, axis, bits):
+    return lax.ppermute(value, axis, [(i, i ^ bits) for i in range(16)])
+
+
+def z_shift(k):
+    return [(z * 2 + c, ((z + k) % 8) * 2 + c) for z in range(8) for c in range(2)]
+
+
+def gather_near(piece, unit):
+    return jnp.concatenate([piece] + [swap(piece, "col", k * unit) for k in (1, 2, 3)], axis=0)
+
+
+def scatter_z(pieces, gram):
+    z = lax.axis_index("row") // 2
+
+    def own(k):
+        return lax.dynamic_index_in_dim(pieces, (z + k) % 8, 0, keepdims=False)
+
+    down, up = own(-4), own(3)
+    for k, bits in enumerate((2, 4, 14)):
+        down = lax.ppermute(down, "row", z_shift(-1)) + own(k - 3)
+        up = lax.ppermute(up, "row", z_shift(1))
+        up = up + own(2 - k)
+        gram = gram + swap(gram, "row", bits)
+        down, up, gram = lax.optimization_barrier((down, up, gram))
+    gram = gather_near(gram[None], 1)
+    total = up + lax.ppermute(down, "row", z_shift(-1))
+    return lax.optimization_barrier((total, gather_near(gram, 4)))
 
 
 def local(gradient, momentum, weight, right_factor):
@@ -366,19 +389,19 @@
     piece = jnp.sum(exchange(partial.reshape(16, 32, RANK), "col"), axis=0)
     left = spread(piece, "col", 16).reshape(512, RANK)
     gram = dot_tn(lax.dynamic_slice(left, (0, col * 16), (512, 16)), left)
-    gram = jnp.sum(spread(gram, "row", 16), axis=0)
+    left, gram = lax.optimization_barrier((left, gram))
+    gram = gram + swap(gram, "row", 1)
     mine, other = cross_part(core, left, momentum, gradient)
-    gram, other = lax.optimization_barrier((gram, other))
     mine = mine + lax.ppermute(other, "row", CORE_SWAP)
-    mine = jnp.sum(exchange(mine.reshape(8, 16, 1664), "row", Z_GROUPS), axis=0)
-    jitter, first, gram = first_part(col.reshape(1), gather_col(gram))
-    mine, first = lax.optimization_barrier((mine, first))
+    mine, gram = lax.optimization_barrier((mine, gram))
+    mine, gram = scatter_z(mine.reshape(8, 16, 1664), gram)
+    mine = spread(mine, "row", 8, Z_GROUPS).reshape(HALF, 1664)
+    jitter, first, gram = first_part(col.reshape(1), gram)
     inverse, ortho = second_part(jitter, first, gram, left)
-    mine = spread(mine, "row", 8, Z_GROUPS).reshape(HALF, 1664)
     mine, inverse = lax.optimization_barrier((mine, inverse))
     other = lax.ppermute(mine, "row", CORE_SWAP)
     right, squares = right_part(core, inverse, mine, other)
-    squares = spread(squares, "col", 16).reshape(16, RANK)
+    squares = exchange(squares, "col")
     new_momentum, turned, high, low = momentum_part(momentum, gradient, ortho, right)
     new_weight, new_factor = weight_part(squares, weight, ortho, turned, high, low)
     return (new_weight, new_momentum, new_factor)

time: 154 us -> 139 us (0.903)
  waiting for transfers between devices: 48.2 us -> 25.1 us
  starting transfers between devices: 34.2 us -> 46.4 us
  local copies, waits for them, and re-layouts: 8.4 us -> 6.11 us
    ppermute x4 -> x17, starting transfers between devices: 1.44 us -> 23 us  [the longest x10 10.9 us: swap(): return lax.ppermute(value, axis, [(i, i ^ bits) for i in range(16)])]
    all_to_all x5 -> x3, waiting for transfers between devices: 29 us -> 9.64 us  [exchange(): return lax.all_to_all(pieces, axis, 0, 0, axis_index_groups=groups)]
    all_to_all x5 -> x3, starting transfers between devices: 28.6 us -> 12.5 us  [exchange(): return lax.all_to_all(pieces, axis, 0, 0, axis_index_groups=groups)]
    ppermute x1, starting transfers between devices: 4.09 us -> 8.12 us  [local(): other = lax.ppermute(mine, 'row', CORE_SWAP)]
    ppermute x1, starting transfers between devices: 0.09 us -> 2.84 us  [local(): mine = mine + lax.ppermute(other, 'row', CORE_SWAP)]
    ppermute x1, waiting for transfers between devices: 2.58 us -> 0.34 us  [local(): mine = mine + lax.ppermute(other, 'row', CORE_SWAP)]
    broadcast_in_dim x4 -> x2, local copies, waits for them, and re-layouts: 3.82 us -> 1.8 us  [spread(): jnp.broadcast_to(piece[None], (count,) + piece.shape)]
    pallas_call x1, Pallas kernels: 4.36 us -> 2.47 us  [right_part(): pl.pallas_call(right_kernel, in_specs=[pl.BlockSpec(memory_space=pltpu.SM...]
  transfers between devices with their start and end apart: 11 -> 22, of which waited for: 10 -> 10; matrix products, arithmetic and copies ran while one was open for 0% -> 0% of each run, Pallas kernels for 17% -> 18%
where the time goes in v3:
time: 139 us; the launch traced here: 138 us
  starting transfers between devices  46.4 us (33%)
  Pallas kernels  40.9 us (29%)
  waiting for transfers between devices  25.1 us (18%)
  blocking collectives  18.2 us (13%)
  local copies, waits for them, and re-layouts  6.11 us (4%)
    all_to_all x1, blocking collectives, exchange(): return lax.all_to_all(pieces, axis, 0, 0, axis_index_groups=groups)  18.2 us
    all_to_all x3, starting transfers between devices, exchange(): return lax.all_to_all(pieces, axis, 0, 0, axis_index_groups=groups)  12.5 us
    ppermute x10, waiting for transfers between devices, swap(): return lax.ppermute(value, axis, [(i, i ^ bits) for i in range(16)])  11.8 us
    ppermute x10, starting transfers between devices, swap(): return lax.ppermute(value, axis, [(i, i ^ bits) for i in range(16)])  10.9 us
    pallas_call x1, Pallas kernels, second_part(): pl.pallas_call(second_kernel, out_shape=(jax.ShapeDtypeStruct((RANK, RANK...  9.71 us
    all_to_all x3, waiting for transfers between devices, exchange(): return lax.all_to_all(pieces, axis, 0, 0, axis_index_groups=groups)  9.64 us
    ppermute x3, starting transfers between devices, scatter_z(): down = lax.ppermute(down, 'row', z_shift(-1)) + own(k - 3)  8.6 us
    ppermute x1, starting transfers between devices, local(): other = lax.ppermute(mine, 'row', CORE_SWAP)  8.12 us
  transfers between devices with their start and end apart: 22, of which 10 were waited for; matrix products, arithmetic and copies ran while one was open for 0% of the time, Pallas kernels for 18%

profile of v3, /device:TPU:1, one launch (start us, length us, event | category | flops | bytes accessed | tf_op | source)
XLA Modules:
  0.0 138.5 jit_solution(14410546085917480406)
XLA Ops:
  0.6 5.2 %left_part.1 = f32[512,256]{1,0:T(8,128)} custom-call(bf16[512,1664]{1,0:T(8,128)(2,1)} %m_ref.5, bf16[512,1664]{1,0:T(8,128)(2,1)} %g_ref.5, f32[1664,256]{1,0:T(8,128)} %r_ref.1), custom_call_target="tpu_custom_call" | custom-call | flops 1744830464 | bytes 5600000 | tf_op jit(solution)/shard_map/left_part/pallas_call | solution.py:178
  5.8 18.2 %all_to_all.20 = f32[16,32,256]{2,1,0:T(8,128)S(1)} all-to-all(f32[16,32,256]{2,1,0:T(8,128)} %bitcast.34), channel_id=1, replica_groups=mesh['row'=16,'col'=16] {'col'}, dimensions={0} | all-to-all | bytes 1048576 | tf_op jit(solution)/shard_map/all_to_all | solution.py:348
  24.9 3.6 %all-to-all-start.1 = ((f32[16,32,256]{2,1,0:T(8,128)}), f32[16,32,256]{2,1,0:T(8,128)S(1)}, u32[]{:S(2)}, u32[]{:S(2)}) async-start(f32[16,32,256]{2,1,0:T(8,128)} %broadcast_in_dim.6), calls=%async_computation.1 | async-start | bytes 1048576 | tf_op jit(solution)/shard_map/all_to_all | solution.py:348
  28.5 9.6 %all-to-all-done.1 = f32[16,32,256]{2,1,0:T(8,128)S(1)} async-done(((f32[16,32,256]{2,1,0:T(8,128)}), f32[16,32,256]{2,1,0:T(8,128)S(1)}, u32[]{:S(2)}, u32[]{:S(2)}) %all-to-all-start.1) | async-done | bytes 524320 | tf_op jit(solution)/shard_map/all_to_all | solution.py:348
  38.8 1.5 %copy-done.2 = bf16[512,1664]{1,0:T(8,128)(2,1)S(1)} copy-done((bf16[512,1664]{1,0:T(8,128)(2,1)S(1)}, bf16[512,1664]{1,0:T(8,128)(2,1)}, u32[]{:S(2)}) %copy-start.2) | copy-done | bytes 1703960
  40.3 3.0 %cross_part.1 = (f32[128,1664]{1,0:T(8,128)S(1)}, f32[128,1664]{1,0:T(8,128)}) custom-call(s32[1]{0:T(128)} %bitcast.core_ref, f32[512,256]{1,0:T(8,128)S(1)} %bitcast.26, bf16[512,1664]{1,0:T(8,128)(2,1)S(1)} %copy-done.1, bf16[512,1664]{1,0:T(8,128)(2,1)S(1)} %copy-done.2), custom_call_target="tpu_custom_call" | custom-call | flops 1744830464 | bytes 5600000 | tf_op jit(solution)/shard_map/cross_part/pallas_call | solution.py:211
  43.3 2.8 %collective-permute-start = (f32[128,1664]{1,0:T(8,128)}, f32[128,1664]{1,0:T(8,128)S(1)}, u32[]{:S(2)}, u32[]{:S(2)}) collective-permute-start(f32[128,1664]{1,0:T(8,128)} %get-tuple-element.37), channel_id=1, source_target_pairs={{0,16},{16,0},{32,48},{48,32},{64,80},{80,64},{96,112},{112,96},{1... | collective-permute-start | bytes 2555912 | tf_op jit(solution)/shard_map/ppermute | solution.py:395
  46.1 1.9 %collective-permute-done.1 = f32[16,256]{1,0:T(8,128)S(1)} collective-permute-done((f32[16,256]{1,0:T(8,128)S(1)}, f32[16,256]{1,0:T(8,128)S(1)}, u32[]{:S(2)}, u32[]{:S(2)}) %collective-permute-start.1) | collective-permute-done | bytes 16416 | tf_op jit(solution)/shard_map/ppermute | solution.py:356
  48.5 1.7 %collective-permute-start.3 = (f32[16,1664]{1,0:T(8,128)S(1)}, f32[16,1664]{1,0:T(8,128)S(1)}, u32[]{:S(2)}, u32[]{:S(2)}) collective-permute-start(f32[16,1664]{1,0:T(8,128)S(1)} %get-tuple-element.73), channel_id=1, source_target_pairs={{0,32},{16,48},{32,64},{48,80},{64,96},{80,112},{96,128},{112,144}... | collective-permute-start | bytes 319496 | tf_op jit(solution)/shard_map/ppermute | solution.py:376
  50.2 4.0 %collective-permute-start.2 = (f32[16,1664]{1,0:T(8,128)S(1)}, f32[16,1664]{1,0:T(8,128)S(1)}, u32[]{:S(2)}, u32[]{:S(2)}) collective-permute-start(f32[16,1664]{1,0:T(8,128)S(1)} %get-tuple-element.74), channel_id=1, source_target_pairs={{0,224},{16,240},{32,0},{48,16},{64,32},{80,48},{96,64},{112,80},{... | collective-permute-start | bytes 319496 | tf_op jit(solution)/shard_map/ppermute | solution.py:375
  54.3 2.9 %collective-permute-done.4 = f32[16,256]{1,0:T(8,128)S(1)} collective-permute-done((f32[16,256]{1,0:T(8,128)S(1)}, f32[16,256]{1,0:T(8,128)S(1)}, u32[]{:S(2)}, u32[]{:S(2)}) %collective-permute-start.4) | collective-permute-done | bytes 16416 | tf_op jit(solution)/shard_map/ppermute | solution.py:356
  57.2 2.5 %collective-permute-start.5 = (f32[16,1664]{1,0:T(8,128)S(1)}, f32[16,1664]{1,0:T(8,128)S(1)}, u32[]{:S(2)}, u32[]{:S(2)}) collective-permute-start(f32[16,1664]{1,0:T(8,128)S(1)} %get-tuple-element.41), channel_id=1, source_target_pairs={{0,224},{16,240},{32,0},{48,16},{64,32},{80,48},{96,64},{112,80},{... | collective-permute-start | bytes 319496 | tf_op jit(solution)/shard_map/ppermute | solution.py:375
  59.8 1.6 %collective-permute-start.7 = (f32[16,256]{1,0:T(8,128)S(1)}, f32[16,256]{1,0:T(8,128)S(1)}, u32[]{:S(2)}, u32[]{:S(2)}) collective-permute-start(f32[16,256]{1,0:T(8,128)S(1)} %add.132), channel_id=1, source_target_pairs={{0,64},{16,80},{32,96},{48,112},{64,0},{80,16},{96,32},{112,48},{1... | collective-permute-start | bytes 49160 | tf_op jit(solution)/shard_map/ppermute | solution.py:356
  61.3 1.9 %collective-permute-done.7 = f32[16,256]{1,0:T(8,128)S(1)} collective-permute-done((f32[16,256]{1,0:T(8,128)S(1)}, f32[16,256]{1,0:T(8,128)S(1)}, u32[]{:S(2)}, u32[]{:S(2)}) %collective-permute-start.7) | collective-permute-done | bytes 16416 | tf_op jit(solution)/shard_map/ppermute | solution.py:356
  63.3 1.3 collective-permute-done.6
  64.6 2.1 %collective-permute-start.8 = (f32[16,1664]{1,0:T(8,128)S(1)}, f32[16,1664]{1,0:T(8,128)S(1)}, u32[]{:S(2)}, u32[]{:S(2)}) collective-permute-start(f32[16,1664]{1,0:T(8,128)S(1)} %get-tuple-element.44), channel_id=1, source_target_pairs={{0,224},{16,240},{32,0},{48,16},{64,32},{80,48},{96,64},{112,80},{... | collective-permute-start | bytes 319496 | tf_op jit(solution)/shard_map/ppermute | solution.py:375
  66.6 2.7 %collective-permute-start.10 = (f32[16,256]{1,0:T(8,128)S(1)}, f32[16,256]{1,0:T(8,128)S(1)}, u32[]{:S(2)}, u32[]{:S(2)}) collective-permute-start(f32[16,256]{1,0:T(8,128)S(1)} %add.141), channel_id=1, source_target_pairs={{0,224},{16,240},{32,192},{48,208},{64,160},{80,176},{96,128},{112... | collective-permute-start | bytes 49160 | tf_op jit(solution)/shard_map/ppermute | solution.py:356
  69.3 2.4 %collective-permute-done.10 = f32[16,256]{1,0:T(8,128)S(1)} collective-permute-done((f32[16,256]{1,0:T(8,128)S(1)}, f32[16,256]{1,0:T(8,128)S(1)}, u32[]{:S(2)}, u32[]{:S(2)}) %collective-permute-start.10) | collective-permute-done | bytes 16416 | tf_op jit(solution)/shard_map/ppermute | solution.py:356
  72.0 1.9 %collective-permute-start.13 = (f32[1,16,256]{2,1,0:T(8,128)S(1)}, f32[1,16,256]{2,1,0:T(8,128)S(1)}, u32[]{:S(2)}, u32[]{:S(2)}) collective-permute-start(f32[1,16,256]{2,1,0:T(8,128)S(1)} %bitcast.36), channel_id=1, source_target_pairs={{0,2},{1,3},{2,0},{3,1},{4,6},{5,7},{6,4},{7,5},{8,10},{9,11},{10,... | collective-permute-start | bytes 49160 | tf_op jit(solution)/shard_map/ppermute | solution.py:356
  75.1 1.7 %collective-permute-start.11 = (f32[16,1664]{1,0:T(8,128)S(1)}, f32[16,1664]{1,0:T(8,128)S(1)}, u32[]{:S(2)}, u32[]{:S(2)}) collective-permute-start(f32[16,1664]{1,0:T(8,128)S(1)} %get-tuple-element.48), channel_id=1, source_target_pairs={{0,224},{16,240},{32,0},{48,16},{64,32},{80,48},{96,64},{112,80},{... | collective-permute-start | bytes 319496 | tf_op jit(solution)/shard_map/ppermute | solution.py:381
  78.4 1.8 %collective-permute-start.15 = (f32[4,16,256]{2,1,0:T(8,128)S(1)}, f32[4,16,256]{2,1,0:T(8,128)S(1)}, u32[]{:S(2)}, u32[]{:S(2)}) collective-permute-start(f32[4,16,256]{2,1,0:T(8,128)S(1)} %pad_maximum_fusion), channel_id=1, source_target_pairs={{0,4},{1,5},{2,6},{3,7},{4,0},{5,1},{6,2},{7,3},{8,12},{9,13},{10,... | collective-permute-start | bytes 196616 | tf_op jit(solution)/shard_map/ppermute | solution.py:356
  80.2 2.6 %collective-permute-done.15 = f32[4,16,256]{2,1,0:T(8,128)S(1)} collective-permute-done((f32[4,16,256]{2,1,0:T(8,128)S(1)}, f32[4,16,256]{2,1,0:T(8,128)S(1)}, u32[]{:S(2)}, u32[]{:S(2)}) %collective-permute-start.15) | collective-permute-done | bytes 65568 | tf_op jit(solution)/shard_map/ppermute | solution.py:356
  83.9 4.0 %all-to-all-start.2 = ((f32[8,16,1664]{2,1,0:T(8,128)}), f32[8,16,1664]{2,1,0:T(8,128)S(1)}, u32[]{:S(2)}, u32[]{:S(2)}) async-start(f32[8,16,1664]{2,1,0:T(8,128)} %broadcast_in_dim.8), calls=%async_computation.2 | async-start | bytes 1703936 | tf_op jit(solution)/shard_map/all_to_all | solution.py:348
  87.9 7.7 %first_factor.1 = (f32[8,128]{1,0:T(8,128)}, f32[128,128]{1,0:T(8,128)}, f32[256,256]{1,0:T(8,128)}) custom-call(s32[1]{0:T(128)} %bitcast.14.col_ref, f32[16,16,256]{2,1,0:T(8,128)} %copy-done.6), custom_call_target="tpu_custom_call" | custom-call | flops 6000000 | bytes 20000000 | tf_op jit(solution)/shard_map/first_factor/pallas_call | solution.py:124
  95.6 9.7 %second_factor.1 = (f32[256,256]{1,0:T(8,128)}, f32[512,256]{1,0:T(8,128)}) custom-call(f32[256,256]{1,0:T(8,128)} %get-tuple-element.52.gram_ref, f32[8,128]{1,0:T(8,128)} %get-tuple-element.53.jitter_ref, f32[128,128]{1,0:T(8,128)} %get-tuple-element.54.first_ref, f32[512,256]{1,0:T(8,128)} %bitcast.27), custom_call_target="tpu_custom_call" | custom-call | flops 6000000 | bytes 24000000 | tf_op jit(solution)/shard_map/second_factor/pallas_call | solution.py:139
  105.3 8.1 %collective-permute-start.18 = (f32[128,1664]{1,0:T(8,128)S(1)}, f32[128,1664]{1,0:T(8,128)S(1)}, u32[]{:S(2)}, u32[]{:S(2)}) collective-permute-start(f32[128,1664]{1,0:T(8,128)S(1)} %bitcast.28), channel_id=1, source_target_pairs={{0,16},{16,0},{32,48},{48,32},{64,80},{80,64},{96,112},{112,96},{1... | collective-permute-start | bytes 2555912 | tf_op jit(solution)/shard_map/ppermute | solution.py:402
  113.4 2.0 %collective-permute-done.18.other_ref = f32[128,1664]{1,0:T(8,128)S(1)} collective-permute-done((f32[128,1664]{1,0:T(8,128)S(1)}, f32[128,1664]{1,0:T(8,128)S(1)}, u32[]{:S(2)}, u32[]{:S(2)}) %collective-permute-start.18) | collective-permute-done | bytes 852000 | tf_op jit(solution)/shard_map/ppermute | solution.py:402
  116.4 2.5 %right_part.1 = (f32[256,1664]{1,0:T(8,128)S(1)}, f32[16,8,256]{2,1,0:T(8,128)}) custom-call(s32[1]{0:T(128)} %bitcast.core_ref, f32[256,256]{1,0:T(8,128)S(1)} %copy-done.4, f32[128,1664]{1,0:T(8,128)S(1)} %bitcast.29, f32[128,1664]{1,0:T(8,128)S(1)} %collective-permute-done.18.other_ref), custom_call_target="tpu_custom_call" | custom-call | flops 1300000000 | bytes 3400000 | tf_op jit(solution)/shard_map/right_part/pallas_call | solution.py:244
  118.8 1.2 copy-done.3
  120.0 4.9 %all-to-all-start.3 = ((f32[16,8,256]{2,1,0:T(8,128)}), f32[16,8,256]{2,1,0:T(8,128)S(1)}, u32[]{:S(2)}, u32[]{:S(2)}) async-start(f32[16,8,256]{2,1,0:T(8,128)} %get-tuple-element.58), calls=%async_computation.3 | async-start | bytes 262144 | tf_op jit(solution)/shard_map/all_to_all | solution.py:348
  125.0 6.9 %momentum_part.1 = (bf16[512,1664]{1,0:T(8,128)(2,1)}, f32[1664,256]{1,0:T(8,128)}, bf16[256,1664]{1,0:T(8,128)(2,1)}, bf16[256,1664]{1,0:T(8,128)(2,1)}) custom-call(bf16[512,1664]{1,0:T(8,128)(2,1)} %m_ref.5, bf16[512,1664]{1,0:T(8,128)(2,1)} %g_ref.5, f32[512,256]{1,0:T(8,128)} %get-tuple-element.59.ortho_ref, f32[256,1664]{1,0:T(8,128)} %copy-done.3), custom_call_target="tpu_custom_call" | custom-call | flops 1308622848 | bytes 7500000 | tf_op jit(solution)/shard_map/momentum_part/pallas_call | solution.py:287
  132.5 6.0 %weight_part.1 = (bf16[512,1664]{1,0:T(8,128)(2,1)}, f32[1664,256]{1,0:T(8,128)}) custom-call(f32[16,8,256]{2,1,0:T(8,128)} %copy-done.5, bf16[512,1664]{1,0:T(8,128)(2,1)} %weight_ref.1, f32[512,256]{1,0:T(8,128)} %get-tuple-element.59.ortho_ref, f32[1664,256]{1,0:T(8,128)} %get-tuple-element.61.turned_ref, bf16[256,1664]{1,0:T(8,128)(2,1)} %get-tuple-element.62.high_ref, ...), custom_call_target="tpu_custom_call" | custom-call | flops 1308622848 | bytes 7500000 | tf_op jit(solution)/shard_map/weight_part/pallas_call | solution.py:325
  (56 shorter events, 7.8 us)
Async XLA Ops:
  5.8 33.0 %copy-start.1 = (bf16[512,1664]{1,0:T(8,128)(2,1)S(1)}, bf16[512,1664]{1,0:T(8,128)(2,1)}, u32[]{:S(2)}) copy-start(bf16[512,1664]{1,0:T(8,128)(2,1)} %m_ref.5) | copy-start | bytes 5111812
  24.9 13.2 %all-to-all-start.1 = ((f32[16,32,256]{2,1,0:T(8,128)}), f32[16,32,256]{2,1,0:T(8,128)S(1)}, u32[]{:S(2)}, u32[]{:S(2)}) async-start(f32[16,32,256]{2,1,0:T(8,128)} %broadcast_in_dim.6), calls=%async_computation.1 | async-start | bytes 1048576 | tf_op jit(solution)/shard_map/all_to_all | solution.py:348
  38.1 5.2 %copy-start = (f32[16,32,256]{2,1,0:T(8,128)}, f32[16,32,256]{2,1,0:T(8,128)S(1)}, u32[]{:S(2)}) copy-start(f32[16,32,256]{2,1,0:T(8,128)S(1)} %all-to-all-done.1) | copy-start | bytes 1572868
  38.8 1.5 %copy-start.2 = (bf16[512,1664]{1,0:T(8,128)(2,1)S(1)}, bf16[512,1664]{1,0:T(8,128)(2,1)}, u32[]{:S(2)}) copy-start(bf16[512,1664]{1,0:T(8,128)(2,1)} %g_ref.5) | copy-start | bytes 5111812
  43.3 5.1 %collective-permute-start = (f32[128,1664]{1,0:T(8,128)}, f32[128,1664]{1,0:T(8,128)S(1)}, u32[]{:S(2)}, u32[]{:S(2)}) collective-permute-start(f32[128,1664]{1,0:T(8,128)} %get-tuple-element.37), channel_id=1, source_target_pairs={{0,16},{16,0},{32,48},{48,32},{64,80},{80,64},{96,112},{112,96},{1... | collective-permute-start | bytes 2555912 | tf_op jit(solution)/shard_map/ppermute | solution.py:395
  46.1 1.9 %collective-permute-start.1 = (f32[16,256]{1,0:T(8,128)S(1)}, f32[16,256]{1,0:T(8,128)S(1)}, u32[]{:S(2)}, u32[]{:S(2)}) collective-permute-start(f32[16,256]{1,0:T(8,128)S(1)} %fusion), channel_id=1, source_target_pairs={{0,16},{16,0},{32,48},{48,32},{64,80},{80,64},{96,112},{112,96},{1... | collective-permute-start | bytes 49160 | tf_op jit(solution)/shard_map/ppermute | solution.py:356
  48.5 8.7 %collective-permute-start.3 = (f32[16,1664]{1,0:T(8,128)S(1)}, f32[16,1664]{1,0:T(8,128)S(1)}, u32[]{:S(2)}, u32[]{:S(2)}) collective-permute-start(f32[16,1664]{1,0:T(8,128)S(1)} %get-tuple-element.73), channel_id=1, source_target_pairs={{0,32},{16,48},{32,64},{48,80},{64,96},{80,112},{96,128},{112,144}... | collective-permute-start | bytes 319496 | tf_op jit(solution)/shard_map/ppermute | solution.py:376
  50.2 7.0 %collective-permute-start.2 = (f32[16,1664]{1,0:T(8,128)S(1)}, f32[16,1664]{1,0:T(8,128)S(1)}, u32[]{:S(2)}, u32[]{:S(2)}) collective-permute-start(f32[16,1664]{1,0:T(8,128)S(1)} %get-tuple-element.74), channel_id=1, source_target_pairs={{0,224},{16,240},{32,0},{48,16},{64,32},{80,48},{96,64},{112,80},{... | collective-permute-start | bytes 319496 | tf_op jit(solution)/shard_map/ppermute | solution.py:375
  54.3 2.9 %collective-permute-start.4 = (f32[16,256]{1,0:T(8,128)S(1)}, f32[16,256]{1,0:T(8,128)S(1)}, u32[]{:S(2)}, u32[]{:S(2)}) collective-permute-start(f32[16,256]{1,0:T(8,128)S(1)} %add.117), channel_id=1, source_target_pairs={{0,32},{16,48},{32,0},{48,16},{64,96},{80,112},{96,64},{112,80},{1... | collective-permute-start | bytes 49160 | tf_op jit(solution)/shard_map/ppermute | solution.py:356
  57.2 6.0 %collective-permute-start.5 = (f32[16,1664]{1,0:T(8,128)S(1)}, f32[16,1664]{1,0:T(8,128)S(1)}, u32[]{:S(2)}, u32[]{:S(2)}) collective-permute-start(f32[16,1664]{1,0:T(8,128)S(1)} %get-tuple-element.41), channel_id=1, source_target_pairs={{0,224},{16,240},{32,0},{48,16},{64,32},{80,48},{96,64},{112,80},{... | collective-permute-start | bytes 319496 | tf_op jit(solution)/shard_map/ppermute | solution.py:375
  59.8 4.8 %collective-permute-start.6 = (f32[16,1664]{1,0:T(8,128)S(1)}, f32[16,1664]{1,0:T(8,128)S(1)}, u32[]{:S(2)}, u32[]{:S(2)}) collective-permute-start(f32[16,1664]{1,0:T(8,128)S(1)} %get-tuple-element.42), channel_id=1, source_target_pairs={{0,32},{16,48},{32,64},{48,80},{64,96},{80,112},{96,128},{112,144}... | collective-permute-start | bytes 319496 | tf_op jit(solution)/shard_map/ppermute | solution.py:376
  59.8 3.5 %collective-permute-start.7 = (f32[16,256]{1,0:T(8,128)S(1)}, f32[16,256]{1,0:T(8,128)S(1)}, u32[]{:S(2)}, u32[]{:S(2)}) collective-permute-start(f32[16,256]{1,0:T(8,128)S(1)} %add.132), channel_id=1, source_target_pairs={{0,64},{16,80},{32,96},{48,112},{64,0},{80,16},{96,32},{112,48},{1... | collective-permute-start | bytes 49160 | tf_op jit(solution)/shard_map/ppermute | solution.py:356
  64.6 7.2 %collective-permute-start.8 = (f32[16,1664]{1,0:T(8,128)S(1)}, f32[16,1664]{1,0:T(8,128)S(1)}, u32[]{:S(2)}, u32[]{:S(2)}) collective-permute-start(f32[16,1664]{1,0:T(8,128)S(1)} %get-tuple-element.44), channel_id=1, source_target_pairs={{0,224},{16,240},{32,0},{48,16},{64,32},{80,48},{96,64},{112,80},{... | collective-permute-start | bytes 319496 | tf_op jit(solution)/shard_map/ppermute | solution.py:375
  66.6 5.1 %collective-permute-start.9 = (f32[16,1664]{1,0:T(8,128)S(1)}, f32[16,1664]{1,0:T(8,128)S(1)}, u32[]{:S(2)}, u32[]{:S(2)}) collective-permute-start(f32[16,1664]{1,0:T(8,128)S(1)} %get-tuple-element.45), channel_id=1, source_target_pairs={{0,32},{16,48},{32,64},{48,80},{64,96},{80,112},{96,128},{112,144}... | collective-permute-start | bytes 319496 | tf_op jit(solution)/shard_map/ppermute | solution.py:376
  66.6 5.1 %collective-permute-start.10 = (f32[16,256]{1,0:T(8,128)S(1)}, f32[16,256]{1,0:T(8,128)S(1)}, u32[]{:S(2)}, u32[]{:S(2)}) collective-permute-start(f32[16,256]{1,0:T(8,128)S(1)} %add.141), channel_id=1, source_target_pairs={{0,224},{16,240},{32,192},{48,208},{64,160},{80,176},{96,128},{112... | collective-permute-start | bytes 49160 | tf_op jit(solution)/shard_map/ppermute | solution.py:356
  71.8 5.0 %collective-permute-start.14 = (f32[1,16,256]{2,1,0:T(8,128)S(1)}, f32[1,16,256]{2,1,0:T(8,128)S(1)}, u32[]{:S(2)}, u32[]{:S(2)}) collective-permute-start(f32[1,16,256]{2,1,0:T(8,128)S(1)} %bitcast.35), channel_id=1, source_target_pairs={{0,3},{1,2},{2,1},{3,0},{4,7},{5,6},{6,5},{7,4},{8,11},{9,10},{10,... | collective-permute-start | bytes 49160 | tf_op jit(solution)/shard_map/ppermute | solution.py:356
  72.0 4.8 %collective-permute-start.13 = (f32[1,16,256]{2,1,0:T(8,128)S(1)}, f32[1,16,256]{2,1,0:T(8,128)S(1)}, u32[]{:S(2)}, u32[]{:S(2)}) collective-permute-start(f32[1,16,256]{2,1,0:T(8,128)S(1)} %bitcast.36), channel_id=1, source_target_pairs={{0,2},{1,3},{2,0},{3,1},{4,6},{5,7},{6,4},{7,5},{8,10},{9,11},{10,... | collective-permute-start | bytes 49160 | tf_op jit(solution)/shard_map/ppermute | solution.py:356
  73.9 2.9 %collective-permute-start.12 = (f32[1,16,256]{2,1,0:T(8,128)S(1)}, f32[1,16,256]{2,1,0:T(8,128)S(1)}, u32[]{:S(2)}, u32[]{:S(2)}) collective-permute-start(f32[1,16,256]{2,1,0:T(8,128)S(1)} %bitcast.37), channel_id=1, source_target_pairs={{0,1},{1,0},{2,3},{3,2},{4,5},{5,4},{6,7},{7,6},{8,9},{9,8},{10,11... | collective-permute-start | bytes 49160 | tf_op jit(solution)/shard_map/ppermute | solution.py:356
  75.1 7.8 %collective-permute-start.11 = (f32[16,1664]{1,0:T(8,128)S(1)}, f32[16,1664]{1,0:T(8,128)S(1)}, u32[]{:S(2)}, u32[]{:S(2)}) collective-permute-start(f32[16,1664]{1,0:T(8,128)S(1)} %get-tuple-element.48), channel_id=1, source_target_pairs={{0,224},{16,240},{32,0},{48,16},{64,32},{80,48},{96,64},{112,80},{... | collective-permute-start | bytes 319496 | tf_op jit(solution)/shard_map/ppermute | solution.py:381
  76.8 6.0 %collective-permute-start.17 = (f32[4,16,256]{2,1,0:T(8,128)S(1)}, f32[4,16,256]{2,1,0:T(8,128)S(1)}, u32[]{:S(2)}, u32[]{:S(2)}) collective-permute-start(f32[4,16,256]{2,1,0:T(8,128)S(1)} %pad_maximum_fusion), channel_id=1, source_target_pairs={{0,12},{1,13},{2,14},{3,15},{4,8},{5,9},{6,10},{7,11},{8,4},{9,5},... | collective-permute-start | bytes 196616 | tf_op jit(solution)/shard_map/ppermute | solution.py:356
  77.5 5.4 %collective-permute-start.16 = (f32[4,16,256]{2,1,0:T(8,128)S(1)}, f32[4,16,256]{2,1,0:T(8,128)S(1)}, u32[]{:S(2)}, u32[]{:S(2)}) collective-permute-start(f32[4,16,256]{2,1,0:T(8,128)S(1)} %pad_maximum_fusion), channel_id=1, source_target_pairs={{0,8},{1,9},{2,10},{3,11},{4,12},{5,13},{6,14},{7,15},{8,0},{9,1},... | collective-permute-start | bytes 196616 | tf_op jit(solution)/shard_map/ppermute | solution.py:356
  78.4 4.4 %collective-permute-start.15 = (f32[4,16,256]{2,1,0:T(8,128)S(1)}, f32[4,16,256]{2,1,0:T(8,128)S(1)}, u32[]{:S(2)}, u32[]{:S(2)}) collective-permute-start(f32[4,16,256]{2,1,0:T(8,128)S(1)} %pad_maximum_fusion), channel_id=1, source_target_pairs={{0,4},{1,5},{2,6},{3,7},{4,0},{5,1},{6,2},{7,3},{8,12},{9,13},{10,... | collective-permute-start | bytes 196616 | tf_op jit(solution)/shard_map/ppermute | solution.py:356
  82.9 5.0 %copy-start.6 = (f32[16,16,256]{2,1,0:T(8,128)}, f32[16,16,256]{2,1,0:T(8,128)S(1)}, u32[]{:S(2)}) copy-start(f32[16,16,256]{2,1,0:T(8,128)S(1)} %constant_dynamic-update-slice_fusion.gather_ref) | copy-start | bytes 786436
  83.9 21.4 %all-to-all-start.2 = ((f32[8,16,1664]{2,1,0:T(8,128)}), f32[8,16,1664]{2,1,0:T(8,128)S(1)}, u32[]{:S(2)}, u32[]{:S(2)}) async-start(f32[8,16,1664]{2,1,0:T(8,128)} %broadcast_in_dim.8), calls=%async_computation.2 | async-start | bytes 1703936 | tf_op jit(solution)/shard_map/all_to_all | solution.py:348
  105.3 10.1 %collective-permute-start.18 = (f32[128,1664]{1,0:T(8,128)S(1)}, f32[128,1664]{1,0:T(8,128)S(1)}, u32[]{:S(2)}, u32[]{:S(2)}) collective-permute-start(f32[128,1664]{1,0:T(8,128)S(1)} %bitcast.28), channel_id=1, source_target_pairs={{0,16},{16,0},{32,48},{48,32},{64,80},{80,64},{96,112},{112,96},{1... | collective-permute-start | bytes 2555912 | tf_op jit(solution)/shard_map/ppermute | solution.py:402
  115.4 0.9 copy-start.4
  118.8 1.2 copy-start.3
  120.0 11.8 %all-to-all-start.3 = ((f32[16,8,256]{2,1,0:T(8,128)}), f32[16,8,256]{2,1,0:T(8,128)S(1)}, u32[]{:S(2)}, u32[]{:S(2)}) async-start(f32[16,8,256]{2,1,0:T(8,128)} %get-tuple-element.58), calls=%async_computation.3 | async-start | bytes 262144 | tf_op jit(solution)/shard_map/all_to_all | solution.py:348
  131.8 0.7 copy-start.5

commit v4 on v3

--- a/solution.py
+++ b/solution.py
@@ -130,6 +130,7 @@
             jax.ShapeDtypeStruct((HALF, HALF), jnp.float32),
             jax.ShapeDtypeStruct((RANK, RANK), jnp.float32),
         ),
+        compiler_params=params(24),
         cost_estimate=pl.CostEstimate(flops=6000000, bytes_accessed=20000000, transcendentals=0),
         name="first_factor",
     )(col, gather)
@@ -142,6 +143,7 @@
             jax.ShapeDtypeStruct((RANK, RANK), jnp.float32),
             jax.ShapeDtypeStruct(left.shape, jnp.float32),
         ),
+        compiler_params=params(24),
         cost_estimate=pl.CostEstimate(flops=6000000, bytes_accessed=24000000, transcendentals=0),
         name="second_factor",
     )(gram, jitter, first, left)
@@ -379,7 +381,7 @@
         down, up, gram = lax.optimization_barrier((down, up, gram))
     gram = gather_near(gram[None], 1)
     total = up + lax.ppermute(down, "row", z_shift(-1))
-    return lax.optimization_barrier((total, gather_near(gram, 4)))
+    return lax.optimization_barrier((total, gram))
 
 
 def local(gradient, momentum, weight, right_factor):
@@ -395,6 +397,7 @@
     mine = mine + lax.ppermute(other, "row", CORE_SWAP)
     mine, gram = lax.optimization_barrier((mine, gram))
     mine, gram = scatter_z(mine.reshape(8, 16, 1664), gram)
+    gram = gather_near(gram, 4)
     mine = spread(mine, "row", 8, Z_GROUPS).reshape(HALF, 1664)
     jitter, first, gram = first_part(col.reshape(1), gram)
     inverse, ortho = second_part(jitter, first, gram, left)

time: 139 us -> 136 us (0.978)
  Pallas kernels: 40.9 us -> 37.3 us
  waiting for transfers between devices: 25.1 us -> 26.6 us
    pallas_call x1, Pallas kernels: 9.71 us -> 7.77 us  [second_part(): pl.pallas_call(second_kernel, out_shape=(jax.ShapeDtypeStruct((RANK, RANK...]
    ppermute x1, waiting for transfers between devices: 0.01 us -> 1.84 us  [scatter_z(): total = up + lax.ppermute(down, 'row', z_shift(-1))]
    pallas_call x1, Pallas kernels: 7.68 us -> 6 us  [first_part(): pl.pallas_call(first_kernel, in_specs=[pl.BlockSpec(memory_space=pltpu.SM...]
    unnamed x20 -> x10, local copies, waits for them, and re-layouts: 4.28 us -> 4.07 us
  transfers between devices with their start and end apart: 22 -> 22, of which waited for: 10 -> 13; matrix products, arithmetic and copies ran while one was open for 0% -> 0% of each run, Pallas kernels for 18% -> 15%
where the time goes in v4:
time: 136 us
  starting transfers between devices  45.9 us (34%)
  Pallas kernels  37.3 us (27%)
  waiting for transfers between devices  26.6 us (20%)
  blocking collectives  18.2 us (13%)
  local copies, waits for them, and re-layouts  5.9 us (4%)
    all_to_all x1, blocking collectives, exchange(): return lax.all_to_all(pieces, axis, 0, 0, axis_index_groups=groups)  18.2 us
    all_to_all x3, starting transfers between devices, exchange(): return lax.all_to_all(pieces, axis, 0, 0, axis_index_groups=groups)  11.9 us
    ppermute x10, waiting for transfers between devices, swap(): return lax.ppermute(value, axis, [(i, i ^ bits) for i in range(16)])  11.5 us
    ppermute x10, starting transfers between devices, swap(): return lax.ppermute(value, axis, [(i, i ^ bits) for i in range(16)])  10.9 us
    all_to_all x3, waiting for transfers between devices, exchange(): return lax.all_to_all(pieces, axis, 0, 0, axis_index_groups=groups)  9.64 us
    ppermute x3, starting transfers between devices, scatter_z(): down = lax.ppermute(down, 'row', z_shift(-1)) + own(k - 3)  8.6 us
    ppermute x1, starting transfers between devices, local(): other = lax.ppermute(mine, 'row', CORE_SWAP)  8.35 us
    pallas_call x1, Pallas kernels, second_part(): pl.pallas_call(second_kernel, out_shape=(jax.ShapeDtypeStruct((RANK, RANK...  7.77 us
  transfers between devices with their start and end apart: 22, of which 13 were waited for; matrix products, arithmetic and copies ran while one was open for 0% of the time, Pallas kernels for 15%

profile of v4, /device:TPU:1, one launch (start us, length us, event | category | flops | bytes accessed | tf_op | source)
XLA Modules:
  0.0 135.7 jit_solution(11661615338833396920)
XLA Ops:
  0.6 5.2 %left_part.1 = f32[512,256]{1,0:T(8,128)} custom-call(bf16[512,1664]{1,0:T(8,128)(2,1)} %m_ref.5, bf16[512,1664]{1,0:T(8,128)(2,1)} %g_ref.5, f32[1664,256]{1,0:T(8,128)} %r_ref.1), custom_call_target="tpu_custom_call" | custom-call | flops 1744830464 | bytes 5600000 | tf_op jit(solution)/shard_map/left_part/pallas_call | solution.py:180
  5.8 18.2 %all_to_all.20 = f32[16,32,256]{2,1,0:T(8,128)S(1)} all-to-all(f32[16,32,256]{2,1,0:T(8,128)} %bitcast.33), channel_id=1, replica_groups=mesh['row'=16,'col'=16] {'col'}, dimensions={0} | all-to-all | bytes 1048576 | tf_op jit(solution)/shard_map/all_to_all | solution.py:350
  24.9 3.6 %all-to-all-start.1 = ((f32[16,32,256]{2,1,0:T(8,128)}), f32[16,32,256]{2,1,0:T(8,128)S(1)}, u32[]{:S(2)}, u32[]{:S(2)}) async-start(f32[16,32,256]{2,1,0:T(8,128)} %broadcast_in_dim.6), calls=%async_computation.1 | async-start | bytes 1048576 | tf_op jit(solution)/shard_map/all_to_all | solution.py:350
  28.5 9.6 %all-to-all-done.1 = f32[16,32,256]{2,1,0:T(8,128)S(1)} async-done(((f32[16,32,256]{2,1,0:T(8,128)}), f32[16,32,256]{2,1,0:T(8,128)S(1)}, u32[]{:S(2)}, u32[]{:S(2)}) %all-to-all-start.1) | async-done | bytes 524320 | tf_op jit(solution)/shard_map/all_to_all | solution.py:350
  38.8 1.5 %copy-done.2 = bf16[512,1664]{1,0:T(8,128)(2,1)S(1)} copy-done((bf16[512,1664]{1,0:T(8,128)(2,1)S(1)}, bf16[512,1664]{1,0:T(8,128)(2,1)}, u32[]{:S(2)}) %copy-start.2) | copy-done | bytes 1703960
  40.3 3.0 %cross_part.1 = (f32[128,1664]{1,0:T(8,128)S(1)}, f32[128,1664]{1,0:T(8,128)}) custom-call(s32[1]{0:T(128)} %bitcast.core_ref, f32[512,256]{1,0:T(8,128)S(1)} %bitcast.25, bf16[512,1664]{1,0:T(8,128)(2,1)S(1)} %copy-done.1, bf16[512,1664]{1,0:T(8,128)(2,1)S(1)} %copy-done.2), custom_call_target="tpu_custom_call" | custom-call | flops 1744830464 | bytes 5600000 | tf_op jit(solution)/shard_map/cross_part/pallas_call | solution.py:213
  43.3 2.8 %collective-permute-start = (f32[128,1664]{1,0:T(8,128)}, f32[128,1664]{1,0:T(8,128)S(1)}, u32[]{:S(2)}, u32[]{:S(2)}) collective-permute-start(f32[128,1664]{1,0:T(8,128)} %get-tuple-element.37), channel_id=1, source_target_pairs={{0,16},{16,0},{32,48},{48,32},{64,80},{80,64},{96,112},{112,96},{1... | collective-permute-start | bytes 2555912 | tf_op jit(solution)/shard_map/ppermute | solution.py:397
  46.1 1.9 %collective-permute-done.1 = f32[16,256]{1,0:T(8,128)S(1)} collective-permute-done((f32[16,256]{1,0:T(8,128)S(1)}, f32[16,256]{1,0:T(8,128)S(1)}, u32[]{:S(2)}, u32[]{:S(2)}) %collective-permute-start.1) | collective-permute-done | bytes 16416 | tf_op jit(solution)/shard_map/ppermute | solution.py:358
  48.5 1.7 %collective-permute-start.3 = (f32[16,1664]{1,0:T(8,128)S(1)}, f32[16,1664]{1,0:T(8,128)S(1)}, u32[]{:S(2)}, u32[]{:S(2)}) collective-permute-start(f32[16,1664]{1,0:T(8,128)S(1)} %get-tuple-element.73), channel_id=1, source_target_pairs={{0,32},{16,48},{32,64},{48,80},{64,96},{80,112},{96,128},{112,144}... | collective-permute-start | bytes 319496 | tf_op jit(solution)/shard_map/ppermute | solution.py:378
  50.2 4.0 %collective-permute-start.2 = (f32[16,1664]{1,0:T(8,128)S(1)}, f32[16,1664]{1,0:T(8,128)S(1)}, u32[]{:S(2)}, u32[]{:S(2)}) collective-permute-start(f32[16,1664]{1,0:T(8,128)S(1)} %get-tuple-element.74), channel_id=1, source_target_pairs={{0,224},{16,240},{32,0},{48,16},{64,32},{80,48},{96,64},{112,80},{... | collective-permute-start | bytes 319496 | tf_op jit(solution)/shard_map/ppermute | solution.py:377
  54.2 2.9 %collective-permute-done.4 = f32[16,256]{1,0:T(8,128)S(1)} collective-permute-done((f32[16,256]{1,0:T(8,128)S(1)}, f32[16,256]{1,0:T(8,128)S(1)}, u32[]{:S(2)}, u32[]{:S(2)}) %collective-permute-start.4) | collective-permute-done | bytes 16416 | tf_op jit(solution)/shard_map/ppermute | solution.py:358
  57.2 2.5 %collective-permute-start.5 = (f32[16,1664]{1,0:T(8,128)S(1)}, f32[16,1664]{1,0:T(8,128)S(1)}, u32[]{:S(2)}, u32[]{:S(2)}) collective-permute-start(f32[16,1664]{1,0:T(8,128)S(1)} %get-tuple-element.41), channel_id=1, source_target_pairs={{0,224},{16,240},{32,0},{48,16},{64,32},{80,48},{96,64},{112,80},{... | collective-permute-start | bytes 319496 | tf_op jit(solution)/shard_map/ppermute | solution.py:377
  59.8 1.6 %collective-permute-start.7 = (f32[16,256]{1,0:T(8,128)S(1)}, f32[16,256]{1,0:T(8,128)S(1)}, u32[]{:S(2)}, u32[]{:S(2)}) collective-permute-start(f32[16,256]{1,0:T(8,128)S(1)} %add.132), channel_id=1, source_target_pairs={{0,64},{16,80},{32,96},{48,112},{64,0},{80,16},{96,32},{112,48},{1... | collective-permute-start | bytes 49160 | tf_op jit(solution)/shard_map/ppermute | solution.py:358
  61.3 1.9 %collective-permute-done.7 = f32[16,256]{1,0:T(8,128)S(1)} collective-permute-done((f32[16,256]{1,0:T(8,128)S(1)}, f32[16,256]{1,0:T(8,128)S(1)}, u32[]{:S(2)}, u32[]{:S(2)}) %collective-permute-start.7) | collective-permute-done | bytes 16416 | tf_op jit(solution)/shard_map/ppermute | solution.py:358
  63.2 1.3 collective-permute-done.6
  64.5 2.1 %collective-permute-start.8 = (f32[16,1664]{1,0:T(8,128)S(1)}, f32[16,1664]{1,0:T(8,128)S(1)}, u32[]{:S(2)}, u32[]{:S(2)}) collective-permute-start(f32[16,1664]{1,0:T(8,128)S(1)} %get-tuple-element.44), channel_id=1, source_target_pairs={{0,224},{16,240},{32,0},{48,16},{64,32},{80,48},{96,64},{112,80},{... | collective-permute-start | bytes 319496 | tf_op jit(solution)/shard_map/ppermute | solution.py:377
  66.6 2.7 %collective-permute-start.10 = (f32[16,256]{1,0:T(8,128)S(1)}, f32[16,256]{1,0:T(8,128)S(1)}, u32[]{:S(2)}, u32[]{:S(2)}) collective-permute-start(f32[16,256]{1,0:T(8,128)S(1)} %add.141), channel_id=1, source_target_pairs={{0,224},{16,240},{32,192},{48,208},{64,160},{80,176},{96,128},{112... | collective-permute-start | bytes 49160 | tf_op jit(solution)/shard_map/ppermute | solution.py:358
  69.3 2.4 %collective-permute-done.10 = f32[16,256]{1,0:T(8,128)S(1)} collective-permute-done((f32[16,256]{1,0:T(8,128)S(1)}, f32[16,256]{1,0:T(8,128)S(1)}, u32[]{:S(2)}, u32[]{:S(2)}) %collective-permute-start.10) | collective-permute-done | bytes 16416 | tf_op jit(solution)/shard_map/ppermute | solution.py:358
  72.0 1.9 %collective-permute-start.13 = (f32[1,16,256]{2,1,0:T(8,128)S(1)}, f32[1,16,256]{2,1,0:T(8,128)S(1)}, u32[]{:S(2)}, u32[]{:S(2)}) collective-permute-start(f32[1,16,256]{2,1,0:T(8,128)S(1)} %bitcast.35), channel_id=1, source_target_pairs={{0,2},{1,3},{2,0},{3,1},{4,6},{5,7},{6,4},{7,5},{8,10},{9,11},{10,... | collective-permute-start | bytes 49160 | tf_op jit(solution)/shard_map/ppermute | solution.py:358
  75.1 1.7 %collective-permute-start.11 = (f32[16,1664]{1,0:T(8,128)S(1)}, f32[16,1664]{1,0:T(8,128)S(1)}, u32[]{:S(2)}, u32[]{:S(2)}) collective-permute-start(f32[16,1664]{1,0:T(8,128)S(1)} %get-tuple-element.48), channel_id=1, source_target_pairs={{0,224},{16,240},{32,0},{48,16},{64,32},{80,48},{96,64},{112,80},{... | collective-permute-start | bytes 319496 | tf_op jit(solution)/shard_map/ppermute | solution.py:383
  76.8 1.8 %collective-permute-done.11 = f32[16,1664]{1,0:T(8,128)S(1)} collective-permute-done((f32[16,1664]{1,0:T(8,128)S(1)}, f32[16,1664]{1,0:T(8,128)S(1)}, u32[]{:S(2)}, u32[]{:S(2)}) %collective-permute-start.11) | collective-permute-done | bytes 106528 | tf_op jit(solution)/shard_map/ppermute | solution.py:383
  79.7 4.8 %all-to-all-start.2 = ((f32[8,16,1664]{2,1,0:T(8,128)}), f32[8,16,1664]{2,1,0:T(8,128)S(1)}, u32[]{:S(2)}, u32[]{:S(2)}) async-start(f32[8,16,1664]{2,1,0:T(8,128)} %broadcast_in_dim.8), calls=%async_computation.2 | async-start | bytes 1703936 | tf_op jit(solution)/shard_map/all_to_all | solution.py:350
  85.7 2.0 %collective-permute-start.15 = (f32[4,16,256]{2,1,0:T(8,128)S(1)}, f32[4,16,256]{2,1,0:T(8,128)S(1)}, u32[]{:S(2)}, u32[]{:S(2)}) collective-permute-start(f32[4,16,256]{2,1,0:T(8,128)S(1)} %pad_maximum_fusion.1), channel_id=1, source_target_pairs={{0,4},{1,5},{2,6},{3,7},{4,0},{5,1},{6,2},{7,3},{8,12},{9,13},{10,... | collective-permute-start | bytes 196616 | tf_op jit(solution)/shard_map/ppermute | solution.py:358
  90.1 6.0 %first_factor.1 = (f32[8,128]{1,0:T(8,128)S(1)}, f32[128,128]{1,0:T(8,128)S(1)}, f32[256,256]{1,0:T(8,128)S(1)}) custom-call(s32[1]{0:T(128)} %bitcast.14.col_ref, f32[16,16,256]{2,1,0:T(8,128)S(1)} %pad_maximum_fusion.gather_ref), custom_call_target="tpu_custom_call" | custom-call | flops 6000000 | bytes 20000000 | tf_op jit(solution)/shard_map/first_factor/pallas_call | solution.py:124
  96.1 7.8 %second_factor.1 = (f32[256,256]{1,0:T(8,128)S(1)}, f32[512,256]{1,0:T(8,128)S(1)}) custom-call(f32[256,256]{1,0:T(8,128)S(1)} %get-tuple-element.52.gram_ref, f32[8,128]{1,0:T(8,128)S(1)} %get-tuple-element.53.jitter_ref, f32[128,128]{1,0:T(8,128)S(1)} %get-tuple-element.54.first_ref, f32[512,256]{1,0:T(8,128)S(1)} %bitcast.26), custom_call_target="tpu_custom_call" | custom-call | flops 6000000 | bytes 24000000 | tf_op jit(solution)/shard_map/second_factor/pallas_call | solution.py:140
  104.6 8.3 %collective-permute-start.18 = (f32[128,1664]{1,0:T(8,128)S(1)}, f32[128,1664]{1,0:T(8,128)S(1)}, u32[]{:S(2)}, u32[]{:S(2)}) collective-permute-start(f32[128,1664]{1,0:T(8,128)S(1)} %bitcast.27), channel_id=1, source_target_pairs={{0,16},{16,0},{32,48},{48,32},{64,80},{80,64},{96,112},{112,96},{1... | collective-permute-start | bytes 2555912 | tf_op jit(solution)/shard_map/ppermute | solution.py:405
  113.0 2.0 %collective-permute-done.18.other_ref = f32[128,1664]{1,0:T(8,128)S(1)} collective-permute-done((f32[128,1664]{1,0:T(8,128)S(1)}, f32[128,1664]{1,0:T(8,128)S(1)}, u32[]{:S(2)}, u32[]{:S(2)}) %collective-permute-start.18) | collective-permute-done | bytes 852000 | tf_op jit(solution)/shard_map/ppermute | solution.py:405
  115.0 2.5 %right_part.1 = (f32[256,1664]{1,0:T(8,128)S(1)}, f32[16,8,256]{2,1,0:T(8,128)}) custom-call(s32[1]{0:T(128)} %bitcast.core_ref, f32[256,256]{1,0:T(8,128)S(1)} %get-tuple-element.56.w_ref, f32[128,1664]{1,0:T(8,128)S(1)} %bitcast.28, f32[128,1664]{1,0:T(8,128)S(1)} %collective-permute-done.18.other_ref), custom_call_target="tpu_custom_call" | custom-call | flops 1300000000 | bytes 3400000 | tf_op jit(solution)/shard_map/right_part/pallas_call | solution.py:246
  117.5 1.2 copy-done.3
  118.6 3.5 %all-to-all-start.3 = ((f32[16,8,256]{2,1,0:T(8,128)}), f32[16,8,256]{2,1,0:T(8,128)S(1)}, u32[]{:S(2)}, u32[]{:S(2)}) async-start(f32[16,8,256]{2,1,0:T(8,128)} %get-tuple-element.58), calls=%async_computation.3 | async-start | bytes 262144 | tf_op jit(solution)/shard_map/all_to_all | solution.py:350
  122.2 6.9 %momentum_part.1 = (bf16[512,1664]{1,0:T(8,128)(2,1)}, f32[1664,256]{1,0:T(8,128)}, bf16[256,1664]{1,0:T(8,128)(2,1)}, bf16[256,1664]{1,0:T(8,128)(2,1)}) custom-call(bf16[512,1664]{1,0:T(8,128)(2,1)} %m_ref.5, bf16[512,1664]{1,0:T(8,128)(2,1)} %g_ref.5, f32[512,256]{1,0:T(8,128)} %copy-done, f32[256,1664]{1,0:T(8,128)} %copy-done.3), custom_call_target="tpu_custom_call" | custom-call | flops 1308622848 | bytes 7500000 | tf_op jit(solution)/shard_map/momentum_part/pallas_call | solution.py:289
  129.7 6.0 %weight_part.1 = (bf16[512,1664]{1,0:T(8,128)(2,1)}, f32[1664,256]{1,0:T(8,128)}) custom-call(f32[16,8,256]{2,1,0:T(8,128)} %copy-done.4, bf16[512,1664]{1,0:T(8,128)(2,1)} %weight_ref.1, f32[512,256]{1,0:T(8,128)} %copy-done, f32[1664,256]{1,0:T(8,128)} %get-tuple-element.61.turned_ref, bf16[256,1664]{1,0:T(8,128)(2,1)} %get-tuple-element.62.high_ref, ...), custom_call_target="tpu_custom_call" | custom-call | flops 1308622848 | bytes 7500000 | tf_op jit(solution)/shard_map/weight_part/pallas_call | solution.py:327
  (46 shorter events, 9.7 us)
Async XLA Ops:
  5.8 33.0 %copy-start.1 = (bf16[512,1664]{1,0:T(8,128)(2,1)S(1)}, bf16[512,1664]{1,0:T(8,128)(2,1)}, u32[]{:S(2)}) copy-start(bf16[512,1664]{1,0:T(8,128)(2,1)} %m_ref.5) | copy-start | bytes 5111812
  24.9 13.2 %all-to-all-start.1 = ((f32[16,32,256]{2,1,0:T(8,128)}), f32[16,32,256]{2,1,0:T(8,128)S(1)}, u32[]{:S(2)}, u32[]{:S(2)}) async-start(f32[16,32,256]{2,1,0:T(8,128)} %broadcast_in_dim.6), calls=%async_computation.1 | async-start | bytes 1048576 | tf_op jit(solution)/shard_map/all_to_all | solution.py:350
  38.8 1.5 %copy-start.2 = (bf16[512,1664]{1,0:T(8,128)(2,1)S(1)}, bf16[512,1664]{1,0:T(8,128)(2,1)}, u32[]{:S(2)}) copy-start(bf16[512,1664]{1,0:T(8,128)(2,1)} %g_ref.5) | copy-start | bytes 5111812
  43.3 5.1 %collective-permute-start = (f32[128,1664]{1,0:T(8,128)}, f32[128,1664]{1,0:T(8,128)S(1)}, u32[]{:S(2)}, u32[]{:S(2)}) collective-permute-start(f32[128,1664]{1,0:T(8,128)} %get-tuple-element.37), channel_id=1, source_target_pairs={{0,16},{16,0},{32,48},{48,32},{64,80},{80,64},{96,112},{112,96},{1... | collective-permute-start | bytes 2555912 | tf_op jit(solution)/shard_map/ppermute | solution.py:397
  46.1 1.9 %collective-permute-start.1 = (f32[16,256]{1,0:T(8,128)S(1)}, f32[16,256]{1,0:T(8,128)S(1)}, u32[]{:S(2)}, u32[]{:S(2)}) collective-permute-start(f32[16,256]{1,0:T(8,128)S(1)} %fusion), channel_id=1, source_target_pairs={{0,16},{16,0},{32,48},{48,32},{64,80},{80,64},{96,112},{112,96},{1... | collective-permute-start | bytes 49160 | tf_op jit(solution)/shard_map/ppermute | solution.py:358
  48.5 8.7 %collective-permute-start.3 = (f32[16,1664]{1,0:T(8,128)S(1)}, f32[16,1664]{1,0:T(8,128)S(1)}, u32[]{:S(2)}, u32[]{:S(2)}) collective-permute-start(f32[16,1664]{1,0:T(8,128)S(1)} %get-tuple-element.73), channel_id=1, source_target_pairs={{0,32},{16,48},{32,64},{48,80},{64,96},{80,112},{96,128},{112,144}... | collective-permute-start | bytes 319496 | tf_op jit(solution)/shard_map/ppermute | solution.py:378
  50.2 7.0 %collective-permute-start.2 = (f32[16,1664]{1,0:T(8,128)S(1)}, f32[16,1664]{1,0:T(8,128)S(1)}, u32[]{:S(2)}, u32[]{:S(2)}) collective-permute-start(f32[16,1664]{1,0:T(8,128)S(1)} %get-tuple-element.74), channel_id=1, source_target_pairs={{0,224},{16,240},{32,0},{48,16},{64,32},{80,48},{96,64},{112,80},{... | collective-permute-start | bytes 319496 | tf_op jit(solution)/shard_map/ppermute | solution.py:377
  54.2 2.9 %collective-permute-start.4 = (f32[16,256]{1,0:T(8,128)S(1)}, f32[16,256]{1,0:T(8,128)S(1)}, u32[]{:S(2)}, u32[]{:S(2)}) collective-permute-start(f32[16,256]{1,0:T(8,128)S(1)} %add.117), channel_id=1, source_target_pairs={{0,32},{16,48},{32,0},{48,16},{64,96},{80,112},{96,64},{112,80},{1... | collective-permute-start | bytes 49160 | tf_op jit(solution)/shard_map/ppermute | solution.py:358
  57.2 6.0 %collective-permute-start.5 = (f32[16,1664]{1,0:T(8,128)S(1)}, f32[16,1664]{1,0:T(8,128)S(1)}, u32[]{:S(2)}, u32[]{:S(2)}) collective-permute-start(f32[16,1664]{1,0:T(8,128)S(1)} %get-tuple-element.41), channel_id=1, source_target_pairs={{0,224},{16,240},{32,0},{48,16},{64,32},{80,48},{96,64},{112,80},{... | collective-permute-start | bytes 319496 | tf_op jit(solution)/shard_map/ppermute | solution.py:377
  59.7 4.8 %collective-permute-start.6 = (f32[16,1664]{1,0:T(8,128)S(1)}, f32[16,1664]{1,0:T(8,128)S(1)}, u32[]{:S(2)}, u32[]{:S(2)}) collective-permute-start(f32[16,1664]{1,0:T(8,128)S(1)} %get-tuple-element.42), channel_id=1, source_target_pairs={{0,32},{16,48},{32,64},{48,80},{64,96},{80,112},{96,128},{112,144}... | collective-permute-start | bytes 319496 | tf_op jit(solution)/shard_map/ppermute | solution.py:378
  59.8 3.5 %collective-permute-start.7 = (f32[16,256]{1,0:T(8,128)S(1)}, f32[16,256]{1,0:T(8,128)S(1)}, u32[]{:S(2)}, u32[]{:S(2)}) collective-permute-start(f32[16,256]{1,0:T(8,128)S(1)} %add.132), channel_id=1, source_target_pairs={{0,64},{16,80},{32,96},{48,112},{64,0},{80,16},{96,32},{112,48},{1... | collective-permute-start | bytes 49160 | tf_op jit(solution)/shard_map/ppermute | solution.py:358
  64.5 7.2 %collective-permute-start.8 = (f32[16,1664]{1,0:T(8,128)S(1)}, f32[16,1664]{1,0:T(8,128)S(1)}, u32[]{:S(2)}, u32[]{:S(2)}) collective-permute-start(f32[16,1664]{1,0:T(8,128)S(1)} %get-tuple-element.44), channel_id=1, source_target_pairs={{0,224},{16,240},{32,0},{48,16},{64,32},{80,48},{96,64},{112,80},{... | collective-permute-start | bytes 319496 | tf_op jit(solution)/shard_map/ppermute | solution.py:377
  66.6 5.1 %collective-permute-start.9 = (f32[16,1664]{1,0:T(8,128)S(1)}, f32[16,1664]{1,0:T(8,128)S(1)}, u32[]{:S(2)}, u32[]{:S(2)}) collective-permute-start(f32[16,1664]{1,0:T(8,128)S(1)} %get-tuple-element.45), channel_id=1, source_target_pairs={{0,32},{16,48},{32,64},{48,80},{64,96},{80,112},{96,128},{112,144}... | collective-permute-start | bytes 319496 | tf_op jit(solution)/shard_map/ppermute | solution.py:378
  66.6 5.1 %collective-permute-start.10 = (f32[16,256]{1,0:T(8,128)S(1)}, f32[16,256]{1,0:T(8,128)S(1)}, u32[]{:S(2)}, u32[]{:S(2)}) collective-permute-start(f32[16,256]{1,0:T(8,128)S(1)} %add.141), channel_id=1, source_target_pairs={{0,224},{16,240},{32,192},{48,208},{64,160},{80,176},{96,128},{112... | collective-permute-start | bytes 49160 | tf_op jit(solution)/shard_map/ppermute | solution.py:358
  71.8 5.0 %collective-permute-start.14 = (f32[1,16,256]{2,1,0:T(8,128)S(1)}, f32[1,16,256]{2,1,0:T(8,128)S(1)}, u32[]{:S(2)}, u32[]{:S(2)}) collective-permute-start(f32[1,16,256]{2,1,0:T(8,128)S(1)} %bitcast.34), channel_id=1, source_target_pairs={{0,3},{1,2},{2,1},{3,0},{4,7},{5,6},{6,5},{7,4},{8,11},{9,10},{10,... | collective-permute-start | bytes 49160 | tf_op jit(solution)/shard_map/ppermute | solution.py:358
  72.0 4.8 %collective-permute-start.13 = (f32[1,16,256]{2,1,0:T(8,128)S(1)}, f32[1,16,256]{2,1,0:T(8,128)S(1)}, u32[]{:S(2)}, u32[]{:S(2)}) collective-permute-start(f32[1,16,256]{2,1,0:T(8,128)S(1)} %bitcast.35), channel_id=1, source_target_pairs={{0,2},{1,3},{2,0},{3,1},{4,6},{5,7},{6,4},{7,5},{8,10},{9,11},{10,... | collective-permute-start | bytes 49160 | tf_op jit(solution)/shard_map/ppermute | solution.py:358
  73.9 2.9 %collective-permute-start.12 = (f32[1,16,256]{2,1,0:T(8,128)S(1)}, f32[1,16,256]{2,1,0:T(8,128)S(1)}, u32[]{:S(2)}, u32[]{:S(2)}) collective-permute-start(f32[1,16,256]{2,1,0:T(8,128)S(1)} %bitcast.36), channel_id=1, source_target_pairs={{0,1},{1,0},{2,3},{3,2},{4,5},{5,4},{6,7},{7,6},{8,9},{9,8},{10,11... | collective-permute-start | bytes 49160 | tf_op jit(solution)/shard_map/ppermute | solution.py:358
  75.1 3.6 %collective-permute-start.11 = (f32[16,1664]{1,0:T(8,128)S(1)}, f32[16,1664]{1,0:T(8,128)S(1)}, u32[]{:S(2)}, u32[]{:S(2)}) collective-permute-start(f32[16,1664]{1,0:T(8,128)S(1)} %get-tuple-element.48), channel_id=1, source_target_pairs={{0,224},{16,240},{32,0},{48,16},{64,32},{80,48},{96,64},{112,80},{... | collective-permute-start | bytes 319496 | tf_op jit(solution)/shard_map/ppermute | solution.py:383
  79.7 25.0 %all-to-all-start.2 = ((f32[8,16,1664]{2,1,0:T(8,128)}), f32[8,16,1664]{2,1,0:T(8,128)S(1)}, u32[]{:S(2)}, u32[]{:S(2)}) async-start(f32[8,16,1664]{2,1,0:T(8,128)} %broadcast_in_dim.8), calls=%async_computation.2 | async-start | bytes 1703936 | tf_op jit(solution)/shard_map/all_to_all | solution.py:350
  84.4 4.3 %collective-permute-start.17 = (f32[4,16,256]{2,1,0:T(8,128)S(1)}, f32[4,16,256]{2,1,0:T(8,128)S(1)}, u32[]{:S(2)}, u32[]{:S(2)}) collective-permute-start(f32[4,16,256]{2,1,0:T(8,128)S(1)} %pad_maximum_fusion.1), channel_id=1, source_target_pairs={{0,12},{1,13},{2,14},{3,15},{4,8},{5,9},{6,10},{7,11},{8,4},{9,5},... | collective-permute-start | bytes 196616 | tf_op jit(solution)/shard_map/ppermute | solution.py:358
  85.0 4.6 %collective-permute-start.16 = (f32[4,16,256]{2,1,0:T(8,128)S(1)}, f32[4,16,256]{2,1,0:T(8,128)S(1)}, u32[]{:S(2)}, u32[]{:S(2)}) collective-permute-start(f32[4,16,256]{2,1,0:T(8,128)S(1)} %pad_maximum_fusion.1), channel_id=1, source_target_pairs={{0,8},{1,9},{2,10},{3,11},{4,12},{5,13},{6,14},{7,15},{8,0},{9,1},... | collective-permute-start | bytes 196616 | tf_op jit(solution)/shard_map/ppermute | solution.py:358
  85.7 4.3 %collective-permute-start.15 = (f32[4,16,256]{2,1,0:T(8,128)S(1)}, f32[4,16,256]{2,1,0:T(8,128)S(1)}, u32[]{:S(2)}, u32[]{:S(2)}) collective-permute-start(f32[4,16,256]{2,1,0:T(8,128)S(1)} %pad_maximum_fusion.1), channel_id=1, source_target_pairs={{0,4},{1,5},{2,6},{3,7},{4,0},{5,1},{6,2},{7,3},{8,12},{9,13},{10,... | collective-permute-start | bytes 196616 | tf_op jit(solution)/shard_map/ppermute | solution.py:358
  103.9 0.8 copy-start
  104.6 10.4 %collective-permute-start.18 = (f32[128,1664]{1,0:T(8,128)S(1)}, f32[128,1664]{1,0:T(8,128)S(1)}, u32[]{:S(2)}, u32[]{:S(2)}) collective-permute-start(f32[128,1664]{1,0:T(8,128)S(1)} %bitcast.27), channel_id=1, source_target_pairs={{0,16},{16,0},{32,48},{48,32},{64,80},{80,64},{96,112},{112,96},{1... | collective-permute-start | bytes 2555912 | tf_op jit(solution)/shard_map/ppermute | solution.py:405
  117.5 1.2 copy-start.3
  118.6 10.4 %all-to-all-start.3 = ((f32[16,8,256]{2,1,0:T(8,128)}), f32[16,8,256]{2,1,0:T(8,128)S(1)}, u32[]{:S(2)}, u32[]{:S(2)}) async-start(f32[16,8,256]{2,1,0:T(8,128)} %get-tuple-element.58), calls=%async_computation.3 | async-start | bytes 262144 | tf_op jit(solution)/shard_map/all_to_all | solution.py:350
  129.0 0.6 copy-start.4

commit v5 on v4

--- a/solution.py
+++ b/solution.py
@@ -105,7 +105,7 @@
     w_ref[...] = inverse_factor(gram[:HALF, :HALF] + jnp.where(rows == lanes, jitter, 0.0))
 
 
-def second_kernel(gram_ref, jitter_ref, first_ref, left_ref, w_ref, ortho_ref):
+def second_kernel(gram_ref, jitter_ref, first_ref, w_ref):
     first = first_ref[...]
     rows = lax.broadcasted_iota(jnp.int32, (HALF, HALF), 0)
     lanes = lax.broadcasted_iota(jnp.int32, (HALF, HALF), 1)
@@ -116,7 +116,6 @@
     w_ref[:HALF, HALF:] = jnp.zeros((HALF, HALF), jnp.float32)
     w_ref[HALF:, :HALF] = -dot_nn(second, dot_nn(low, first))
     w_ref[HALF:, HALF:] = second
-    ortho_ref[...] = dot_nt(left_ref[...], w_ref[...])
 
 
 def first_part(col, gather):
@@ -136,17 +135,14 @@
     )(col, gather)
 
 
-def second_part(jitter, first, gram, left):
+def second_part(jitter, first, gram):
     return pl.pallas_call(
         second_kernel,
-        out_shape=(
-            jax.ShapeDtypeStruct((RANK, RANK), jnp.float32),
-            jax.ShapeDtypeStruct(left.shape, jnp.float32),
-        ),
+        out_shape=jax.ShapeDtypeStruct((RANK, RANK), jnp.float32),
         compiler_params=params(24),
         cost_estimate=pl.CostEstimate(flops=6000000, bytes_accessed=24000000, transcendentals=0),
         name="second_factor",
-    )(gram, jitter, first, left)
+    )(gram, jitter, first)
 
 
 def halves(value):
@@ -263,7 +259,9 @@
     return total[:count] + total[count:] + product(ortho[:count], low_ref[:, start:stop])
 
 
-def momentum_kernel(m_ref, g_ref, ortho_ref, right_ref, out_ref, turned_ref, high_ref, low_ref):
+def momentum_kernel(
+    m_ref, g_ref, left_ref, w_ref, right_ref, out_ref, turned_ref, high_ref, low_ref, ortho_ref
+):
     columns = right_ref.shape[1]
 
     @pl.when(pl.program_id(0) == 0)
@@ -273,7 +271,9 @@
             high_ref[:, start : start + HALF], low_ref[:, start : start + HALF] = halves(block)
             turned_ref[start : start + HALF, :] = block.T
 
-    ortho = jnp.concatenate(halves(ortho_ref[...]), axis=0)
+    ortho = dot_nt(left_ref[...], w_ref[...])
+    ortho_ref[...] = ortho
+    ortho = jnp.concatenate(halves(ortho), axis=0)
     for start in range(0, columns, 256):
         stop = min(start + 256, columns)
         buffer = m_ref[:, start:stop].astype(jnp.float32) + g_ref[:, start:stop].astype(jnp.float32)
@@ -281,26 +281,28 @@
         out_ref[:, start:stop] = (buffer - (1.0 - decay) * update).astype(jnp.bfloat16)
 
 
-def momentum_part(momentum, gradient, ortho, right):
+def momentum_part(momentum, gradient, left, w, right):
     rows, columns = momentum.shape
     step = rows // 4
     block = pl.BlockSpec((step, columns), lambda i: (i, 0))
+    thin = pl.BlockSpec((step, RANK), lambda i: (i, 0))
     wide = pl.BlockSpec((RANK, columns), lambda i: (0, 0))
     return pl.pallas_call(
         momentum_kernel,
         grid=(4,),
-        in_specs=[block, block, pl.BlockSpec((step, RANK), lambda i: (i, 0)), wide],
-        out_specs=(block, pl.BlockSpec((columns, RANK), lambda i: (0, 0)), wide, wide),
+        in_specs=[block, block, thin, pl.BlockSpec((RANK, RANK), lambda i: (0, 0)), wide],
+        out_specs=(block, pl.BlockSpec((columns, RANK), lambda i: (0, 0)), wide, wide, thin),
         out_shape=(
             jax.ShapeDtypeStruct((rows, columns), jnp.bfloat16),
             jax.ShapeDtypeStruct((columns, RANK), jnp.float32),
             jax.ShapeDtypeStruct((RANK, columns), jnp.bfloat16),
             jax.ShapeDtypeStruct((RANK, columns), jnp.bfloat16),
+            jax.ShapeDtypeStruct((rows, RANK), jnp.float32),
         ),
         compiler_params=params(60),
         cost_estimate=pl.CostEstimate(flops=1308622848, bytes_accessed=7500000, transcendentals=0),
         name="momentum_part",
-    )(momentum, gradient, ortho, right)
+    )(momentum, gradient, left, w, right)
 
 
 def weight_kernel(squares_ref, weight_ref, ortho_ref, turned_ref, high_ref, low_ref, out_ref, factor_ref):
@@ -320,13 +322,13 @@
 
 def weight_part(squares, weight, ortho, turned, high, low):
     rows, columns = weight.shape
-    step = rows // 4
+    step = rows // 2
     block = pl.BlockSpec((step, columns), lambda i: (i, 0))
     wide = pl.BlockSpec((RANK, columns), lambda i: (0, 0))
-    factor = pl.BlockSpec((columns // 4, RANK), lambda i: (i, 0))
+    factor = pl.BlockSpec((columns // 2, RANK), lambda i: (i, 0))
     return pl.pallas_call(
         weight_kernel,
-        grid=(4,),
+        grid=(2,),
         in_specs=[
             pl.BlockSpec((16, 8, RANK), lambda i: (0, 0, 0)),
             block,
@@ -400,12 +402,14 @@
     gram = gather_near(gram, 4)
     mine = spread(mine, "row", 8, Z_GROUPS).reshape(HALF, 1664)
     jitter, first, gram = first_part(col.reshape(1), gram)
-    inverse, ortho = second_part(jitter, first, gram, left)
+    inverse = second_part(jitter, first, gram)
     mine, inverse = lax.optimization_barrier((mine, inverse))
     other = lax.ppermute(mine, "row", CORE_SWAP)
     right, squares = right_part(core, inverse, mine, other)
     squares = exchange(squares, "col")
-    new_momentum, turned, high, low = momentum_part(momentum, gradient, ortho, right)
+    new_momentum, turned, high, low, ortho = momentum_part(
+        momentum, gradient, left, inverse, right
+    )
     new_weight, new_factor = weight_part(squares, weight, ortho, turned, high, low)
     return (new_weight, new_momentum, new_factor)
 

time: 136 us -> 136 us (level)
    unnamed x10 -> x12, local copies, waits for them, and re-layouts: 4.07 us -> 3.3 us
  transfers between devices with their start and end apart: 22 -> 22, of which waited for: 13 -> 13; matrix products, arithmetic and copies ran while one was open for 0% -> 0% of each run, Pallas kernels for 15% -> 16%
where the time goes in v5:
time: 136 us; the launch traced here: 135 us
  starting transfers between devices  46.2 us (34%)
  Pallas kernels  37.2 us (27%)
  waiting for transfers between devices  26.6 us (20%)
  blocking collectives  18.2 us (13%)
  local copies, waits for them, and re-layouts  5.12 us (4%)
    all_to_all x1, blocking collectives, exchange(): return lax.all_to_all(pieces, axis, 0, 0, axis_index_groups=groups)  18.2 us
    all_to_all x3, starting transfers between devices, exchange(): return lax.all_to_all(pieces, axis, 0, 0, axis_index_groups=groups)  11.9 us
    ppermute x10, waiting for transfers between devices, swap(): return lax.ppermute(value, axis, [(i, i ^ bits) for i in range(16)])  11.5 us
    ppermute x10, starting transfers between devices, swap(): return lax.ppermute(value, axis, [(i, i ^ bits) for i in range(16)])  10.9 us
    all_to_all x3, waiting for transfers between devices, exchange(): return lax.all_to_all(pieces, axis, 0, 0, axis_index_groups=groups)  9.64 us
    ppermute x1, starting transfers between devices, local(): other = lax.ppermute(mine, 'row', CORE_SWAP)  8.65 us
    ppermute x3, starting transfers between devices, scatter_z(): down = lax.ppermute(down, 'row', z_shift(-1)) + own(k - 3)  8.6 us
    pallas_call x1, Pallas kernels, momentum_part(): pl.pallas_call(momentum_kernel, grid=(4,), in_specs=[block, block, thin,...  8.32 us
  transfers between devices with their start and end apart: 22, of which 13 were waited for; matrix products, arithmetic and copies ran while one was open for 0% of the time, Pallas kernels for 16%

profile of v5, /device:TPU:1, one launch (start us, length us, event | category | flops | bytes accessed | tf_op | source)
XLA Modules:
  0.0 135.2 jit_solution(4073376978831658317)
XLA Ops:
  0.6 5.2 %left_part.1 = f32[512,256]{1,0:T(8,128)} custom-call(bf16[512,1664]{1,0:T(8,128)(2,1)} %m_ref.5, bf16[512,1664]{1,0:T(8,128)(2,1)} %g_ref.5, f32[1664,256]{1,0:T(8,128)} %r_ref.1), custom_call_target="tpu_custom_call" | custom-call | flops 1744830464 | bytes 5600000 | tf_op jit(solution)/shard_map/left_part/pallas_call | solution.py:176
  5.8 18.2 %all_to_all.20 = f32[16,32,256]{2,1,0:T(8,128)S(1)} all-to-all(f32[16,32,256]{2,1,0:T(8,128)} %bitcast.33), channel_id=1, replica_groups=mesh['row'=16,'col'=16] {'col'}, dimensions={0} | all-to-all | bytes 1048576 | tf_op jit(solution)/shard_map/all_to_all | solution.py:352
  24.9 3.6 %all-to-all-start.1 = ((f32[16,32,256]{2,1,0:T(8,128)}), f32[16,32,256]{2,1,0:T(8,128)S(1)}, u32[]{:S(2)}, u32[]{:S(2)}) async-start(f32[16,32,256]{2,1,0:T(8,128)} %broadcast_in_dim.6), calls=%async_computation.1 | async-start | bytes 1048576 | tf_op jit(solution)/shard_map/all_to_all | solution.py:352
  28.5 9.6 %all-to-all-done.1 = f32[16,32,256]{2,1,0:T(8,128)S(1)} async-done(((f32[16,32,256]{2,1,0:T(8,128)}), f32[16,32,256]{2,1,0:T(8,128)S(1)}, u32[]{:S(2)}, u32[]{:S(2)}) %all-to-all-start.1) | async-done | bytes 524320 | tf_op jit(solution)/shard_map/all_to_all | solution.py:352
  38.8 1.5 %copy-done.2 = bf16[512,1664]{1,0:T(8,128)(2,1)S(1)} copy-done((bf16[512,1664]{1,0:T(8,128)(2,1)S(1)}, bf16[512,1664]{1,0:T(8,128)(2,1)}, u32[]{:S(2)}) %copy-start.2) | copy-done | bytes 1703960
  40.3 3.0 %cross_part.1 = (f32[128,1664]{1,0:T(8,128)S(1)}, f32[128,1664]{1,0:T(8,128)}) custom-call(s32[1]{0:T(128)} %bitcast.core_ref, f32[512,256]{1,0:T(8,128)S(1)} %bitcast.25, bf16[512,1664]{1,0:T(8,128)(2,1)S(1)} %copy-done.1, bf16[512,1664]{1,0:T(8,128)(2,1)S(1)} %copy-done.2), custom_call_target="tpu_custom_call" | custom-call | flops 1744830464 | bytes 5600000 | tf_op jit(solution)/shard_map/cross_part/pallas_call | solution.py:209
  43.3 2.8 %collective-permute-start = (f32[128,1664]{1,0:T(8,128)}, f32[128,1664]{1,0:T(8,128)S(1)}, u32[]{:S(2)}, u32[]{:S(2)}) collective-permute-start(f32[128,1664]{1,0:T(8,128)} %get-tuple-element.36), channel_id=1, source_target_pairs={{0,16},{16,0},{32,48},{48,32},{64,80},{80,64},{96,112},{112,96},{1... | collective-permute-start | bytes 2555912 | tf_op jit(solution)/shard_map/ppermute | solution.py:399
  46.1 1.9 %collective-permute-done.1 = f32[16,256]{1,0:T(8,128)S(1)} collective-permute-done((f32[16,256]{1,0:T(8,128)S(1)}, f32[16,256]{1,0:T(8,128)S(1)}, u32[]{:S(2)}, u32[]{:S(2)}) %collective-permute-start.1) | collective-permute-done | bytes 16416 | tf_op jit(solution)/shard_map/ppermute | solution.py:360
  48.5 1.7 %collective-permute-start.3 = (f32[16,1664]{1,0:T(8,128)S(1)}, f32[16,1664]{1,0:T(8,128)S(1)}, u32[]{:S(2)}, u32[]{:S(2)}) collective-permute-start(f32[16,1664]{1,0:T(8,128)S(1)} %get-tuple-element.71), channel_id=1, source_target_pairs={{0,32},{16,48},{32,64},{48,80},{64,96},{80,112},{96,128},{112,144}... | collective-permute-start | bytes 319496 | tf_op jit(solution)/shard_map/ppermute | solution.py:380
  50.2 4.0 %collective-permute-start.2 = (f32[16,1664]{1,0:T(8,128)S(1)}, f32[16,1664]{1,0:T(8,128)S(1)}, u32[]{:S(2)}, u32[]{:S(2)}) collective-permute-start(f32[16,1664]{1,0:T(8,128)S(1)} %get-tuple-element.72), channel_id=1, source_target_pairs={{0,224},{16,240},{32,0},{48,16},{64,32},{80,48},{96,64},{112,80},{... | collective-permute-start | bytes 319496 | tf_op jit(solution)/shard_map/ppermute | solution.py:379
  54.3 2.9 %collective-permute-done.4 = f32[16,256]{1,0:T(8,128)S(1)} collective-permute-done((f32[16,256]{1,0:T(8,128)S(1)}, f32[16,256]{1,0:T(8,128)S(1)}, u32[]{:S(2)}, u32[]{:S(2)}) %collective-permute-start.4) | collective-permute-done | bytes 16416 | tf_op jit(solution)/shard_map/ppermute | solution.py:360
  57.2 2.5 %collective-permute-start.5 = (f32[16,1664]{1,0:T(8,128)S(1)}, f32[16,1664]{1,0:T(8,128)S(1)}, u32[]{:S(2)}, u32[]{:S(2)}) collective-permute-start(f32[16,1664]{1,0:T(8,128)S(1)} %get-tuple-element.40), channel_id=1, source_target_pairs={{0,224},{16,240},{32,0},{48,16},{64,32},{80,48},{96,64},{112,80},{... | collective-permute-start | bytes 319496 | tf_op jit(solution)/shard_map/ppermute | solution.py:379
  59.8 1.6 %collective-permute-start.7 = (f32[16,256]{1,0:T(8,128)S(1)}, f32[16,256]{1,0:T(8,128)S(1)}, u32[]{:S(2)}, u32[]{:S(2)}) collective-permute-start(f32[16,256]{1,0:T(8,128)S(1)} %add.132), channel_id=1, source_target_pairs={{0,64},{16,80},{32,96},{48,112},{64,0},{80,16},{96,32},{112,48},{1... | collective-permute-start | bytes 49160 | tf_op jit(solution)/shard_map/ppermute | solution.py:360
  61.3 1.9 %collective-permute-done.7 = f32[16,256]{1,0:T(8,128)S(1)} collective-permute-done((f32[16,256]{1,0:T(8,128)S(1)}, f32[16,256]{1,0:T(8,128)S(1)}, u32[]{:S(2)}, u32[]{:S(2)}) %collective-permute-start.7) | collective-permute-done | bytes 16416 | tf_op jit(solution)/shard_map/ppermute | solution.py:360
  63.3 1.3 collective-permute-done.6
  64.6 2.1 %collective-permute-start.8 = (f32[16,1664]{1,0:T(8,128)S(1)}, f32[16,1664]{1,0:T(8,128)S(1)}, u32[]{:S(2)}, u32[]{:S(2)}) collective-permute-start(f32[16,1664]{1,0:T(8,128)S(1)} %get-tuple-element.43), channel_id=1, source_target_pairs={{0,224},{16,240},{32,0},{48,16},{64,32},{80,48},{96,64},{112,80},{... | collective-permute-start | bytes 319496 | tf_op jit(solution)/shard_map/ppermute | solution.py:379
  66.6 2.7 %collective-permute-start.10 = (f32[16,256]{1,0:T(8,128)S(1)}, f32[16,256]{1,0:T(8,128)S(1)}, u32[]{:S(2)}, u32[]{:S(2)}) collective-permute-start(f32[16,256]{1,0:T(8,128)S(1)} %add.141), channel_id=1, source_target_pairs={{0,224},{16,240},{32,192},{48,208},{64,160},{80,176},{96,128},{112... | collective-permute-start | bytes 49160 | tf_op jit(solution)/shard_map/ppermute | solution.py:360
  69.3 2.4 %collective-permute-done.10 = f32[16,256]{1,0:T(8,128)S(1)} collective-permute-done((f32[16,256]{1,0:T(8,128)S(1)}, f32[16,256]{1,0:T(8,128)S(1)}, u32[]{:S(2)}, u32[]{:S(2)}) %collective-permute-start.10) | collective-permute-done | bytes 16416 | tf_op jit(solution)/shard_map/ppermute | solution.py:360
  72.0 1.9 %collective-permute-start.13 = (f32[1,16,256]{2,1,0:T(8,128)S(1)}, f32[1,16,256]{2,1,0:T(8,128)S(1)}, u32[]{:S(2)}, u32[]{:S(2)}) collective-permute-start(f32[1,16,256]{2,1,0:T(8,128)S(1)} %bitcast.35), channel_id=1, source_target_pairs={{0,2},{1,3},{2,0},{3,1},{4,6},{5,7},{6,4},{7,5},{8,10},{9,11},{10,... | collective-permute-start | bytes 49160 | tf_op jit(solution)/shard_map/ppermute | solution.py:360
  75.1 1.7 %collective-permute-start.11 = (f32[16,1664]{1,0:T(8,128)S(1)}, f32[16,1664]{1,0:T(8,128)S(1)}, u32[]{:S(2)}, u32[]{:S(2)}) collective-permute-start(f32[16,1664]{1,0:T(8,128)S(1)} %get-tuple-element.47), channel_id=1, source_target_pairs={{0,224},{16,240},{32,0},{48,16},{64,32},{80,48},{96,64},{112,80},{... | collective-permute-start | bytes 319496 | tf_op jit(solution)/shard_map/ppermute | solution.py:385
  76.8 1.8 %collective-permute-done.11 = f32[16,1664]{1,0:T(8,128)S(1)} collective-permute-done((f32[16,1664]{1,0:T(8,128)S(1)}, f32[16,1664]{1,0:T(8,128)S(1)}, u32[]{:S(2)}, u32[]{:S(2)}) %collective-permute-start.11) | collective-permute-done | bytes 106528 | tf_op jit(solution)/shard_map/ppermute | solution.py:385
  79.7 4.8 %all-to-all-start.2 = ((f32[8,16,1664]{2,1,0:T(8,128)}), f32[8,16,1664]{2,1,0:T(8,128)S(1)}, u32[]{:S(2)}, u32[]{:S(2)}) async-start(f32[8,16,1664]{2,1,0:T(8,128)} %broadcast_in_dim.8), calls=%async_computation.2 | async-start | bytes 1703936 | tf_op jit(solution)/shard_map/all_to_all | solution.py:352
  85.7 2.0 %collective-permute-start.15 = (f32[4,16,256]{2,1,0:T(8,128)S(1)}, f32[4,16,256]{2,1,0:T(8,128)S(1)}, u32[]{:S(2)}, u32[]{:S(2)}) collective-permute-start(f32[4,16,256]{2,1,0:T(8,128)S(1)} %pad_maximum_fusion.1), channel_id=1, source_target_pairs={{0,4},{1,5},{2,6},{3,7},{4,0},{5,1},{6,2},{7,3},{8,12},{9,13},{10,... | collective-permute-start | bytes 196616 | tf_op jit(solution)/shard_map/ppermute | solution.py:360
  90.1 6.0 %first_factor.1 = (f32[8,128]{1,0:T(8,128)S(1)}, f32[128,128]{1,0:T(8,128)S(1)}, f32[256,256]{1,0:T(8,128)S(1)}) custom-call(s32[1]{0:T(128)} %bitcast.14.col_ref, f32[16,16,256]{2,1,0:T(8,128)S(1)} %pad_maximum_fusion.gather_ref), custom_call_target="tpu_custom_call" | custom-call | flops 6000000 | bytes 20000000 | tf_op jit(solution)/shard_map/first_factor/pallas_call | solution.py:123
  96.1 7.1 %second_factor.1.w_ref = f32[256,256]{1,0:T(8,128)S(1)} custom-call(f32[256,256]{1,0:T(8,128)S(1)} %get-tuple-element.51.gram_ref, f32[8,128]{1,0:T(8,128)S(1)} %get-tuple-element.52.jitter_ref, f32[128,128]{1,0:T(8,128)S(1)} %get-tuple-element.53.first_ref), custom_call_target="tpu_custom_call" | custom-call | flops 6000000 | bytes 24000000 | tf_op jit(solution)/shard_map/second_factor/pallas_call | solution.py:139
  103.2 8.7 %collective-permute-start.18 = (f32[128,1664]{1,0:T(8,128)S(1)}, f32[128,1664]{1,0:T(8,128)S(1)}, u32[]{:S(2)}, u32[]{:S(2)}) collective-permute-start(f32[128,1664]{1,0:T(8,128)S(1)} %bitcast.27), channel_id=1, source_target_pairs={{0,16},{16,0},{32,48},{48,32},{64,80},{80,64},{96,112},{112,96},{1... | collective-permute-start | bytes 2555912 | tf_op jit(solution)/shard_map/ppermute | solution.py:407
  111.9 2.0 %collective-permute-done.18.other_ref = f32[128,1664]{1,0:T(8,128)S(1)} collective-permute-done((f32[128,1664]{1,0:T(8,128)S(1)}, f32[128,1664]{1,0:T(8,128)S(1)}, u32[]{:S(2)}, u32[]{:S(2)}) %collective-permute-start.18) | collective-permute-done | bytes 852000 | tf_op jit(solution)/shard_map/ppermute | solution.py:407
  113.9 2.5 %right_part.1 = (f32[256,1664]{1,0:T(8,128)S(1)}, f32[16,8,256]{2,1,0:T(8,128)}) custom-call(s32[1]{0:T(128)} %bitcast.core_ref, f32[256,256]{1,0:T(8,128)S(1)} %second_factor.1.w_ref, f32[128,1664]{1,0:T(8,128)S(1)} %bitcast.28, f32[128,1664]{1,0:T(8,128)S(1)} %collective-permute-done.18.other_ref), custom_call_target="tpu_custom_call" | custom-call | flops 1300000000 | bytes 3400000 | tf_op jit(solution)/shard_map/right_part/pallas_call | solution.py:242
  116.3 1.2 copy-done.3
  117.5 3.5 %all-to-all-start.3 = ((f32[16,8,256]{2,1,0:T(8,128)}), f32[16,8,256]{2,1,0:T(8,128)S(1)}, u32[]{:S(2)}, u32[]{:S(2)}) async-start(f32[16,8,256]{2,1,0:T(8,128)} %get-tuple-element.56), calls=%async_computation.3 | async-start | bytes 262144 | tf_op jit(solution)/shard_map/all_to_all | solution.py:352
  121.0 8.3 %momentum_part.1 = (bf16[512,1664]{1,0:T(8,128)(2,1)}, f32[1664,256]{1,0:T(8,128)}, bf16[256,1664]{1,0:T(8,128)(2,1)}, bf16[256,1664]{1,0:T(8,128)(2,1)}, f32[512,256]{1,0:T(8,128)}) custom-call(bf16[512,1664]{1,0:T(8,128)(2,1)} %m_ref.5, bf16[512,1664]{1,0:T(8,128)(2,1)} %g_ref.5, f32[512,256]{1,0:T(8,128)} %bitcast.26, f32[256,256]{1,0:T(8,128)} %copy-done.4, ...), custom_call_target="tpu_custom_call" | custom-call | flops 1308622848 | bytes 7500000 | tf_op jit(solution)/shard_map/momentum_part/pallas_call | solution.py:290
  130.0 5.2 %weight_part.1 = (bf16[512,1664]{1,0:T(8,128)(2,1)}, f32[1664,256]{1,0:T(8,128)}) custom-call(f32[16,8,256]{2,1,0:T(8,128)} %copy-done.5, bf16[512,1664]{1,0:T(8,128)(2,1)} %weight_ref.1, f32[512,256]{1,0:T(8,128)} %get-tuple-element.58.ortho_ref, f32[1664,256]{1,0:T(8,128)} %get-tuple-element.59.turned_ref, bf16[256,1664]{1,0:T(8,128)(2,1)} %get-tuple-element.60.high_ref, ...), custom_call_target="tpu_custom_call" | custom-call | flops 1308622848 | bytes 7500000 | tf_op jit(solution)/shard_map/weight_part/pallas_call | solution.py:329
  (48 shorter events, 8.9 us)
Async XLA Ops:
  5.8 33.0 %copy-start.1 = (bf16[512,1664]{1,0:T(8,128)(2,1)S(1)}, bf16[512,1664]{1,0:T(8,128)(2,1)}, u32[]{:S(2)}) copy-start(bf16[512,1664]{1,0:T(8,128)(2,1)} %m_ref.5) | copy-start | bytes 5111812
  24.9 13.2 %all-to-all-start.1 = ((f32[16,32,256]{2,1,0:T(8,128)}), f32[16,32,256]{2,1,0:T(8,128)S(1)}, u32[]{:S(2)}, u32[]{:S(2)}) async-start(f32[16,32,256]{2,1,0:T(8,128)} %broadcast_in_dim.6), calls=%async_computation.1 | async-start | bytes 1048576 | tf_op jit(solution)/shard_map/all_to_all | solution.py:352
  38.1 5.2 %copy-start = (f32[16,32,256]{2,1,0:T(8,128)}, f32[16,32,256]{2,1,0:T(8,128)S(1)}, u32[]{:S(2)}) copy-start(f32[16,32,256]{2,1,0:T(8,128)S(1)} %all-to-all-done.1) | copy-start | bytes 1572868
  38.8 1.5 %copy-start.2 = (bf16[512,1664]{1,0:T(8,128)(2,1)S(1)}, bf16[512,1664]{1,0:T(8,128)(2,1)}, u32[]{:S(2)}) copy-start(bf16[512,1664]{1,0:T(8,128)(2,1)} %g_ref.5) | copy-start | bytes 5111812
  43.3 5.1 %collective-permute-start = (f32[128,1664]{1,0:T(8,128)}, f32[128,1664]{1,0:T(8,128)S(1)}, u32[]{:S(2)}, u32[]{:S(2)}) collective-permute-start(f32[128,1664]{1,0:T(8,128)} %get-tuple-element.36), channel_id=1, source_target_pairs={{0,16},{16,0},{32,48},{48,32},{64,80},{80,64},{96,112},{112,96},{1... | collective-permute-start | bytes 2555912 | tf_op jit(solution)/shard_map/ppermute | solution.py:399
  46.1 1.9 %collective-permute-start.1 = (f32[16,256]{1,0:T(8,128)S(1)}, f32[16,256]{1,0:T(8,128)S(1)}, u32[]{:S(2)}, u32[]{:S(2)}) collective-permute-start(f32[16,256]{1,0:T(8,128)S(1)} %fusion), channel_id=1, source_target_pairs={{0,16},{16,0},{32,48},{48,32},{64,80},{80,64},{96,112},{112,96},{1... | collective-permute-start | bytes 49160 | tf_op jit(solution)/shard_map/ppermute | solution.py:360
  48.5 8.7 %collective-permute-start.3 = (f32[16,1664]{1,0:T(8,128)S(1)}, f32[16,1664]{1,0:T(8,128)S(1)}, u32[]{:S(2)}, u32[]{:S(2)}) collective-permute-start(f32[16,1664]{1,0:T(8,128)S(1)} %get-tuple-element.71), channel_id=1, source_target_pairs={{0,32},{16,48},{32,64},{48,80},{64,96},{80,112},{96,128},{112,144}... | collective-permute-start | bytes 319496 | tf_op jit(solution)/shard_map/ppermute | solution.py:380
  50.2 7.0 %collective-permute-start.2 = (f32[16,1664]{1,0:T(8,128)S(1)}, f32[16,1664]{1,0:T(8,128)S(1)}, u32[]{:S(2)}, u32[]{:S(2)}) collective-permute-start(f32[16,1664]{1,0:T(8,128)S(1)} %get-tuple-element.72), channel_id=1, source_target_pairs={{0,224},{16,240},{32,0},{48,16},{64,32},{80,48},{96,64},{112,80},{... | collective-permute-start | bytes 319496 | tf_op jit(solution)/shard_map/ppermute | solution.py:379
  54.3 2.9 %collective-permute-start.4 = (f32[16,256]{1,0:T(8,128)S(1)}, f32[16,256]{1,0:T(8,128)S(1)}, u32[]{:S(2)}, u32[]{:S(2)}) collective-permute-start(f32[16,256]{1,0:T(8,128)S(1)} %add.117), channel_id=1, source_target_pairs={{0,32},{16,48},{32,0},{48,16},{64,96},{80,112},{96,64},{112,80},{1... | collective-permute-start | bytes 49160 | tf_op jit(solution)/shard_map/ppermute | solution.py:360
  57.2 6.0 %collective-permute-start.5 = (f32[16,1664]{1,0:T(8,128)S(1)}, f32[16,1664]{1,0:T(8,128)S(1)}, u32[]{:S(2)}, u32[]{:S(2)}) collective-permute-start(f32[16,1664]{1,0:T(8,128)S(1)} %get-tuple-element.40), channel_id=1, source_target_pairs={{0,224},{16,240},{32,0},{48,16},{64,32},{80,48},{96,64},{112,80},{... | collective-permute-start | bytes 319496 | tf_op jit(solution)/shard_map/ppermute | solution.py:379
  59.8 4.8 %collective-permute-start.6 = (f32[16,1664]{1,0:T(8,128)S(1)}, f32[16,1664]{1,0:T(8,128)S(1)}, u32[]{:S(2)}, u32[]{:S(2)}) collective-permute-start(f32[16,1664]{1,0:T(8,128)S(1)} %get-tuple-element.41), channel_id=1, source_target_pairs={{0,32},{16,48},{32,64},{48,80},{64,96},{80,112},{96,128},{112,144}... | collective-permute-start | bytes 319496 | tf_op jit(solution)/shard_map/ppermute | solution.py:380
  59.8 3.5 %collective-permute-start.7 = (f32[16,256]{1,0:T(8,128)S(1)}, f32[16,256]{1,0:T(8,128)S(1)}, u32[]{:S(2)}, u32[]{:S(2)}) collective-permute-start(f32[16,256]{1,0:T(8,128)S(1)} %add.132), channel_id=1, source_target_pairs={{0,64},{16,80},{32,96},{48,112},{64,0},{80,16},{96,32},{112,48},{1... | collective-permute-start | bytes 49160 | tf_op jit(solution)/shard_map/ppermute | solution.py:360
  64.6 7.2 %collective-permute-start.8 = (f32[16,1664]{1,0:T(8,128)S(1)}, f32[16,1664]{1,0:T(8,128)S(1)}, u32[]{:S(2)}, u32[]{:S(2)}) collective-permute-start(f32[16,1664]{1,0:T(8,128)S(1)} %get-tuple-element.43), channel_id=1, source_target_pairs={{0,224},{16,240},{32,0},{48,16},{64,32},{80,48},{96,64},{112,80},{... | collective-permute-start | bytes 319496 | tf_op jit(solution)/shard_map/ppermute | solution.py:379
  66.6 5.1 %collective-permute-start.9 = (f32[16,1664]{1,0:T(8,128)S(1)}, f32[16,1664]{1,0:T(8,128)S(1)}, u32[]{:S(2)}, u32[]{:S(2)}) collective-permute-start(f32[16,1664]{1,0:T(8,128)S(1)} %get-tuple-element.44), channel_id=1, source_target_pairs={{0,32},{16,48},{32,64},{48,80},{64,96},{80,112},{96,128},{112,144}... | collective-permute-start | bytes 319496 | tf_op jit(solution)/shard_map/ppermute | solution.py:380
  66.6 5.1 %collective-permute-start.10 = (f32[16,256]{1,0:T(8,128)S(1)}, f32[16,256]{1,0:T(8,128)S(1)}, u32[]{:S(2)}, u32[]{:S(2)}) collective-permute-start(f32[16,256]{1,0:T(8,128)S(1)} %add.141), channel_id=1, source_target_pairs={{0,224},{16,240},{32,192},{48,208},{64,160},{80,176},{96,128},{112... | collective-permute-start | bytes 49160 | tf_op jit(solution)/shard_map/ppermute | solution.py:360
  71.8 5.0 %collective-permute-start.14 = (f32[1,16,256]{2,1,0:T(8,128)S(1)}, f32[1,16,256]{2,1,0:T(8,128)S(1)}, u32[]{:S(2)}, u32[]{:S(2)}) collective-permute-start(f32[1,16,256]{2,1,0:T(8,128)S(1)} %bitcast.34), channel_id=1, source_target_pairs={{0,3},{1,2},{2,1},{3,0},{4,7},{5,6},{6,5},{7,4},{8,11},{9,10},{10,... | collective-permute-start | bytes 49160 | tf_op jit(solution)/shard_map/ppermute | solution.py:360
  72.0 4.8 %collective-permute-start.13 = (f32[1,16,256]{2,1,0:T(8,128)S(1)}, f32[1,16,256]{2,1,0:T(8,128)S(1)}, u32[]{:S(2)}, u32[]{:S(2)}) collective-permute-start(f32[1,16,256]{2,1,0:T(8,128)S(1)} %bitcast.35), channel_id=1, source_target_pairs={{0,2},{1,3},{2,0},{3,1},{4,6},{5,7},{6,4},{7,5},{8,10},{9,11},{10,... | collective-permute-start | bytes 49160 | tf_op jit(solution)/shard_map/ppermute | solution.py:360
  73.9 2.9 %collective-permute-start.12 = (f32[1,16,256]{2,1,0:T(8,128)S(1)}, f32[1,16,256]{2,1,0:T(8,128)S(1)}, u32[]{:S(2)}, u32[]{:S(2)}) collective-permute-start(f32[1,16,256]{2,1,0:T(8,128)S(1)} %bitcast.36), channel_id=1, source_target_pairs={{0,1},{1,0},{2,3},{3,2},{4,5},{5,4},{6,7},{7,6},{8,9},{9,8},{10,11... | collective-permute-start | bytes 49160 | tf_op jit(solution)/shard_map/ppermute | solution.py:360
  75.1 3.6 %collective-permute-start.11 = (f32[16,1664]{1,0:T(8,128)S(1)}, f32[16,1664]{1,0:T(8,128)S(1)}, u32[]{:S(2)}, u32[]{:S(2)}) collective-permute-start(f32[16,1664]{1,0:T(8,128)S(1)} %get-tuple-element.47), channel_id=1, source_target_pairs={{0,224},{16,240},{32,0},{48,16},{64,32},{80,48},{96,64},{112,80},{... | collective-permute-start | bytes 319496 | tf_op jit(solution)/shard_map/ppermute | solution.py:385
  79.7 23.6 %all-to-all-start.2 = ((f32[8,16,1664]{2,1,0:T(8,128)}), f32[8,16,1664]{2,1,0:T(8,128)S(1)}, u32[]{:S(2)}, u32[]{:S(2)}) async-start(f32[8,16,1664]{2,1,0:T(8,128)} %broadcast_in_dim.8), calls=%async_computation.2 | async-start | bytes 1703936 | tf_op jit(solution)/shard_map/all_to_all | solution.py:352
  84.5 4.3 %collective-permute-start.17 = (f32[4,16,256]{2,1,0:T(8,128)S(1)}, f32[4,16,256]{2,1,0:T(8,128)S(1)}, u32[]{:S(2)}, u32[]{:S(2)}) collective-permute-start(f32[4,16,256]{2,1,0:T(8,128)S(1)} %pad_maximum_fusion.1), channel_id=1, source_target_pairs={{0,12},{1,13},{2,14},{3,15},{4,8},{5,9},{6,10},{7,11},{8,4},{9,5},... | collective-permute-start | bytes 196616 | tf_op jit(solution)/shard_map/ppermute | solution.py:360
  85.0 4.6 %collective-permute-start.16 = (f32[4,16,256]{2,1,0:T(8,128)S(1)}, f32[4,16,256]{2,1,0:T(8,128)S(1)}, u32[]{:S(2)}, u32[]{:S(2)}) collective-permute-start(f32[4,16,256]{2,1,0:T(8,128)S(1)} %pad_maximum_fusion.1), channel_id=1, source_target_pairs={{0,8},{1,9},{2,10},{3,11},{4,12},{5,13},{6,14},{7,15},{8,0},{9,1},... | collective-permute-start | bytes 196616 | tf_op jit(solution)/shard_map/ppermute | solution.py:360
  85.7 4.3 %collective-permute-start.15 = (f32[4,16,256]{2,1,0:T(8,128)S(1)}, f32[4,16,256]{2,1,0:T(8,128)S(1)}, u32[]{:S(2)}, u32[]{:S(2)}) collective-permute-start(f32[4,16,256]{2,1,0:T(8,128)S(1)} %pad_maximum_fusion.1), channel_id=1, source_target_pairs={{0,4},{1,5},{2,6},{3,7},{4,0},{5,1},{6,2},{7,3},{8,12},{9,13},{10,... | collective-permute-start | bytes 196616 | tf_op jit(solution)/shard_map/ppermute | solution.py:360
  103.2 13.1 %copy-start.4 = (f32[256,256]{1,0:T(8,128)}, f32[256,256]{1,0:T(8,128)S(1)}, u32[]{:S(2)}) copy-start(f32[256,256]{1,0:T(8,128)S(1)} %second_factor.1.w_ref) | copy-start | bytes 786436
  103.2 10.7 %collective-permute-start.18 = (f32[128,1664]{1,0:T(8,128)S(1)}, f32[128,1664]{1,0:T(8,128)S(1)}, u32[]{:S(2)}, u32[]{:S(2)}) collective-permute-start(f32[128,1664]{1,0:T(8,128)S(1)} %bitcast.27), channel_id=1, source_target_pairs={{0,16},{16,0},{32,48},{48,32},{64,80},{80,64},{96,112},{112,96},{1... | collective-permute-start | bytes 2555912 | tf_op jit(solution)/shard_map/ppermute | solution.py:407
  116.3 1.2 copy-start.3
  117.5 11.8 %all-to-all-start.3 = ((f32[16,8,256]{2,1,0:T(8,128)}), f32[16,8,256]{2,1,0:T(8,128)S(1)}, u32[]{:S(2)}, u32[]{:S(2)}) async-start(f32[16,8,256]{2,1,0:T(8,128)} %get-tuple-element.56), calls=%async_computation.3 | async-start | bytes 262144 | tf_op jit(solution)/shard_map/all_to_all | solution.py:352
  129.4 0.6 copy-start.5

commit v6 on v5

--- a/solution.py
+++ b/solution.py
@@ -283,13 +283,13 @@
 
 def momentum_part(momentum, gradient, left, w, right):
     rows, columns = momentum.shape
-    step = rows // 4
+    step = rows // 2
     block = pl.BlockSpec((step, columns), lambda i: (i, 0))
     thin = pl.BlockSpec((step, RANK), lambda i: (i, 0))
     wide = pl.BlockSpec((RANK, columns), lambda i: (0, 0))
     return pl.pallas_call(
         momentum_kernel,
-        grid=(4,),
+        grid=(2,),
         in_specs=[block, block, thin, pl.BlockSpec((RANK, RANK), lambda i: (0, 0)), wide],
         out_specs=(block, pl.BlockSpec((columns, RANK), lambda i: (0, 0)), wide, wide, thin),
         out_shape=(

time: 136 us -> 134 us (0.985)
  transfers between devices with their start and end apart: 22 -> 22, of which waited for: 13 -> 13; matrix products, arithmetic and copies ran while one was open for 0% -> 0% of each run, Pallas kernels for 16% -> 15%
where the time goes in v6:
time: 134 us
  starting transfers between devices  46.2 us (34%)
  Pallas kernels  36 us (27%)
  waiting for transfers between devices  26.6 us (20%)
  blocking collectives  18.2 us (14%)
  local copies, waits for them, and re-layouts  5.12 us (4%)
    all_to_all x1, blocking collectives, exchange(): return lax.all_to_all(pieces, axis, 0, 0, axis_index_groups=groups)  18.2 us
    all_to_all x3, starting transfers between devices, exchange(): return lax.all_to_all(pieces, axis, 0, 0, axis_index_groups=groups)  11.9 us
    ppermute x10, waiting for transfers between devices, swap(): return lax.ppermute(value, axis, [(i, i ^ bits) for i in range(16)])  11.5 us
    ppermute x10, starting transfers between devices, swap(): return lax.ppermute(value, axis, [(i, i ^ bits) for i in range(16)])  10.9 us
    all_to_all x3, waiting for transfers between devices, exchange(): return lax.all_to_all(pieces, axis, 0, 0, axis_index_groups=groups)  9.64 us
    ppermute x1, starting transfers between devices, local(): other = lax.ppermute(mine, 'row', CORE_SWAP)  8.65 us
    ppermute x3, starting transfers between devices, scatter_z(): down = lax.ppermute(down, 'row', z_shift(-1)) + own(k - 3)  8.6 us
    pallas_call x1, Pallas kernels, second_part(): pl.pallas_call(second_kernel, out_shape=jax.ShapeDtypeStruct((RANK, RANK)...  7.11 us
  transfers between devices with their start and end apart: 22, of which 13 were waited for; matrix products, arithmetic and copies ran while one was open for 0% of the time, Pallas kernels for 15%

profile of v6, /device:TPU:1, one launch (start us, length us, event | category | flops | bytes accessed | tf_op | source)
XLA Modules:
  0.0 133.9 jit_solution(16721932320019381893)
XLA Ops:
  0.6 5.2 %left_part.1 = f32[512,256]{1,0:T(8,128)} custom-call(bf16[512,1664]{1,0:T(8,128)(2,1)} %m_ref.5, bf16[512,1664]{1,0:T(8,128)(2,1)} %g_ref.5, f32[1664,256]{1,0:T(8,128)} %r_ref.1), custom_call_target="tpu_custom_call" | custom-call | flops 1744830464 | bytes 5600000 | tf_op jit(solution)/shard_map/left_part/pallas_call | solution.py:176
  5.8 18.2 %all_to_all.20 = f32[16,32,256]{2,1,0:T(8,128)S(1)} all-to-all(f32[16,32,256]{2,1,0:T(8,128)} %bitcast.33), channel_id=1, replica_groups=mesh['row'=16,'col'=16] {'col'}, dimensions={0} | all-to-all | bytes 1048576 | tf_op jit(solution)/shard_map/all_to_all | solution.py:352
  24.9 3.6 %all-to-all-start.1 = ((f32[16,32,256]{2,1,0:T(8,128)}), f32[16,32,256]{2,1,0:T(8,128)S(1)}, u32[]{:S(2)}, u32[]{:S(2)}) async-start(f32[16,32,256]{2,1,0:T(8,128)} %broadcast_in_dim.6), calls=%async_computation.1 | async-start | bytes 1048576 | tf_op jit(solution)/shard_map/all_to_all | solution.py:352
  28.5 9.6 %all-to-all-done.1 = f32[16,32,256]{2,1,0:T(8,128)S(1)} async-done(((f32[16,32,256]{2,1,0:T(8,128)}), f32[16,32,256]{2,1,0:T(8,128)S(1)}, u32[]{:S(2)}, u32[]{:S(2)}) %all-to-all-start.1) | async-done | bytes 524320 | tf_op jit(solution)/shard_map/all_to_all | solution.py:352
  38.8 1.5 %copy-done.2 = bf16[512,1664]{1,0:T(8,128)(2,1)S(1)} copy-done((bf16[512,1664]{1,0:T(8,128)(2,1)S(1)}, bf16[512,1664]{1,0:T(8,128)(2,1)}, u32[]{:S(2)}) %copy-start.2) | copy-done | bytes 1703960
  40.3 3.0 %cross_part.1 = (f32[128,1664]{1,0:T(8,128)S(1)}, f32[128,1664]{1,0:T(8,128)}) custom-call(s32[1]{0:T(128)} %bitcast.core_ref, f32[512,256]{1,0:T(8,128)S(1)} %bitcast.25, bf16[512,1664]{1,0:T(8,128)(2,1)S(1)} %copy-done.1, bf16[512,1664]{1,0:T(8,128)(2,1)S(1)} %copy-done.2), custom_call_target="tpu_custom_call" | custom-call | flops 1744830464 | bytes 5600000 | tf_op jit(solution)/shard_map/cross_part/pallas_call | solution.py:209
  43.3 2.8 %collective-permute-start = (f32[128,1664]{1,0:T(8,128)}, f32[128,1664]{1,0:T(8,128)S(1)}, u32[]{:S(2)}, u32[]{:S(2)}) collective-permute-start(f32[128,1664]{1,0:T(8,128)} %get-tuple-element.36), channel_id=1, source_target_pairs={{0,16},{16,0},{32,48},{48,32},{64,80},{80,64},{96,112},{112,96},{1... | collective-permute-start | bytes 2555912 | tf_op jit(solution)/shard_map/ppermute | solution.py:399
  46.1 1.9 %collective-permute-done.1 = f32[16,256]{1,0:T(8,128)S(1)} collective-permute-done((f32[16,256]{1,0:T(8,128)S(1)}, f32[16,256]{1,0:T(8,128)S(1)}, u32[]{:S(2)}, u32[]{:S(2)}) %collective-permute-start.1) | collective-permute-done | bytes 16416 | tf_op jit(solution)/shard_map/ppermute | solution.py:360
  48.5 1.7 %collective-permute-start.3 = (f32[16,1664]{1,0:T(8,128)S(1)}, f32[16,1664]{1,0:T(8,128)S(1)}, u32[]{:S(2)}, u32[]{:S(2)}) collective-permute-start(f32[16,1664]{1,0:T(8,128)S(1)} %get-tuple-element.71), channel_id=1, source_target_pairs={{0,32},{16,48},{32,64},{48,80},{64,96},{80,112},{96,128},{112,144}... | collective-permute-start | bytes 319496 | tf_op jit(solution)/shard_map/ppermute | solution.py:380
  50.2 4.0 %collective-permute-start.2 = (f32[16,1664]{1,0:T(8,128)S(1)}, f32[16,1664]{1,0:T(8,128)S(1)}, u32[]{:S(2)}, u32[]{:S(2)}) collective-permute-start(f32[16,1664]{1,0:T(8,128)S(1)} %get-tuple-element.72), channel_id=1, source_target_pairs={{0,224},{16,240},{32,0},{48,16},{64,32},{80,48},{96,64},{112,80},{... | collective-permute-start | bytes 319496 | tf_op jit(solution)/shard_map/ppermute | solution.py:379
  54.3 2.9 %collective-permute-done.4 = f32[16,256]{1,0:T(8,128)S(1)} collective-permute-done((f32[16,256]{1,0:T(8,128)S(1)}, f32[16,256]{1,0:T(8,128)S(1)}, u32[]{:S(2)}, u32[]{:S(2)}) %collective-permute-start.4) | collective-permute-done | bytes 16416 | tf_op jit(solution)/shard_map/ppermute | solution.py:360
  57.2 2.5 %collective-permute-start.5 = (f32[16,1664]{1,0:T(8,128)S(1)}, f32[16,1664]{1,0:T(8,128)S(1)}, u32[]{:S(2)}, u32[]{:S(2)}) collective-permute-start(f32[16,1664]{1,0:T(8,128)S(1)} %get-tuple-element.40), channel_id=1, source_target_pairs={{0,224},{16,240},{32,0},{48,16},{64,32},{80,48},{96,64},{112,80},{... | collective-permute-start | bytes 319496 | tf_op jit(solution)/shard_map/ppermute | solution.py:379
  59.8 1.6 %collective-permute-start.7 = (f32[16,256]{1,0:T(8,128)S(1)}, f32[16,256]{1,0:T(8,128)S(1)}, u32[]{:S(2)}, u32[]{:S(2)}) collective-permute-start(f32[16,256]{1,0:T(8,128)S(1)} %add.132), channel_id=1, source_target_pairs={{0,64},{16,80},{32,96},{48,112},{64,0},{80,16},{96,32},{112,48},{1... | collective-permute-start | bytes 49160 | tf_op jit(solution)/shard_map/ppermute | solution.py:360
  61.3 1.9 %collective-permute-done.7 = f32[16,256]{1,0:T(8,128)S(1)} collective-permute-done((f32[16,256]{1,0:T(8,128)S(1)}, f32[16,256]{1,0:T(8,128)S(1)}, u32[]{:S(2)}, u32[]{:S(2)}) %collective-permute-start.7) | collective-permute-done | bytes 16416 | tf_op jit(solution)/shard_map/ppermute | solution.py:360
  63.3 1.3 collective-permute-done.6
  64.6 2.1 %collective-permute-start.8 = (f32[16,1664]{1,0:T(8,128)S(1)}, f32[16,1664]{1,0:T(8,128)S(1)}, u32[]{:S(2)}, u32[]{:S(2)}) collective-permute-start(f32[16,1664]{1,0:T(8,128)S(1)} %get-tuple-element.43), channel_id=1, source_target_pairs={{0,224},{16,240},{32,0},{48,16},{64,32},{80,48},{96,64},{112,80},{... | collective-permute-start | bytes 319496 | tf_op jit(solution)/shard_map/ppermute | solution.py:379
  66.6 2.7 %collective-permute-start.10 = (f32[16,256]{1,0:T(8,128)S(1)}, f32[16,256]{1,0:T(8,128)S(1)}, u32[]{:S(2)}, u32[]{:S(2)}) collective-permute-start(f32[16,256]{1,0:T(8,128)S(1)} %add.141), channel_id=1, source_target_pairs={{0,224},{16,240},{32,192},{48,208},{64,160},{80,176},{96,128},{112... | collective-permute-start | bytes 49160 | tf_op jit(solution)/shard_map/ppermute | solution.py:360
  69.3 2.4 %collective-permute-done.10 = f32[16,256]{1,0:T(8,128)S(1)} collective-permute-done((f32[16,256]{1,0:T(8,128)S(1)}, f32[16,256]{1,0:T(8,128)S(1)}, u32[]{:S(2)}, u32[]{:S(2)}) %collective-permute-start.10) | collective-permute-done | bytes 16416 | tf_op jit(solution)/shard_map/ppermute | solution.py:360
  72.0 1.9 %collective-permute-start.13 = (f32[1,16,256]{2,1,0:T(8,128)S(1)}, f32[1,16,256]{2,1,0:T(8,128)S(1)}, u32[]{:S(2)}, u32[]{:S(2)}) collective-permute-start(f32[1,16,256]{2,1,0:T(8,128)S(1)} %bitcast.35), channel_id=1, source_target_pairs={{0,2},{1,3},{2,0},{3,1},{4,6},{5,7},{6,4},{7,5},{8,10},{9,11},{10,... | collective-permute-start | bytes 49160 | tf_op jit(solution)/shard_map/ppermute | solution.py:360
  75.1 1.7 %collective-permute-start.11 = (f32[16,1664]{1,0:T(8,128)S(1)}, f32[16,1664]{1,0:T(8,128)S(1)}, u32[]{:S(2)}, u32[]{:S(2)}) collective-permute-start(f32[16,1664]{1,0:T(8,128)S(1)} %get-tuple-element.47), channel_id=1, source_target_pairs={{0,224},{16,240},{32,0},{48,16},{64,32},{80,48},{96,64},{112,80},{... | collective-permute-start | bytes 319496 | tf_op jit(solution)/shard_map/ppermute | solution.py:385
  76.8 1.8 %collective-permute-done.11 = f32[16,1664]{1,0:T(8,128)S(1)} collective-permute-done((f32[16,1664]{1,0:T(8,128)S(1)}, f32[16,1664]{1,0:T(8,128)S(1)}, u32[]{:S(2)}, u32[]{:S(2)}) %collective-permute-start.11) | collective-permute-done | bytes 106528 | tf_op jit(solution)/shard_map/ppermute | solution.py:385
  79.7 4.8 %all-to-all-start.2 = ((f32[8,16,1664]{2,1,0:T(8,128)}), f32[8,16,1664]{2,1,0:T(8,128)S(1)}, u32[]{:S(2)}, u32[]{:S(2)}) async-start(f32[8,16,1664]{2,1,0:T(8,128)} %broadcast_in_dim.8), calls=%async_computation.2 | async-start | bytes 1703936 | tf_op jit(solution)/shard_map/all_to_all | solution.py:352
  85.7 2.0 %collective-permute-start.15 = (f32[4,16,256]{2,1,0:T(8,128)S(1)}, f32[4,16,256]{2,1,0:T(8,128)S(1)}, u32[]{:S(2)}, u32[]{:S(2)}) collective-permute-start(f32[4,16,256]{2,1,0:T(8,128)S(1)} %pad_maximum_fusion.1), channel_id=1, source_target_pairs={{0,4},{1,5},{2,6},{3,7},{4,0},{5,1},{6,2},{7,3},{8,12},{9,13},{10,... | collective-permute-start | bytes 196616 | tf_op jit(solution)/shard_map/ppermute | solution.py:360
  90.1 6.0 %first_factor.1 = (f32[8,128]{1,0:T(8,128)S(1)}, f32[128,128]{1,0:T(8,128)S(1)}, f32[256,256]{1,0:T(8,128)S(1)}) custom-call(s32[1]{0:T(128)} %bitcast.14.col_ref, f32[16,16,256]{2,1,0:T(8,128)S(1)} %pad_maximum_fusion.gather_ref), custom_call_target="tpu_custom_call" | custom-call | flops 6000000 | bytes 20000000 | tf_op jit(solution)/shard_map/first_factor/pallas_call | solution.py:123
  96.1 7.1 %second_factor.1.w_ref = f32[256,256]{1,0:T(8,128)S(1)} custom-call(f32[256,256]{1,0:T(8,128)S(1)} %get-tuple-element.51.gram_ref, f32[8,128]{1,0:T(8,128)S(1)} %get-tuple-element.52.jitter_ref, f32[128,128]{1,0:T(8,128)S(1)} %get-tuple-element.53.first_ref), custom_call_target="tpu_custom_call" | custom-call | flops 6000000 | bytes 24000000 | tf_op jit(solution)/shard_map/second_factor/pallas_call | solution.py:139
  103.2 8.7 %collective-permute-start.18 = (f32[128,1664]{1,0:T(8,128)S(1)}, f32[128,1664]{1,0:T(8,128)S(1)}, u32[]{:S(2)}, u32[]{:S(2)}) collective-permute-start(f32[128,1664]{1,0:T(8,128)S(1)} %bitcast.27), channel_id=1, source_target_pairs={{0,16},{16,0},{32,48},{48,32},{64,80},{80,64},{96,112},{112,96},{1... | collective-permute-start | bytes 2555912 | tf_op jit(solution)/shard_map/ppermute | solution.py:407
  111.9 2.0 %collective-permute-done.18.other_ref = f32[128,1664]{1,0:T(8,128)S(1)} collective-permute-done((f32[128,1664]{1,0:T(8,128)S(1)}, f32[128,1664]{1,0:T(8,128)S(1)}, u32[]{:S(2)}, u32[]{:S(2)}) %collective-permute-start.18) | collective-permute-done | bytes 852000 | tf_op jit(solution)/shard_map/ppermute | solution.py:407
  113.9 2.5 %right_part.1 = (f32[256,1664]{1,0:T(8,128)S(1)}, f32[16,8,256]{2,1,0:T(8,128)}) custom-call(s32[1]{0:T(128)} %bitcast.core_ref, f32[256,256]{1,0:T(8,128)S(1)} %second_factor.1.w_ref, f32[128,1664]{1,0:T(8,128)S(1)} %bitcast.28, f32[128,1664]{1,0:T(8,128)S(1)} %collective-permute-done.18.other_ref), custom_call_target="tpu_custom_call" | custom-call | flops 1300000000 | bytes 3400000 | tf_op jit(solution)/shard_map/right_part/pallas_call | solution.py:242
  116.3 1.2 copy-done.3
  117.5 3.5 %all-to-all-start.3 = ((f32[16,8,256]{2,1,0:T(8,128)}), f32[16,8,256]{2,1,0:T(8,128)S(1)}, u32[]{:S(2)}, u32[]{:S(2)}) async-start(f32[16,8,256]{2,1,0:T(8,128)} %get-tuple-element.56), calls=%async_computation.3 | async-start | bytes 262144 | tf_op jit(solution)/shard_map/all_to_all | solution.py:352
  121.0 7.1 %momentum_part.1 = (bf16[512,1664]{1,0:T(8,128)(2,1)}, f32[1664,256]{1,0:T(8,128)}, bf16[256,1664]{1,0:T(8,128)(2,1)}, bf16[256,1664]{1,0:T(8,128)(2,1)}, f32[512,256]{1,0:T(8,128)}) custom-call(bf16[512,1664]{1,0:T(8,128)(2,1)} %m_ref.5, bf16[512,1664]{1,0:T(8,128)(2,1)} %g_ref.5, f32[512,256]{1,0:T(8,128)} %bitcast.26, f32[256,256]{1,0:T(8,128)} %copy-done.4, ...), custom_call_target="tpu_custom_call" | custom-call | flops 1308622848 | bytes 7500000 | tf_op jit(solution)/shard_map/momentum_part/pallas_call | solution.py:290
  128.8 5.2 %weight_part.1 = (bf16[512,1664]{1,0:T(8,128)(2,1)}, f32[1664,256]{1,0:T(8,128)}) custom-call(f32[16,8,256]{2,1,0:T(8,128)} %copy-done.5, bf16[512,1664]{1,0:T(8,128)(2,1)} %weight_ref.1, f32[512,256]{1,0:T(8,128)} %get-tuple-element.58.ortho_ref, f32[1664,256]{1,0:T(8,128)} %get-tuple-element.59.turned_ref, bf16[256,1664]{1,0:T(8,128)(2,1)} %get-tuple-element.60.high_ref, ...), custom_call_target="tpu_custom_call" | custom-call | flops 1308622848 | bytes 7500000 | tf_op jit(solution)/shard_map/weight_part/pallas_call | solution.py:329
  (48 shorter events, 8.9 us)
Async XLA Ops:
  5.8 33.0 %copy-start.1 = (bf16[512,1664]{1,0:T(8,128)(2,1)S(1)}, bf16[512,1664]{1,0:T(8,128)(2,1)}, u32[]{:S(2)}) copy-start(bf16[512,1664]{1,0:T(8,128)(2,1)} %m_ref.5) | copy-start | bytes 5111812
  24.9 13.2 %all-to-all-start.1 = ((f32[16,32,256]{2,1,0:T(8,128)}), f32[16,32,256]{2,1,0:T(8,128)S(1)}, u32[]{:S(2)}, u32[]{:S(2)}) async-start(f32[16,32,256]{2,1,0:T(8,128)} %broadcast_in_dim.6), calls=%async_computation.1 | async-start | bytes 1048576 | tf_op jit(solution)/shard_map/all_to_all | solution.py:352
  38.1 5.2 %copy-start = (f32[16,32,256]{2,1,0:T(8,128)}, f32[16,32,256]{2,1,0:T(8,128)S(1)}, u32[]{:S(2)}) copy-start(f32[16,32,256]{2,1,0:T(8,128)S(1)} %all-to-all-done.1) | copy-start | bytes 1572868
  38.8 1.5 %copy-start.2 = (bf16[512,1664]{1,0:T(8,128)(2,1)S(1)}, bf16[512,1664]{1,0:T(8,128)(2,1)}, u32[]{:S(2)}) copy-start(bf16[512,1664]{1,0:T(8,128)(2,1)} %g_ref.5) | copy-start | bytes 5111812
  43.3 5.1 %collective-permute-start = (f32[128,1664]{1,0:T(8,128)}, f32[128,1664]{1,0:T(8,128)S(1)}, u32[]{:S(2)}, u32[]{:S(2)}) collective-permute-start(f32[128,1664]{1,0:T(8,128)} %get-tuple-element.36), channel_id=1, source_target_pairs={{0,16},{16,0},{32,48},{48,32},{64,80},{80,64},{96,112},{112,96},{1... | collective-permute-start | bytes 2555912 | tf_op jit(solution)/shard_map/ppermute | solution.py:399
  46.1 1.9 %collective-permute-start.1 = (f32[16,256]{1,0:T(8,128)S(1)}, f32[16,256]{1,0:T(8,128)S(1)}, u32[]{:S(2)}, u32[]{:S(2)}) collective-permute-start(f32[16,256]{1,0:T(8,128)S(1)} %fusion), channel_id=1, source_target_pairs={{0,16},{16,0},{32,48},{48,32},{64,80},{80,64},{96,112},{112,96},{1... | collective-permute-start | bytes 49160 | tf_op jit(solution)/shard_map/ppermute | solution.py:360
  48.5 8.7 %collective-permute-start.3 = (f32[16,1664]{1,0:T(8,128)S(1)}, f32[16,1664]{1,0:T(8,128)S(1)}, u32[]{:S(2)}, u32[]{:S(2)}) collective-permute-start(f32[16,1664]{1,0:T(8,128)S(1)} %get-tuple-element.71), channel_id=1, source_target_pairs={{0,32},{16,48},{32,64},{48,80},{64,96},{80,112},{96,128},{112,144}... | collective-permute-start | bytes 319496 | tf_op jit(solution)/shard_map/ppermute | solution.py:380
  50.2 7.0 %collective-permute-start.2 = (f32[16,1664]{1,0:T(8,128)S(1)}, f32[16,1664]{1,0:T(8,128)S(1)}, u32[]{:S(2)}, u32[]{:S(2)}) collective-permute-start(f32[16,1664]{1,0:T(8,128)S(1)} %get-tuple-element.72), channel_id=1, source_target_pairs={{0,224},{16,240},{32,0},{48,16},{64,32},{80,48},{96,64},{112,80},{... | collective-permute-start | bytes 319496 | tf_op jit(solution)/shard_map/ppermute | solution.py:379
  54.3 2.9 %collective-permute-start.4 = (f32[16,256]{1,0:T(8,128)S(1)}, f32[16,256]{1,0:T(8,128)S(1)}, u32[]{:S(2)}, u32[]{:S(2)}) collective-permute-start(f32[16,256]{1,0:T(8,128)S(1)} %add.117), channel_id=1, source_target_pairs={{0,32},{16,48},{32,0},{48,16},{64,96},{80,112},{96,64},{112,80},{1... | collective-permute-start | bytes 49160 | tf_op jit(solution)/shard_map/ppermute | solution.py:360
  57.2 6.0 %collective-permute-start.5 = (f32[16,1664]{1,0:T(8,128)S(1)}, f32[16,1664]{1,0:T(8,128)S(1)}, u32[]{:S(2)}, u32[]{:S(2)}) collective-permute-start(f32[16,1664]{1,0:T(8,128)S(1)} %get-tuple-element.40), channel_id=1, source_target_pairs={{0,224},{16,240},{32,0},{48,16},{64,32},{80,48},{96,64},{112,80},{... | collective-permute-start | bytes 319496 | tf_op jit(solution)/shard_map/ppermute | solution.py:379
  59.8 4.8 %collective-permute-start.6 = (f32[16,1664]{1,0:T(8,128)S(1)}, f32[16,1664]{1,0:T(8,128)S(1)}, u32[]{:S(2)}, u32[]{:S(2)}) collective-permute-start(f32[16,1664]{1,0:T(8,128)S(1)} %get-tuple-element.41), channel_id=1, source_target_pairs={{0,32},{16,48},{32,64},{48,80},{64,96},{80,112},{96,128},{112,144}... | collective-permute-start | bytes 319496 | tf_op jit(solution)/shard_map/ppermute | solution.py:380
  59.8 3.5 %collective-permute-start.7 = (f32[16,256]{1,0:T(8,128)S(1)}, f32[16,256]{1,0:T(8,128)S(1)}, u32[]{:S(2)}, u32[]{:S(2)}) collective-permute-start(f32[16,256]{1,0:T(8,128)S(1)} %add.132), channel_id=1, source_target_pairs={{0,64},{16,80},{32,96},{48,112},{64,0},{80,16},{96,32},{112,48},{1... | collective-permute-start | bytes 49160 | tf_op jit(solution)/shard_map/ppermute | solution.py:360
  64.6 7.2 %collective-permute-start.8 = (f32[16,1664]{1,0:T(8,128)S(1)}, f32[16,1664]{1,0:T(8,128)S(1)}, u32[]{:S(2)}, u32[]{:S(2)}) collective-permute-start(f32[16,1664]{1,0:T(8,128)S(1)} %get-tuple-element.43), channel_id=1, source_target_pairs={{0,224},{16,240},{32,0},{48,16},{64,32},{80,48},{96,64},{112,80},{... | collective-permute-start | bytes 319496 | tf_op jit(solution)/shard_map/ppermute | solution.py:379
  66.6 5.1 %collective-permute-start.9 = (f32[16,1664]{1,0:T(8,128)S(1)}, f32[16,1664]{1,0:T(8,128)S(1)}, u32[]{:S(2)}, u32[]{:S(2)}) collective-permute-start(f32[16,1664]{1,0:T(8,128)S(1)} %get-tuple-element.44), channel_id=1, source_target_pairs={{0,32},{16,48},{32,64},{48,80},{64,96},{80,112},{96,128},{112,144}... | collective-permute-start | bytes 319496 | tf_op jit(solution)/shard_map/ppermute | solution.py:380
  66.6 5.1 %collective-permute-start.10 = (f32[16,256]{1,0:T(8,128)S(1)}, f32[16,256]{1,0:T(8,128)S(1)}, u32[]{:S(2)}, u32[]{:S(2)}) collective-permute-start(f32[16,256]{1,0:T(8,128)S(1)} %add.141), channel_id=1, source_target_pairs={{0,224},{16,240},{32,192},{48,208},{64,160},{80,176},{96,128},{112... | collective-permute-start | bytes 49160 | tf_op jit(solution)/shard_map/ppermute | solution.py:360
  71.8 5.0 %collective-permute-start.14 = (f32[1,16,256]{2,1,0:T(8,128)S(1)}, f32[1,16,256]{2,1,0:T(8,128)S(1)}, u32[]{:S(2)}, u32[]{:S(2)}) collective-permute-start(f32[1,16,256]{2,1,0:T(8,128)S(1)} %bitcast.34), channel_id=1, source_target_pairs={{0,3},{1,2},{2,1},{3,0},{4,7},{5,6},{6,5},{7,4},{8,11},{9,10},{10,... | collective-permute-start | bytes 49160 | tf_op jit(solution)/shard_map/ppermute | solution.py:360
  72.0 4.8 %collective-permute-start.13 = (f32[1,16,256]{2,1,0:T(8,128)S(1)}, f32[1,16,256]{2,1,0:T(8,128)S(1)}, u32[]{:S(2)}, u32[]{:S(2)}) collective-permute-start(f32[1,16,256]{2,1,0:T(8,128)S(1)} %bitcast.35), channel_id=1, source_target_pairs={{0,2},{1,3},{2,0},{3,1},{4,6},{5,7},{6,4},{7,5},{8,10},{9,11},{10,... | collective-permute-start | bytes 49160 | tf_op jit(solution)/shard_map/ppermute | solution.py:360
  73.9 2.9 %collective-permute-start.12 = (f32[1,16,256]{2,1,0:T(8,128)S(1)}, f32[1,16,256]{2,1,0:T(8,128)S(1)}, u32[]{:S(2)}, u32[]{:S(2)}) collective-permute-start(f32[1,16,256]{2,1,0:T(8,128)S(1)} %bitcast.36), channel_id=1, source_target_pairs={{0,1},{1,0},{2,3},{3,2},{4,5},{5,4},{6,7},{7,6},{8,9},{9,8},{10,11... | collective-permute-start | bytes 49160 | tf_op jit(solution)/shard_map/ppermute | solution.py:360
  75.1 3.6 %collective-permute-start.11 = (f32[16,1664]{1,0:T(8,128)S(1)}, f32[16,1664]{1,0:T(8,128)S(1)}, u32[]{:S(2)}, u32[]{:S(2)}) collective-permute-start(f32[16,1664]{1,0:T(8,128)S(1)} %get-tuple-element.47), channel_id=1, source_target_pairs={{0,224},{16,240},{32,0},{48,16},{64,32},{80,48},{96,64},{112,80},{... | collective-permute-start | bytes 319496 | tf_op jit(solution)/shard_map/ppermute | solution.py:385
  79.7 23.6 %all-to-all-start.2 = ((f32[8,16,1664]{2,1,0:T(8,128)}), f32[8,16,1664]{2,1,0:T(8,128)S(1)}, u32[]{:S(2)}, u32[]{:S(2)}) async-start(f32[8,16,1664]{2,1,0:T(8,128)} %broadcast_in_dim.8), calls=%async_computation.2 | async-start | bytes 1703936 | tf_op jit(solution)/shard_map/all_to_all | solution.py:352
  84.5 4.3 %collective-permute-start.17 = (f32[4,16,256]{2,1,0:T(8,128)S(1)}, f32[4,16,256]{2,1,0:T(8,128)S(1)}, u32[]{:S(2)}, u32[]{:S(2)}) collective-permute-start(f32[4,16,256]{2,1,0:T(8,128)S(1)} %pad_maximum_fusion.1), channel_id=1, source_target_pairs={{0,12},{1,13},{2,14},{3,15},{4,8},{5,9},{6,10},{7,11},{8,4},{9,5},... | collective-permute-start | bytes 196616 | tf_op jit(solution)/shard_map/ppermute | solution.py:360
  85.0 4.6 %collective-permute-start.16 = (f32[4,16,256]{2,1,0:T(8,128)S(1)}, f32[4,16,256]{2,1,0:T(8,128)S(1)}, u32[]{:S(2)}, u32[]{:S(2)}) collective-permute-start(f32[4,16,256]{2,1,0:T(8,128)S(1)} %pad_maximum_fusion.1), channel_id=1, source_target_pairs={{0,8},{1,9},{2,10},{3,11},{4,12},{5,13},{6,14},{7,15},{8,0},{9,1},... | collective-permute-start | bytes 196616 | tf_op jit(solution)/shard_map/ppermute | solution.py:360
  85.7 4.3 %collective-permute-start.15 = (f32[4,16,256]{2,1,0:T(8,128)S(1)}, f32[4,16,256]{2,1,0:T(8,128)S(1)}, u32[]{:S(2)}, u32[]{:S(2)}) collective-permute-start(f32[4,16,256]{2,1,0:T(8,128)S(1)} %pad_maximum_fusion.1), channel_id=1, source_target_pairs={{0,4},{1,5},{2,6},{3,7},{4,0},{5,1},{6,2},{7,3},{8,12},{9,13},{10,... | collective-permute-start | bytes 196616 | tf_op jit(solution)/shard_map/ppermute | solution.py:360
  103.2 13.1 %copy-start.4 = (f32[256,256]{1,0:T(8,128)}, f32[256,256]{1,0:T(8,128)S(1)}, u32[]{:S(2)}) copy-start(f32[256,256]{1,0:T(8,128)S(1)} %second_factor.1.w_ref) | copy-start | bytes 786436
  103.2 10.7 %collective-permute-start.18 = (f32[128,1664]{1,0:T(8,128)S(1)}, f32[128,1664]{1,0:T(8,128)S(1)}, u32[]{:S(2)}, u32[]{:S(2)}) collective-permute-start(f32[128,1664]{1,0:T(8,128)S(1)} %bitcast.27), channel_id=1, source_target_pairs={{0,16},{16,0},{32,48},{48,32},{64,80},{80,64},{96,112},{112,96},{1... | collective-permute-start | bytes 2555912 | tf_op jit(solution)/shard_map/ppermute | solution.py:407
  116.3 1.2 copy-start.3
  117.5 10.6 %all-to-all-start.3 = ((f32[16,8,256]{2,1,0:T(8,128)}), f32[16,8,256]{2,1,0:T(8,128)S(1)}, u32[]{:S(2)}, u32[]{:S(2)}) async-start(f32[16,8,256]{2,1,0:T(8,128)} %get-tuple-element.56), calls=%async_computation.3 | async-start | bytes 262144 | tf_op jit(solution)/shard_map/all_to_all | solution.py:352
  128.1 0.6 copy-start.5

commit v7 on v6

--- a/solution.py
+++ b/solution.py
@@ -212,7 +212,7 @@
         out_specs=(vmem, vmem),
         out_shape=(jax.ShapeDtypeStruct((HALF, columns), jnp.float32),) * 2,
         scratch_shapes=[pltpu.VMEM((2 * RANK, rows), jnp.bfloat16)],
-        compiler_params=params(),
+        compiler_params=params(24),
         cost_estimate=pl.CostEstimate(flops=1744830464, bytes_accessed=5600000, transcendentals=0),
         name="cross_part",
     )(core, left, momentum, gradient)

time: 134 us -> 134 us (level)
  no operation moved by 1% of the time
where the time goes in v7:
time: 134 us
  starting transfers between devices  46.2 us (34%)
  Pallas kernels  36 us (27%)
  waiting for transfers between devices  26.6 us (20%)
  blocking collectives  18.2 us (14%)
  local copies, waits for them, and re-layouts  5.12 us (4%)
    all_to_all x1, blocking collectives, exchange(): return lax.all_to_all(pieces, axis, 0, 0, axis_index_groups=groups)  18.2 us
    all_to_all x3, starting transfers between devices, exchange(): return lax.all_to_all(pieces, axis, 0, 0, axis_index_groups=groups)  11.9 us
    ppermute x10, waiting for transfers between devices, swap(): return lax.ppermute(value, axis, [(i, i ^ bits) for i in range(16)])  11.5 us
    ppermute x10, starting transfers between devices, swap(): return lax.ppermute(value, axis, [(i, i ^ bits) for i in range(16)])  10.9 us
    all_to_all x3, waiting for transfers between devices, exchange(): return lax.all_to_all(pieces, axis, 0, 0, axis_index_groups=groups)  9.64 us
    ppermute x1, starting transfers between devices, local(): other = lax.ppermute(mine, 'row', CORE_SWAP)  8.65 us
    ppermute x3, starting transfers between devices, scatter_z(): down = lax.ppermute(down, 'row', z_shift(-1)) + own(k - 3)  8.6 us
    pallas_call x1, Pallas kernels, second_part(): pl.pallas_call(second_kernel, out_shape=jax.ShapeDtypeStruct((RANK, RANK)...  7.11 us
  transfers between devices with their start and end apart: 22, of which 13 were waited for; matrix products, arithmetic and copies ran while one was open for 0% of the time, Pallas kernels for 15%

profile of v7, /device:TPU:1, one launch (start us, length us, event | category | flops | bytes accessed | tf_op | source)
XLA Modules:
  0.0 133.9 jit_solution(652588966333747779)
XLA Ops:
  0.6 5.2 %left_part.1 = f32[512,256]{1,0:T(8,128)} custom-call(bf16[512,1664]{1,0:T(8,128)(2,1)} %m_ref.5, bf16[512,1664]{1,0:T(8,128)(2,1)} %g_ref.5, f32[1664,256]{1,0:T(8,128)} %r_ref.1), custom_call_target="tpu_custom_call" | custom-call | flops 1744830464 | bytes 5600000 | tf_op jit(solution)/shard_map/left_part/pallas_call | solution.py:176
  5.8 18.2 %all_to_all.20 = f32[16,32,256]{2,1,0:T(8,128)S(1)} all-to-all(f32[16,32,256]{2,1,0:T(8,128)} %bitcast.33), channel_id=1, replica_groups=mesh['row'=16,'col'=16] {'col'}, dimensions={0} | all-to-all | bytes 1048576 | tf_op jit(solution)/shard_map/all_to_all | solution.py:352
  24.9 3.6 %all-to-all-start.1 = ((f32[16,32,256]{2,1,0:T(8,128)}), f32[16,32,256]{2,1,0:T(8,128)S(1)}, u32[]{:S(2)}, u32[]{:S(2)}) async-start(f32[16,32,256]{2,1,0:T(8,128)} %broadcast_in_dim.6), calls=%async_computation.1 | async-start | bytes 1048576 | tf_op jit(solution)/shard_map/all_to_all | solution.py:352
  28.5 9.6 %all-to-all-done.1 = f32[16,32,256]{2,1,0:T(8,128)S(1)} async-done(((f32[16,32,256]{2,1,0:T(8,128)}), f32[16,32,256]{2,1,0:T(8,128)S(1)}, u32[]{:S(2)}, u32[]{:S(2)}) %all-to-all-start.1) | async-done | bytes 524320 | tf_op jit(solution)/shard_map/all_to_all | solution.py:352
  38.8 1.5 %copy-done.2 = bf16[512,1664]{1,0:T(8,128)(2,1)S(1)} copy-done((bf16[512,1664]{1,0:T(8,128)(2,1)S(1)}, bf16[512,1664]{1,0:T(8,128)(2,1)}, u32[]{:S(2)}) %copy-start.2) | copy-done | bytes 1703960
  40.3 3.0 %cross_part.1 = (f32[128,1664]{1,0:T(8,128)S(1)}, f32[128,1664]{1,0:T(8,128)}) custom-call(s32[1]{0:T(128)} %bitcast.core_ref, f32[512,256]{1,0:T(8,128)S(1)} %bitcast.25, bf16[512,1664]{1,0:T(8,128)(2,1)S(1)} %copy-done.1, bf16[512,1664]{1,0:T(8,128)(2,1)S(1)} %copy-done.2), custom_call_target="tpu_custom_call" | custom-call | flops 1744830464 | bytes 5600000 | tf_op jit(solution)/shard_map/cross_part/pallas_call | solution.py:209
  43.3 2.8 %collective-permute-start = (f32[128,1664]{1,0:T(8,128)}, f32[128,1664]{1,0:T(8,128)S(1)}, u32[]{:S(2)}, u32[]{:S(2)}) collective-permute-start(f32[128,1664]{1,0:T(8,128)} %get-tuple-element.36), channel_id=1, source_target_pairs={{0,16},{16,0},{32,48},{48,32},{64,80},{80,64},{96,112},{112,96},{1... | collective-permute-start | bytes 2555912 | tf_op jit(solution)/shard_map/ppermute | solution.py:399
  46.1 1.9 %collective-permute-done.1 = f32[16,256]{1,0:T(8,128)S(1)} collective-permute-done((f32[16,256]{1,0:T(8,128)S(1)}, f32[16,256]{1,0:T(8,128)S(1)}, u32[]{:S(2)}, u32[]{:S(2)}) %collective-permute-start.1) | collective-permute-done | bytes 16416 | tf_op jit(solution)/shard_map/ppermute | solution.py:360
  48.5 1.7 %collective-permute-start.3 = (f32[16,1664]{1,0:T(8,128)S(1)}, f32[16,1664]{1,0:T(8,128)S(1)}, u32[]{:S(2)}, u32[]{:S(2)}) collective-permute-start(f32[16,1664]{1,0:T(8,128)S(1)} %get-tuple-element.71), channel_id=1, source_target_pairs={{0,32},{16,48},{32,64},{48,80},{64,96},{80,112},{96,128},{112,144}... | collective-permute-start | bytes 319496 | tf_op jit(solution)/shard_map/ppermute | solution.py:380
  50.2 4.0 %collective-permute-start.2 = (f32[16,1664]{1,0:T(8,128)S(1)}, f32[16,1664]{1,0:T(8,128)S(1)}, u32[]{:S(2)}, u32[]{:S(2)}) collective-permute-start(f32[16,1664]{1,0:T(8,128)S(1)} %get-tuple-element.72), channel_id=1, source_target_pairs={{0,224},{16,240},{32,0},{48,16},{64,32},{80,48},{96,64},{112,80},{... | collective-permute-start | bytes 319496 | tf_op jit(solution)/shard_map/ppermute | solution.py:379
  54.3 2.9 %collective-permute-done.4 = f32[16,256]{1,0:T(8,128)S(1)} collective-permute-done((f32[16,256]{1,0:T(8,128)S(1)}, f32[16,256]{1,0:T(8,128)S(1)}, u32[]{:S(2)}, u32[]{:S(2)}) %collective-permute-start.4) | collective-permute-done | bytes 16416 | tf_op jit(solution)/shard_map/ppermute | solution.py:360
  57.2 2.5 %collective-permute-start.5 = (f32[16,1664]{1,0:T(8,128)S(1)}, f32[16,1664]{1,0:T(8,128)S(1)}, u32[]{:S(2)}, u32[]{:S(2)}) collective-permute-start(f32[16,1664]{1,0:T(8,128)S(1)} %get-tuple-element.40), channel_id=1, source_target_pairs={{0,224},{16,240},{32,0},{48,16},{64,32},{80,48},{96,64},{112,80},{... | collective-permute-start | bytes 319496 | tf_op jit(solution)/shard_map/ppermute | solution.py:379
  59.8 1.6 %collective-permute-start.7 = (f32[16,256]{1,0:T(8,128)S(1)}, f32[16,256]{1,0:T(8,128)S(1)}, u32[]{:S(2)}, u32[]{:S(2)}) collective-permute-start(f32[16,256]{1,0:T(8,128)S(1)} %add.132), channel_id=1, source_target_pairs={{0,64},{16,80},{32,96},{48,112},{64,0},{80,16},{96,32},{112,48},{1... | collective-permute-start | bytes 49160 | tf_op jit(solution)/shard_map/ppermute | solution.py:360
  61.3 1.9 %collective-permute-done.7 = f32[16,256]{1,0:T(8,128)S(1)} collective-permute-done((f32[16,256]{1,0:T(8,128)S(1)}, f32[16,256]{1,0:T(8,128)S(1)}, u32[]{:S(2)}, u32[]{:S(2)}) %collective-permute-start.7) | collective-permute-done | bytes 16416 | tf_op jit(solution)/shard_map/ppermute | solution.py:360
  63.3 1.3 collective-permute-done.6
  64.6 2.1 %collective-permute-start.8 = (f32[16,1664]{1,0:T(8,128)S(1)}, f32[16,1664]{1,0:T(8,128)S(1)}, u32[]{:S(2)}, u32[]{:S(2)}) collective-permute-start(f32[16,1664]{1,0:T(8,128)S(1)} %get-tuple-element.43), channel_id=1, source_target_pairs={{0,224},{16,240},{32,0},{48,16},{64,32},{80,48},{96,64},{112,80},{... | collective-permute-start | bytes 319496 | tf_op jit(solution)/shard_map/ppermute | solution.py:379
  66.6 2.7 %collective-permute-start.10 = (f32[16,256]{1,0:T(8,128)S(1)}, f32[16,256]{1,0:T(8,128)S(1)}, u32[]{:S(2)}, u32[]{:S(2)}) collective-permute-start(f32[16,256]{1,0:T(8,128)S(1)} %add.141), channel_id=1, source_target_pairs={{0,224},{16,240},{32,192},{48,208},{64,160},{80,176},{96,128},{112... | collective-permute-start | bytes 49160 | tf_op jit(solution)/shard_map/ppermute | solution.py:360
  69.3 2.4 %collective-permute-done.10 = f32[16,256]{1,0:T(8,128)S(1)} collective-permute-done((f32[16,256]{1,0:T(8,128)S(1)}, f32[16,256]{1,0:T(8,128)S(1)}, u32[]{:S(2)}, u32[]{:S(2)}) %collective-permute-start.10) | collective-permute-done | bytes 16416 | tf_op jit(solution)/shard_map/ppermute | solution.py:360
  72.0 1.9 %collective-permute-start.13 = (f32[1,16,256]{2,1,0:T(8,128)S(1)}, f32[1,16,256]{2,1,0:T(8,128)S(1)}, u32[]{:S(2)}, u32[]{:S(2)}) collective-permute-start(f32[1,16,256]{2,1,0:T(8,128)S(1)} %bitcast.35), channel_id=1, source_target_pairs={{0,2},{1,3},{2,0},{3,1},{4,6},{5,7},{6,4},{7,5},{8,10},{9,11},{10,... | collective-permute-start | bytes 49160 | tf_op jit(solution)/shard_map/ppermute | solution.py:360
  75.1 1.7 %collective-permute-start.11 = (f32[16,1664]{1,0:T(8,128)S(1)}, f32[16,1664]{1,0:T(8,128)S(1)}, u32[]{:S(2)}, u32[]{:S(2)}) collective-permute-start(f32[16,1664]{1,0:T(8,128)S(1)} %get-tuple-element.47), channel_id=1, source_target_pairs={{0,224},{16,240},{32,0},{48,16},{64,32},{80,48},{96,64},{112,80},{... | collective-permute-start | bytes 319496 | tf_op jit(solution)/shard_map/ppermute | solution.py:385
  76.8 1.8 %collective-permute-done.11 = f32[16,1664]{1,0:T(8,128)S(1)} collective-permute-done((f32[16,1664]{1,0:T(8,128)S(1)}, f32[16,1664]{1,0:T(8,128)S(1)}, u32[]{:S(2)}, u32[]{:S(2)}) %collective-permute-start.11) | collective-permute-done | bytes 106528 | tf_op jit(solution)/shard_map/ppermute | solution.py:385
  79.7 4.8 %all-to-all-start.2 = ((f32[8,16,1664]{2,1,0:T(8,128)}), f32[8,16,1664]{2,1,0:T(8,128)S(1)}, u32[]{:S(2)}, u32[]{:S(2)}) async-start(f32[8,16,1664]{2,1,0:T(8,128)} %broadcast_in_dim.8), calls=%async_computation.2 | async-start | bytes 1703936 | tf_op jit(solution)/shard_map/all_to_all | solution.py:352
  85.7 2.0 %collective-permute-start.15 = (f32[4,16,256]{2,1,0:T(8,128)S(1)}, f32[4,16,256]{2,1,0:T(8,128)S(1)}, u32[]{:S(2)}, u32[]{:S(2)}) collective-permute-start(f32[4,16,256]{2,1,0:T(8,128)S(1)} %pad_maximum_fusion.1), channel_id=1, source_target_pairs={{0,4},{1,5},{2,6},{3,7},{4,0},{5,1},{6,2},{7,3},{8,12},{9,13},{10,... | collective-permute-start | bytes 196616 | tf_op jit(solution)/shard_map/ppermute | solution.py:360
  90.1 6.0 %first_factor.1 = (f32[8,128]{1,0:T(8,128)S(1)}, f32[128,128]{1,0:T(8,128)S(1)}, f32[256,256]{1,0:T(8,128)S(1)}) custom-call(s32[1]{0:T(128)} %bitcast.14.col_ref, f32[16,16,256]{2,1,0:T(8,128)S(1)} %pad_maximum_fusion.gather_ref), custom_call_target="tpu_custom_call" | custom-call | flops 6000000 | bytes 20000000 | tf_op jit(solution)/shard_map/first_factor/pallas_call | solution.py:123
  96.1 7.1 %second_factor.1.w_ref = f32[256,256]{1,0:T(8,128)S(1)} custom-call(f32[256,256]{1,0:T(8,128)S(1)} %get-tuple-element.51.gram_ref, f32[8,128]{1,0:T(8,128)S(1)} %get-tuple-element.52.jitter_ref, f32[128,128]{1,0:T(8,128)S(1)} %get-tuple-element.53.first_ref), custom_call_target="tpu_custom_call" | custom-call | flops 6000000 | bytes 24000000 | tf_op jit(solution)/shard_map/second_factor/pallas_call | solution.py:139
  103.2 8.7 %collective-permute-start.18 = (f32[128,1664]{1,0:T(8,128)S(1)}, f32[128,1664]{1,0:T(8,128)S(1)}, u32[]{:S(2)}, u32[]{:S(2)}) collective-permute-start(f32[128,1664]{1,0:T(8,128)S(1)} %bitcast.27), channel_id=1, source_target_pairs={{0,16},{16,0},{32,48},{48,32},{64,80},{80,64},{96,112},{112,96},{1... | collective-permute-start | bytes 2555912 | tf_op jit(solution)/shard_map/ppermute | solution.py:407
  111.9 2.0 %collective-permute-done.18.other_ref = f32[128,1664]{1,0:T(8,128)S(1)} collective-permute-done((f32[128,1664]{1,0:T(8,128)S(1)}, f32[128,1664]{1,0:T(8,128)S(1)}, u32[]{:S(2)}, u32[]{:S(2)}) %collective-permute-start.18) | collective-permute-done | bytes 852000 | tf_op jit(solution)/shard_map/ppermute | solution.py:407
  113.9 2.5 %right_part.1 = (f32[256,1664]{1,0:T(8,128)S(1)}, f32[16,8,256]{2,1,0:T(8,128)}) custom-call(s32[1]{0:T(128)} %bitcast.core_ref, f32[256,256]{1,0:T(8,128)S(1)} %second_factor.1.w_ref, f32[128,1664]{1,0:T(8,128)S(1)} %bitcast.28, f32[128,1664]{1,0:T(8,128)S(1)} %collective-permute-done.18.other_ref), custom_call_target="tpu_custom_call" | custom-call | flops 1300000000 | bytes 3400000 | tf_op jit(solution)/shard_map/right_part/pallas_call | solution.py:242
  116.3 1.2 copy-done.3
  117.5 3.5 %all-to-all-start.3 = ((f32[16,8,256]{2,1,0:T(8,128)}), f32[16,8,256]{2,1,0:T(8,128)S(1)}, u32[]{:S(2)}, u32[]{:S(2)}) async-start(f32[16,8,256]{2,1,0:T(8,128)} %get-tuple-element.56), calls=%async_computation.3 | async-start | bytes 262144 | tf_op jit(solution)/shard_map/all_to_all | solution.py:352
  121.0 7.1 %momentum_part.1 = (bf16[512,1664]{1,0:T(8,128)(2,1)}, f32[1664,256]{1,0:T(8,128)}, bf16[256,1664]{1,0:T(8,128)(2,1)}, bf16[256,1664]{1,0:T(8,128)(2,1)}, f32[512,256]{1,0:T(8,128)}) custom-call(bf16[512,1664]{1,0:T(8,128)(2,1)} %m_ref.5, bf16[512,1664]{1,0:T(8,128)(2,1)} %g_ref.5, f32[512,256]{1,0:T(8,128)} %bitcast.26, f32[256,256]{1,0:T(8,128)} %copy-done.4, ...), custom_call_target="tpu_custom_call" | custom-call | flops 1308622848 | bytes 7500000 | tf_op jit(solution)/shard_map/momentum_part/pallas_call | solution.py:290
  128.8 5.2 %weight_part.1 = (bf16[512,1664]{1,0:T(8,128)(2,1)}, f32[1664,256]{1,0:T(8,128)}) custom-call(f32[16,8,256]{2,1,0:T(8,128)} %copy-done.5, bf16[512,1664]{1,0:T(8,128)(2,1)} %weight_ref.1, f32[512,256]{1,0:T(8,128)} %get-tuple-element.58.ortho_ref, f32[1664,256]{1,0:T(8,128)} %get-tuple-element.59.turned_ref, bf16[256,1664]{1,0:T(8,128)(2,1)} %get-tuple-element.60.high_ref, ...), custom_call_target="tpu_custom_call" | custom-call | flops 1308622848 | bytes 7500000 | tf_op jit(solution)/shard_map/weight_part/pallas_call | solution.py:329
  (48 shorter events, 8.9 us)
Async XLA Ops:
  5.8 33.0 %copy-start.1 = (bf16[512,1664]{1,0:T(8,128)(2,1)S(1)}, bf16[512,1664]{1,0:T(8,128)(2,1)}, u32[]{:S(2)}) copy-start(bf16[512,1664]{1,0:T(8,128)(2,1)} %m_ref.5) | copy-start | bytes 5111812
  24.9 13.2 %all-to-all-start.1 = ((f32[16,32,256]{2,1,0:T(8,128)}), f32[16,32,256]{2,1,0:T(8,128)S(1)}, u32[]{:S(2)}, u32[]{:S(2)}) async-start(f32[16,32,256]{2,1,0:T(8,128)} %broadcast_in_dim.6), calls=%async_computation.1 | async-start | bytes 1048576 | tf_op jit(solution)/shard_map/all_to_all | solution.py:352
  38.1 5.2 %copy-start = (f32[16,32,256]{2,1,0:T(8,128)}, f32[16,32,256]{2,1,0:T(8,128)S(1)}, u32[]{:S(2)}) copy-start(f32[16,32,256]{2,1,0:T(8,128)S(1)} %all-to-all-done.1) | copy-start | bytes 1572868
  38.8 1.5 %copy-start.2 = (bf16[512,1664]{1,0:T(8,128)(2,1)S(1)}, bf16[512,1664]{1,0:T(8,128)(2,1)}, u32[]{:S(2)}) copy-start(bf16[512,1664]{1,0:T(8,128)(2,1)} %g_ref.5) | copy-start | bytes 5111812
  43.3 5.1 %collective-permute-start = (f32[128,1664]{1,0:T(8,128)}, f32[128,1664]{1,0:T(8,128)S(1)}, u32[]{:S(2)}, u32[]{:S(2)}) collective-permute-start(f32[128,1664]{1,0:T(8,128)} %get-tuple-element.36), channel_id=1, source_target_pairs={{0,16},{16,0},{32,48},{48,32},{64,80},{80,64},{96,112},{112,96},{1... | collective-permute-start | bytes 2555912 | tf_op jit(solution)/shard_map/ppermute | solution.py:399
  46.1 1.9 %collective-permute-start.1 = (f32[16,256]{1,0:T(8,128)S(1)}, f32[16,256]{1,0:T(8,128)S(1)}, u32[]{:S(2)}, u32[]{:S(2)}) collective-permute-start(f32[16,256]{1,0:T(8,128)S(1)} %fusion), channel_id=1, source_target_pairs={{0,16},{16,0},{32,48},{48,32},{64,80},{80,64},{96,112},{112,96},{1... | collective-permute-start | bytes 49160 | tf_op jit(solution)/shard_map/ppermute | solution.py:360
  48.5 8.7 %collective-permute-start.3 = (f32[16,1664]{1,0:T(8,128)S(1)}, f32[16,1664]{1,0:T(8,128)S(1)}, u32[]{:S(2)}, u32[]{:S(2)}) collective-permute-start(f32[16,1664]{1,0:T(8,128)S(1)} %get-tuple-element.71), channel_id=1, source_target_pairs={{0,32},{16,48},{32,64},{48,80},{64,96},{80,112},{96,128},{112,144}... | collective-permute-start | bytes 319496 | tf_op jit(solution)/shard_map/ppermute | solution.py:380
  50.2 7.0 %collective-permute-start.2 = (f32[16,1664]{1,0:T(8,128)S(1)}, f32[16,1664]{1,0:T(8,128)S(1)}, u32[]{:S(2)}, u32[]{:S(2)}) collective-permute-start(f32[16,1664]{1,0:T(8,128)S(1)} %get-tuple-element.72), channel_id=1, source_target_pairs={{0,224},{16,240},{32,0},{48,16},{64,32},{80,48},{96,64},{112,80},{... | collective-permute-start | bytes 319496 | tf_op jit(solution)/shard_map/ppermute | solution.py:379
  54.3 2.9 %collective-permute-start.4 = (f32[16,256]{1,0:T(8,128)S(1)}, f32[16,256]{1,0:T(8,128)S(1)}, u32[]{:S(2)}, u32[]{:S(2)}) collective-permute-start(f32[16,256]{1,0:T(8,128)S(1)} %add.117), channel_id=1, source_target_pairs={{0,32},{16,48},{32,0},{48,16},{64,96},{80,112},{96,64},{112,80},{1... | collective-permute-start | bytes 49160 | tf_op jit(solution)/shard_map/ppermute | solution.py:360
  57.2 6.0 %collective-permute-start.5 = (f32[16,1664]{1,0:T(8,128)S(1)}, f32[16,1664]{1,0:T(8,128)S(1)}, u32[]{:S(2)}, u32[]{:S(2)}) collective-permute-start(f32[16,1664]{1,0:T(8,128)S(1)} %get-tuple-element.40), channel_id=1, source_target_pairs={{0,224},{16,240},{32,0},{48,16},{64,32},{80,48},{96,64},{112,80},{... | collective-permute-start | bytes 319496 | tf_op jit(solution)/shard_map/ppermute | solution.py:379
  59.8 4.8 %collective-permute-start.6 = (f32[16,1664]{1,0:T(8,128)S(1)}, f32[16,1664]{1,0:T(8,128)S(1)}, u32[]{:S(2)}, u32[]{:S(2)}) collective-permute-start(f32[16,1664]{1,0:T(8,128)S(1)} %get-tuple-element.41), channel_id=1, source_target_pairs={{0,32},{16,48},{32,64},{48,80},{64,96},{80,112},{96,128},{112,144}... | collective-permute-start | bytes 319496 | tf_op jit(solution)/shard_map/ppermute | solution.py:380
  59.8 3.5 %collective-permute-start.7 = (f32[16,256]{1,0:T(8,128)S(1)}, f32[16,256]{1,0:T(8,128)S(1)}, u32[]{:S(2)}, u32[]{:S(2)}) collective-permute-start(f32[16,256]{1,0:T(8,128)S(1)} %add.132), channel_id=1, source_target_pairs={{0,64},{16,80},{32,96},{48,112},{64,0},{80,16},{96,32},{112,48},{1... | collective-permute-start | bytes 49160 | tf_op jit(solution)/shard_map/ppermute | solution.py:360
  64.6 7.2 %collective-permute-start.8 = (f32[16,1664]{1,0:T(8,128)S(1)}, f32[16,1664]{1,0:T(8,128)S(1)}, u32[]{:S(2)}, u32[]{:S(2)}) collective-permute-start(f32[16,1664]{1,0:T(8,128)S(1)} %get-tuple-element.43), channel_id=1, source_target_pairs={{0,224},{16,240},{32,0},{48,16},{64,32},{80,48},{96,64},{112,80},{... | collective-permute-start | bytes 319496 | tf_op jit(solution)/shard_map/ppermute | solution.py:379
  66.6 5.1 %collective-permute-start.9 = (f32[16,1664]{1,0:T(8,128)S(1)}, f32[16,1664]{1,0:T(8,128)S(1)}, u32[]{:S(2)}, u32[]{:S(2)}) collective-permute-start(f32[16,1664]{1,0:T(8,128)S(1)} %get-tuple-element.44), channel_id=1, source_target_pairs={{0,32},{16,48},{32,64},{48,80},{64,96},{80,112},{96,128},{112,144}... | collective-permute-start | bytes 319496 | tf_op jit(solution)/shard_map/ppermute | solution.py:380
  66.6 5.1 %collective-permute-start.10 = (f32[16,256]{1,0:T(8,128)S(1)}, f32[16,256]{1,0:T(8,128)S(1)}, u32[]{:S(2)}, u32[]{:S(2)}) collective-permute-start(f32[16,256]{1,0:T(8,128)S(1)} %add.141), channel_id=1, source_target_pairs={{0,224},{16,240},{32,192},{48,208},{64,160},{80,176},{96,128},{112... | collective-permute-start | bytes 49160 | tf_op jit(solution)/shard_map/ppermute | solution.py:360
  71.8 5.0 %collective-permute-start.14 = (f32[1,16,256]{2,1,0:T(8,128)S(1)}, f32[1,16,256]{2,1,0:T(8,128)S(1)}, u32[]{:S(2)}, u32[]{:S(2)}) collective-permute-start(f32[1,16,256]{2,1,0:T(8,128)S(1)} %bitcast.34), channel_id=1, source_target_pairs={{0,3},{1,2},{2,1},{3,0},{4,7},{5,6},{6,5},{7,4},{8,11},{9,10},{10,... | collective-permute-start | bytes 49160 | tf_op jit(solution)/shard_map/ppermute | solution.py:360
  72.0 4.8 %collective-permute-start.13 = (f32[1,16,256]{2,1,0:T(8,128)S(1)}, f32[1,16,256]{2,1,0:T(8,128)S(1)}, u32[]{:S(2)}, u32[]{:S(2)}) collective-permute-start(f32[1,16,256]{2,1,0:T(8,128)S(1)} %bitcast.35), channel_id=1, source_target_pairs={{0,2},{1,3},{2,0},{3,1},{4,6},{5,7},{6,4},{7,5},{8,10},{9,11},{10,... | collective-permute-start | bytes 49160 | tf_op jit(solution)/shard_map/ppermute | solution.py:360
  73.9 2.9 %collective-permute-start.12 = (f32[1,16,256]{2,1,0:T(8,128)S(1)}, f32[1,16,256]{2,1,0:T(8,128)S(1)}, u32[]{:S(2)}, u32[]{:S(2)}) collective-permute-start(f32[1,16,256]{2,1,0:T(8,128)S(1)} %bitcast.36), channel_id=1, source_target_pairs={{0,1},{1,0},{2,3},{3,2},{4,5},{5,4},{6,7},{7,6},{8,9},{9,8},{10,11... | collective-permute-start | bytes 49160 | tf_op jit(solution)/shard_map/ppermute | solution.py:360
  75.1 3.6 %collective-permute-start.11 = (f32[16,1664]{1,0:T(8,128)S(1)}, f32[16,1664]{1,0:T(8,128)S(1)}, u32[]{:S(2)}, u32[]{:S(2)}) collective-permute-start(f32[16,1664]{1,0:T(8,128)S(1)} %get-tuple-element.47), channel_id=1, source_target_pairs={{0,224},{16,240},{32,0},{48,16},{64,32},{80,48},{96,64},{112,80},{... | collective-permute-start | bytes 319496 | tf_op jit(solution)/shard_map/ppermute | solution.py:385
  79.7 23.6 %all-to-all-start.2 = ((f32[8,16,1664]{2,1,0:T(8,128)}), f32[8,16,1664]{2,1,0:T(8,128)S(1)}, u32[]{:S(2)}, u32[]{:S(2)}) async-start(f32[8,16,1664]{2,1,0:T(8,128)} %broadcast_in_dim.8), calls=%async_computation.2 | async-start | bytes 1703936 | tf_op jit(solution)/shard_map/all_to_all | solution.py:352
  84.5 4.3 %collective-permute-start.17 = (f32[4,16,256]{2,1,0:T(8,128)S(1)}, f32[4,16,256]{2,1,0:T(8,128)S(1)}, u32[]{:S(2)}, u32[]{:S(2)}) collective-permute-start(f32[4,16,256]{2,1,0:T(8,128)S(1)} %pad_maximum_fusion.1), channel_id=1, source_target_pairs={{0,12},{1,13},{2,14},{3,15},{4,8},{5,9},{6,10},{7,11},{8,4},{9,5},... | collective-permute-start | bytes 196616 | tf_op jit(solution)/shard_map/ppermute | solution.py:360
  85.0 4.6 %collective-permute-start.16 = (f32[4,16,256]{2,1,0:T(8,128)S(1)}, f32[4,16,256]{2,1,0:T(8,128)S(1)}, u32[]{:S(2)}, u32[]{:S(2)}) collective-permute-start(f32[4,16,256]{2,1,0:T(8,128)S(1)} %pad_maximum_fusion.1), channel_id=1, source_target_pairs={{0,8},{1,9},{2,10},{3,11},{4,12},{5,13},{6,14},{7,15},{8,0},{9,1},... | collective-permute-start | bytes 196616 | tf_op jit(solution)/shard_map/ppermute | solution.py:360
  85.7 4.3 %collective-permute-start.15 = (f32[4,16,256]{2,1,0:T(8,128)S(1)}, f32[4,16,256]{2,1,0:T(8,128)S(1)}, u32[]{:S(2)}, u32[]{:S(2)}) collective-permute-start(f32[4,16,256]{2,1,0:T(8,128)S(1)} %pad_maximum_fusion.1), channel_id=1, source_target_pairs={{0,4},{1,5},{2,6},{3,7},{4,0},{5,1},{6,2},{7,3},{8,12},{9,13},{10,... | collective-permute-start | bytes 196616 | tf_op jit(solution)/shard_map/ppermute | solution.py:360
  103.2 13.1 %copy-start.4 = (f32[256,256]{1,0:T(8,128)}, f32[256,256]{1,0:T(8,128)S(1)}, u32[]{:S(2)}) copy-start(f32[256,256]{1,0:T(8,128)S(1)} %second_factor.1.w_ref) | copy-start | bytes 786436
  103.2 10.7 %collective-permute-start.18 = (f32[128,1664]{1,0:T(8,128)S(1)}, f32[128,1664]{1,0:T(8,128)S(1)}, u32[]{:S(2)}, u32[]{:S(2)}) collective-permute-start(f32[128,1664]{1,0:T(8,128)S(1)} %bitcast.27), channel_id=1, source_target_pairs={{0,16},{16,0},{32,48},{48,32},{64,80},{80,64},{96,112},{112,96},{1... | collective-permute-start | bytes 2555912 | tf_op jit(solution)/shard_map/ppermute | solution.py:407
  116.3 1.2 copy-start.3
  117.5 10.6 %all-to-all-start.3 = ((f32[16,8,256]{2,1,0:T(8,128)}), f32[16,8,256]{2,1,0:T(8,128)S(1)}, u32[]{:S(2)}, u32[]{:S(2)}) async-start(f32[16,8,256]{2,1,0:T(8,128)} %get-tuple-element.56), calls=%async_computation.3 | async-start | bytes 262144 | tf_op jit(solution)/shard_map/all_to_all | solution.py:352
  128.1 0.6 copy-start.5
